TPU v7x, 32 devices: a whole 2x2x4 slice. The times are simulated.
32 devices in a mesh: tile: 8 (over z, x), slide: 4 (over y, core).
Axes of the slice: x: 2, y: 2, z: 4, core: 2. Of those that a mesh axis runs over, the one named last changes fastest.
Arguments:
- tiles: bfloat16 [4, 24, 7, 7, 2048], P('slide', 'tile'), may hold values from -6 to 6
- tile_counts: int32 [4, 8], P('slide', 'tile'), may hold values from 1 to 3, as said below
- tile_weights: float32 [4, 24], P('slide', 'tile'), may hold values from 0.1 to 2
- slide_of: int32 [4, 24, 1], P('slide', 'tile'), may hold values from 0 to 7, as said below
- owner_map: int32 [4, 8], P('slide'), may hold values from 0 to 7, each once within a row
- cotangent: bfloat16 [4, 8, 2048], P('slide', 'tile'), may hold values from -6 to 6
- conv_weight: bfloat16 [9, 64, 2048], replicated, may hold values from -0.25 to 0.25
Outputs:
- pooled: float32 [4, 8, 2048], P('slide', 'tile')
- input_grads: float32 [4, 24, 7, 7, 2048], P('slide', 'tile')
- weight_grads: float32 [9, 64, 2048], P(None, None, 'tile')
Inputs may be any that keep to these rules, and one draw needn't show every extreme that they name: On every device the live tiles are the first tile_counts slots; in each slide group one device has all 3 slots live. `slide_of`: in each slide group, max(1, 2) slides name exactly one slot each, the first slot of some device; the other slots name the remaining slides evenly at random.
All inputs are finite; a program needn't handle non-finite values.
Results may differ from a plain program's by a relative error of at most 0.0065.
Values may be sent and summed in bfloat16 or wider, within the bound.
No kernel may reach another device: no remote copies, remote signals or barrier semaphores. Data moves between devices by JAX's collectives and lax.ppermute only.
A program may use at most 128 MiB of HBM per device.

v0:
```python
import functools

import jax
import jax.numpy as jnp
from jax import lax
from jax.experimental import pallas as pl
from jax.experimental.pallas import tpu as pltpu
from jax.sharding import PartitionSpec as P

LOSS_SCALE = 512.0
BLOCK = 256
ROW = 8
F32 = jnp.float32
BF16 = jnp.bfloat16


def vmem_whole():
    return pl.BlockSpec(memory_space=pltpu.VMEM)


def smem_whole():
    return pl.BlockSpec(memory_space=pltpu.SMEM)


def own_scalars(counts_ref, weights_ref, slide_ref, owner_ref, slots):
    coefs, targets = [], []
    for slot in range(slots):
        live = counts_ref[0, 0] > slot
        coefs.append(jnp.where(live, weights_ref[0, slot], 0.0))
        targets.append(owner_ref[0, slide_ref[0, slot]])
    return coefs, targets


def block_diagonal(tap, mask):
    width, channels = tap.shape
    if channels == width:
        return tap
    return jnp.concatenate([tap] * (channels // width), axis=0) * mask


def diagonal_mask(channels, width):
    row = lax.broadcasted_iota(jnp.int32, (channels, channels), 0) // width
    col = lax.broadcasted_iota(jnp.int32, (channels, channels), 1) // width
    return (row == col).astype(F32).astype(BF16)


def shifted(rows):
    count = rows.shape[0]
    return (
        pltpu.roll(rows, 1, 0).astype(BF16),
        rows.astype(BF16),
        pltpu.roll(rows, count - 1, 0).astype(BF16),
    )


def conv_taps(rows_ref, weight_of, pitch, count, flip, dims):
    total = None
    for offset in range(9):
        row_off, col_off = divmod(offset, 3)
        if flip:
            row_off, col_off = 2 - row_off, 2 - col_off
        rows = rows_ref[col_off, pl.ds(row_off * pitch, count), :]
        term = lax.dot_general(rows, weight_of(offset), dims, preferred_element_type=F32)
        total = term if total is None else total + term
    return total


def routing_of(info, slots):
    devices = info.shape[0]
    owners = lax.broadcasted_iota(jnp.int32, (devices, 128), 1).astype(F32)
    routes = []
    total = jnp.zeros((1, 128), F32)
    for slot in range(slots):
        coef = (
            info[:, slot : slot + 1]
            + info[:, slots + slot : slots + slot + 1]
            + info[:, 2 * slots + slot : 2 * slots + slot + 1]
        )
        target = info[:, 3 * slots + slot : 3 * slots + slot + 1]
        route = jnp.where(target == owners, coef, 0.0)
        routes.append(route)
        total = total + jnp.sum(route, axis=0, keepdims=True)
    return routes, jnp.maximum(total, 1.0)


def scaled_rows(cot, denominator):
    rows = []
    for owner in range(cot.shape[0]):
        value = LOSS_SCALE * cot[owner : owner + 1] / denominator[:, owner : owner + 1]
        rows.append(value.astype(BF16).astype(F32))
    return rows


def info_row(coefs, targets, lanes):
    slots = len(coefs)
    lane = lax.broadcasted_iota(jnp.int32, (1, lanes), 1)
    value = jnp.zeros((1, lanes), F32)
    for slot in range(slots):
        for part in range(3):
            value = jnp.where(lane == part * slots + slot, coefs[slot], value)
        value = jnp.where(lane == 3 * slots + slot, targets[slot].astype(F32), value)
    high = value.astype(BF16).astype(F32)
    middle = (value - high).astype(BF16).astype(F32)
    low = (value - high - middle).astype(BF16).astype(F32)
    value = jnp.where((lane >= slots) & (lane < 2 * slots), middle, high)
    return jnp.where((lane >= 2 * slots) & (lane < 3 * slots), low, value)


def pack_kernel(packed, counts_ref, weights_ref, slide_ref, owner_ref, x_ref, cot_ref, out_ref, info_ref):
    devices, slots, side, _, lanes = out_ref.shape
    coefs, targets = own_scalars(counts_ref, weights_ref, slide_ref, owner_ref, slots)
    info = info_row(coefs, targets, info_ref.shape[1])
    info_ref[...] = info
    cot = cot_ref[0].astype(F32)
    for slot in range(slots):
        for high in range(side):
            index = slot * side + high
            rows = x_ref[0, slot, high].astype(F32)
            if packed and index < devices:
                spare = cot[:, index * lanes : (index + 1) * lanes]
            elif packed and index == devices:
                spare = info[:, :lanes]
            else:
                spare = jnp.zeros((1, lanes), F32)
            for device in range(devices):
                part = rows[:, device * lanes : (device + 1) * lanes]
                out_ref[device, slot, high] = jnp.concatenate([part, spare], axis=0).astype(BF16)


def local_kernel(
    counts_ref, weights_ref, slide_ref, owner_ref, x_ref, w_ref, slope_ref, share_ref, rows_ref
):
    step = pl.program_id(0)
    side, kept, lanes = slope_ref.shape
    slots = kept // ROW
    devices = share_ref.shape[0]
    pitch = rows_ref.shape[1] // (side + 2)
    width = w_ref.shape[1]
    for col in range(3):
        rows_ref[col, pl.ds(0, pitch), :] = jnp.zeros((pitch, lanes), BF16)
        rows_ref[col, pl.ds((side + 1) * pitch, pitch), :] = jnp.zeros((pitch, lanes), BF16)
    for high in range(side):
        pieces = []
        for slot in range(slots):
            pieces += [x_ref[0, slot, high].astype(F32), jnp.zeros((ROW - side, lanes), F32)]
        if pitch > kept:
            pieces.append(jnp.zeros((pitch - kept, lanes), F32))
        for col, rows in enumerate(shifted(jnp.concatenate(pieces, axis=0))):
            rows_ref[col, pl.ds((high + 1) * pitch, pitch), :] = rows
    mask = diagonal_mask(lanes, width)
    pre = conv_taps(
        rows_ref,
        lambda tap: block_diagonal(w_ref[tap], mask),
        pitch,
        side * pitch,
        False,
        (((1,), (0,)), ((), ())),
    )
    sigma = jax.nn.sigmoid(pre)
    slope = sigma * (1.0 + pre * (1.0 - sigma))
    active = pre * sigma
    total = active[:pitch]
    slope_ref[0] = slope[:kept]
    for high in range(1, side):
        slope_ref[high] = slope[high * pitch : high * pitch + kept]
        total = total + active[high * pitch : (high + 1) * pitch]
    place = lax.broadcasted_iota(jnp.int32, (ROW, lanes), 0)
    coefs, targets = own_scalars(counts_ref, weights_ref, slide_ref, owner_ref, slots)
    means = []
    for slot in range(slots):
        here = jnp.where(place < side, total[slot * ROW : (slot + 1) * ROW], 0.0)
        mean = jnp.sum(here, axis=0, keepdims=True) / (side * side)
        means.append(mean.astype(BF16).astype(F32))
    for owner in range(devices):
        share = jnp.zeros((1, lanes), F32)
        for slot in range(slots):
            share = share + jnp.where(targets[slot] == owner, coefs[slot], 0.0) * means[slot]
        share_ref[owner, pl.ds(step, 1), :] = share


def weight_kernel(packed, my_ref, got_ref, w_ref, *refs):
    if packed:
        out_ref, rows_ref, grad_ref = refs
    else:
        cot_ref, info_ref, out_ref, rows_ref, grad_ref = refs
    devices, slots, side, _, lanes = got_ref.shape
    width = w_ref.shape[1]
    part = devices * ROW
    pitch = slots * part
    if packed:
        mine = my_ref[0]
        cot = got_ref[:, mine // side, mine % side].astype(F32)[:, ROW - 1, :]
        info = got_ref[:, devices // side, devices % side].astype(F32)[:, ROW - 1, :]
    else:
        cot = cot_ref[...]
        info = info_ref[...]
    routes, denominator = routing_of(info, slots)
    scaled = scaled_rows(cot, denominator)
    place = lax.broadcasted_iota(jnp.int32, (devices, ROW, lanes), 1)
    tile_grads = []
    for slot in range(slots):
        rows = jnp.zeros((devices, lanes), F32)
        for owner in range(devices):
            rows = rows + routes[slot][:, owner : owner + 1] * scaled[owner]
        spread = jnp.broadcast_to(rows[:, None, :], (devices, ROW, lanes)) / (side * side)
        tile_grads.append(jnp.where(place < side, spread, 0.0).reshape(part, lanes))
    tile_grad = jnp.concatenate(tile_grads, axis=0)

    zero = jnp.zeros((pitch, lanes), BF16)
    for col in range(3):
        rows_ref[col, pl.ds(0, pitch), :] = zero
        rows_ref[col, pl.ds((side + 1) * pitch, pitch), :] = zero
    grad_ref[pl.ds(0, pitch), :] = zero
    grad_ref[pl.ds((side + 1) * pitch, pitch), :] = zero
    for high in range(side):
        for slot in range(slots):
            rows = jnp.where(place < side, got_ref[:, slot, high].astype(F32), 0.0)
            for col, moved in enumerate(shifted(rows.reshape(part, lanes))):
                rows_ref[col, pl.ds((high + 1) * pitch + slot * part, part), :] = moved
    mask = diagonal_mask(lanes, width) if lanes > width else None
    pre = conv_taps(
        rows_ref,
        lambda tap: block_diagonal(w_ref[tap], mask),
        pitch,
        side * pitch,
        False,
        (((1,), (0,)), ((), ())),
    )
    sigma = jax.nn.sigmoid(pre)
    slope = sigma * (1.0 + pre * (1.0 - sigma))
    for high in range(side):
        here = slope[high * pitch : (high + 1) * pitch] * tile_grad
        grad_ref[pl.ds((high + 1) * pitch, pitch), :] = here.astype(BF16)
    group = lax.broadcasted_iota(jnp.int32, (width, lanes), 1) // width
    for offset in range(9):
        row_off, col_off = divmod(offset, 3)
        product = lax.dot_general(
            rows_ref[col_off, pl.ds(pitch, side * pitch), :],
            grad_ref[pl.ds((2 - row_off) * pitch, side * pitch), :],
            (((0,), (0,)), ((), ())),
            preferred_element_type=F32,
        )
        result = product[:width]
        for index in range(1, lanes // width):
            result = jnp.where(group == index, product[index * width : (index + 1) * width], result)
        out_ref[offset] = result


def input_kernel(
    packed,
    my_ref,
    counts_ref,
    weights_ref,
    slide_ref,
    owner_ref,
    slope_ref,
    w_ref,
    cot_ref,
    info_ref,
    share_ref,
    out_ref,
    pooled_ref,
    rows_ref,
):
    step = pl.program_id(0)
    side, kept, lanes = slope_ref.shape
    slots = kept // ROW
    devices = share_ref.shape[0]
    pitch = rows_ref.shape[1] // (side + 2)
    width = w_ref.shape[1]
    if packed:
        cot = cot_ref[:, 0, 0].astype(F32)[:, ROW - 1, :]
        info = info_ref[:, 0, 0].astype(F32)[:, ROW - 1, :]
    else:
        cot = cot_ref[...]
        info = info_ref[...]
    _, denominator = routing_of(info, slots)
    scaled = scaled_rows(cot, denominator)
    owners = lax.broadcasted_iota(jnp.int32, (1, 128), 1)
    mine = jnp.sum(jnp.where(owners == my_ref[0], denominator, 0.0), axis=1, keepdims=True)
    shares = share_ref[:, pl.ds(step, 1), :]
    pooled_ref[0] = jnp.sum(shares, axis=0) / mine

    coefs, targets = own_scalars(counts_ref, weights_ref, slide_ref, owner_ref, slots)
    place = lax.broadcasted_iota(jnp.int32, (ROW, lanes), 0)
    pieces = []
    for slot in range(slots):
        row = jnp.zeros((1, lanes), F32)
        for owner in range(devices):
            row = row + jnp.where(targets[slot] == owner, coefs[slot], 0.0) * scaled[owner]
        spread = jnp.broadcast_to(row, (ROW, lanes)) / (side * side)
        pieces.append(jnp.where(place < side, spread, 0.0))
    tile_grad = jnp.concatenate(pieces, axis=0)

    for col in range(3):
        rows_ref[col, pl.ds(0, pitch), :] = jnp.zeros((pitch, lanes), BF16)
        rows_ref[col, pl.ds((side + 1) * pitch, pitch), :] = jnp.zeros((pitch, lanes), BF16)
    for high in range(side):
        rows = slope_ref[high] * tile_grad
        if pitch > kept:
            rows = jnp.concatenate([rows, jnp.zeros((pitch - kept, lanes), F32)], axis=0)
        for col, moved in enumerate(shifted(rows)):
            rows_ref[col, pl.ds((high + 1) * pitch, pitch), :] = moved
    mask = diagonal_mask(lanes, width)
    total = conv_taps(
        rows_ref,
        lambda tap: block_diagonal(w_ref[tap], mask),
        pitch,
        side * pitch,
        True,
        (((1,), (1,)), ((), ())),
    )
    for high in range(side):
        for slot in range(slots):
            start = high * pitch + slot * ROW
            for wide in range(side):
                out_ref[slot, high, wide] = total[start + wide : start + wide + 1]


def params(mebibytes):
    return pltpu.CompilerParams(vmem_limit_bytes=mebibytes * 2**20)


def cost(flops, moved):
    return pl.CostEstimate(flops=flops, bytes_accessed=moved, transcendentals=0)


def exchange_sum(value, axis, step):
    count = lax.axis_size(axis)
    return value, lax.ppermute(value, axis, [(i, i ^ step) for i in range(count)])


def shards(tiles, tile_counts, tile_weights, slide_of, owner_map, cotangent, conv_weight):
    _, slots, side, _, channels = tiles.shape
    taps, width, _ = conv_weight.shape
    devices = lax.axis_size("tile")
    lanes = channels // devices
    blocks = channels // BLOCK
    mine = lax.axis_index("tile").astype(jnp.int32).reshape(1)
    slides = slide_of[:, :, 0]
    packed = lanes == BLOCK and devices + 1 <= slots * side
    scalars = (tile_counts, tile_weights, slides, owner_map)
    kept = slots * ROW
    pitch = -(-kept // 16) * 16
    macs = slots * side * side * taps * width * channels

    chunks, info = pl.pallas_call(
        functools.partial(pack_kernel, packed),
        out_shape=(
            jax.ShapeDtypeStruct((devices, slots, side, ROW, lanes), BF16),
            jax.ShapeDtypeStruct((1, max(lanes, 128)), F32),
        ),
        in_specs=[smem_whole()] * 4 + [vmem_whole()] * 2,
        out_specs=(vmem_whole(), vmem_whole()),
        compiler_params=params(16),
    )(*scalars, tiles, cotangent)
    got = lax.all_to_all(chunks, "tile", 0, 0, tiled=True)

    slope, share = pl.pallas_call(
        local_kernel,
        grid=(blocks,),
        out_shape=(
            jax.ShapeDtypeStruct((side, kept, channels), F32),
            jax.ShapeDtypeStruct((devices, blocks, BLOCK), F32),
        ),
        in_specs=[smem_whole()] * 4
        + [
            pl.BlockSpec((1, slots, side, side, BLOCK), lambda j: (0, 0, 0, 0, j)),
            pl.BlockSpec((taps, width, BLOCK), lambda j: (0, 0, j)),
        ],
        out_specs=(
            pl.BlockSpec((side, kept, BLOCK), lambda j: (0, 0, j)),
            pl.BlockSpec((devices, blocks, BLOCK), lambda j: (0, 0, 0)),
        ),
        scratch_shapes=[pltpu.VMEM((3, (side + 2) * pitch, BLOCK), BF16)],
        compiler_params=params(24),
        cost_estimate=cost(8 * macs, 4 * 2**20),
    )(*scalars, tiles, conv_weight)
    shares = lax.all_to_all(share, "tile", 0, 0, tiled=True)

    own_weight = lax.dynamic_slice_in_dim(conv_weight, mine[0] * lanes, lanes, 2)
    if packed:
        extra = ()
        cot_args = (got, got)
        cot_specs = [
            pl.BlockSpec((devices, 1, 1, ROW, lanes), lambda j: (0, j // side, j % side, 0, 0)),
            pl.BlockSpec(
                (devices, 1, 1, ROW, lanes), lambda j: (0, devices // side, devices % side, 0, 0)
            ),
        ]
    else:
        cot_all = lax.all_gather(cotangent[0], "tile", axis=0, tiled=True).astype(F32)
        info_all = lax.all_gather(info, "tile", axis=0, tiled=True)
        extra = (lax.dynamic_slice_in_dim(cot_all, mine[0] * lanes, lanes, 1), info_all)
        cot_args = (cot_all, info_all)
        cot_specs = [
            pl.BlockSpec((devices, BLOCK), lambda j: (0, j)),
            pl.BlockSpec((devices, 128), lambda j: (0, 0)),
        ]
    pitch_all = slots * devices * ROW
    terms = pl.pallas_call(
        functools.partial(weight_kernel, packed),
        out_shape=jax.ShapeDtypeStruct((taps, width, lanes), F32),
        in_specs=[smem_whole()] + [vmem_whole()] * (2 + len(extra)),
        out_specs=vmem_whole(),
        scratch_shapes=[
            pltpu.VMEM((3, (side + 2) * pitch_all, lanes), BF16),
            pltpu.VMEM(((side + 2) * pitch_all, lanes), BF16),
        ],
        compiler_params=params(32),
        cost_estimate=cost(16 * macs, 4 * 2**20),
    )(mine, got, own_weight, *extra)

    own, other = exchange_sum(terms, "slide", 1)
    total = own + other
    step = 2
    while step < lax.axis_size("slide"):
        own, other = exchange_sum(total.astype(BF16), "slide", step)
        total = own.astype(F32) + other.astype(F32)
        step *= 2
    weight_grads = total / LOSS_SCALE

    grads, pooled = pl.pallas_call(
        functools.partial(input_kernel, packed),
        grid=(blocks,),
        out_shape=(
            jax.ShapeDtypeStruct((slots, side, side, 1, channels), F32),
            jax.ShapeDtypeStruct((1, 1, channels), F32),
        ),
        in_specs=[smem_whole()] * 5
        + [
            pl.BlockSpec((side, kept, BLOCK), lambda j: (0, 0, j)),
            pl.BlockSpec((taps, width, BLOCK), lambda j: (0, 0, j)),
        ]
        + cot_specs
        + [pl.BlockSpec((devices, blocks, BLOCK), lambda j: (0, 0, 0))],
        out_specs=(
            pl.BlockSpec((slots, side, side, 1, BLOCK), lambda j: (0, 0, 0, 0, j)),
            pl.BlockSpec((1, 1, BLOCK), lambda j: (0, 0, j)),
        ),
        scratch_shapes=[pltpu.VMEM((3, (side + 2) * pitch, BLOCK), BF16)],
        compiler_params=params(24),
        cost_estimate=cost(8 * macs, 4 * 2**20),
    )(mine, *scalars, slope, conv_weight, *cot_args, shares)
    input_grads = jnp.transpose(grads, (3, 0, 1, 2, 4))
    return (pooled, input_grads, weight_grads)


def solution(mesh):
    return jax.shard_map(
        shards,
        mesh=mesh,
        in_specs=(
            P("slide", "tile", None, None, None),
            P("slide", "tile"),
            P("slide", "tile"),
            P("slide", "tile", None),
            P("slide", None),
            P("slide", "tile", None),
            P(),
        ),
        out_specs=(
            P("slide", "tile", None),
            P("slide", "tile", None, None, None),
            P(None, None, "tile"),
        ),
        check_vma=False,
    )
```

profile of v0, /device:TPU:0, one launch (start us, length us, event | category | flops | bytes accessed | tf_op | source)
XLA Modules:
  0.0 67.0 jit_solution(12977454623228778674)
XLA Ops:
  1.3 0.0 copy-start.1
  1.3 1.1 %copy-done.1 = bf16[1,3,7,7,2048]{4,3,2,1,0:T(8,128)(2,1)S(1)} copy-done((bf16[1,3,7,7,2048]{4,3,2,1,0:T(8,128)(2,1)S(1)}, bf16[1,3,7,7,2048]{4,3,2,1,0:T(8,128)(2,1)}, u32[]{:S(2)}) %copy-start.1) | copy-done | bytes 602136
  2.4 0.7 %copy-done.3 = bf16[1,1,2048]{2,1,0:T(2,128)(2,1)S(1)} copy-done((bf16[1,1,2048]{2,1,0:T(2,128)(2,1)S(1)}, bf16[1,1,2048]{2,1,0:T(2,128)(2,1)}, u32[]{:S(2)}) %copy-start.3) | copy-done | bytes 4120
  3.1 0.7 copy-done.4
  3.7 0.7 copy-done.6
  4.4 0.7 copy-done.8
  5.0 1.5 %shard_map.95 = (bf16[8,3,7,8,256]{4,3,2,1,0:T(8,128)(2,1)}, f32[1,256]{1,0:T(1,128)}) custom-call(s32[1,1]{1,0:T(1,128)S(6)} %copy.10.counts_ref, f32[1,3]{1,0:T(1,128)S(1)} %copy-done.4, s32[1,3]{1,0:T(1,128)S(1)} %bitcast.3, s32[1,8]{1,0:T(1,128)S(1)} %copy-done.8, bf16[1,3,7,7,2048]{4,3,2,1,0:T(8,128)(2,1)S(1)} %copy-done.1, ...), custom_call_target="tpu_custom_call" | custom-call | tf_op jit(solution)/shard_map/pallas_call | solution.py:347
  6.6 7.3 %all-to-all-start = ((bf16[8,3,7,8,256]{4,3,2,1,0:T(8,128)(2,1)}), bf16[8,3,7,8,256]{4,3,2,1,0:T(8,128)(2,1)S(1)}, u32[]{:S(2)}, u32[]{:S(2)}) async-start(bf16[8,3,7,8,256]{4,3,2,1,0:T(8,128)(2,1)} %get-tuple-element.9), calls=%async_computation | async-start | bytes 1376256 | tf_op jit(solution)/shard_map/all_to_all | solution.py:357
  13.8 1.0 %constant_dynamic-slice_fusion.w_ref = bf16[9,64,256]{2,1,0:T(8,128)(2,1)S(1)} fusion(bf16[9,64,2048]{2,1,0:T(8,128)(2,1)} %w_ref.3, s32[]{:T(128)S(6)} %select_n.3), kind=kLoop, calls=%fused_computation.2 | loop fusion | bytes 589828 | tf_op jit(solution)/shard_map/dynamic_slice | solution.py:381
  14.8 17.0 %all-to-all-done.cot_ref.info_ref.got_ref = bf16[8,3,7,8,256]{4,3,2,1,0:T(8,128)(2,1)S(1)} async-done(((bf16[8,3,7,8,256]{4,3,2,1,0:T(8,128)(2,1)}), bf16[8,3,7,8,256]{4,3,2,1,0:T(8,128)(2,1)S(1)}, u32[]{:S(2)}, u32[]{:S(2)}) %all-to-all-start) | async-done | bytes 688160 | tf_op jit(solution)/shard_map/all_to_all | solution.py:357
  31.8 0.0 copy-start.9
  31.8 6.4 %shard_map.97 = f32[9,64,256]{2,1,0:T(8,128)S(1)} custom-call(s32[1]{0:T(128)} %bitcast.my_ref, bf16[8,3,7,8,256]{4,3,2,1,0:T(8,128)(2,1)S(1)} %all-to-all-done.cot_ref.info_ref.got_ref, bf16[9,64,256]{2,1,0:T(8,128)(2,1)S(1)} %constant_dynamic-slice_fusion.w_ref), custom_call_target="tpu_custom_call" | custom-call | flops 2774532096 | bytes 4194304 | tf_op jit(solution)/shard_map/pallas_call | solution.py:401
  38.2 0.1 collective-permute-start
  38.3 2.0 %collective-permute-done = f32[9,64,256]{2,1,0:T(8,128)S(1)} collective-permute-done((f32[9,64,256]{2,1,0:T(8,128)S(1)}, f32[9,64,256]{2,1,0:T(8,128)S(1)}, u32[]{:S(2)}, u32[]{:S(2)}) %collective-permute-start) | collective-permute-done | bytes 589856 | tf_op jit(solution)/shard_map/ppermute | solution.py:330
  40.3 0.1 add_convert_fusion
  40.4 1.6 %collective-permute-start.1 = (bf16[9,64,256]{2,1,0:T(8,128)(2,1)S(1)}, bf16[9,64,256]{2,1,0:T(8,128)(2,1)S(1)}, u32[]{:S(2)}, u32[]{:S(2)}) collective-permute-start(bf16[9,64,256]{2,1,0:T(8,128)(2,1)S(1)} %add_convert_fusion), channel_id=1, source_target_pairs={{0,2},{1,3},{2,0},{3,1},{4,6},{5,7},{6,4},{7,5},{8,10},{9,11},{10,... | collective-permute-start | bytes 884744 | tf_op jit(solution)/shard_map/ppermute | solution.py:330
  42.0 0.0 copy-done
  42.0 0.0 copy-done.2
  42.0 0.0 copy-done.5
  42.0 5.3 %shard_map.94 = (f32[7,24,2048]{2,1,0:T(8,128)S(1)}, f32[8,8,256]{2,1,0:T(8,128)S(1)}) custom-call(s32[1,1]{1,0:T(1,128)S(6)} %copy.10.counts_ref, f32[1,3]{1,0:T(1,128)S(1)} %copy-done.5, s32[1,3]{1,0:T(1,128)S(1)} %bitcast.4, s32[1,8]{1,0:T(1,128)S(1)} %copy-done.9, bf16[1,3,7,7,2048]{4,3,2,1,0:T(8,128)(2,1)S(1)} %copy-done.2, bf16[9,64,2048]{2,1,0:T(8,128)(2,1)S(1)} %copy-done), custom_call_target="tpu_custom_call" | custom-call | flops 1387266048 | bytes 4194304 | tf_op jit(solution)/shard_map/pallas_call | solution.py:359
  47.3 10.3 %all_to_all.10.share_ref = f32[8,8,256]{2,1,0:T(8,128)S(1)} all-to-all(f32[8,8,256]{2,1,0:T(8,128)S(1)} %get-tuple-element.10), channel_id=1, replica_groups=mesh['tile'=8,'slide'=4] {'tile'}, dimensions={0} | all-to-all | bytes 131072 | tf_op jit(solution)/shard_map/all_to_all | solution.py:379
  57.7 8.4 %shard_map.96 = (f32[3,7,7,1,2048]{4,3,2,1,0:T(1,128)}, f32[1,1,2048]{2,1,0:T(1,128)}) custom-call(s32[1]{0:T(128)} %bitcast.my_ref, s32[1,1]{1,0:T(1,128)S(6)} %copy.10.counts_ref, f32[1,3]{1,0:T(1,128)S(1)} %copy-done.5, s32[1,3]{1,0:T(1,128)S(1)} %bitcast.5, s32[1,8]{1,0:T(1,128)S(1)} %copy-done.9, f32[7,24,2048]{2,1,0:T(8,128)S(1)} %get-tuple-element.8.slope_ref, ...), custom_call_target="tpu_custom_call" | custom-call | flops 1387266048 | bytes 4194304 | tf_op jit(solution)/shard_map/pallas_call | solution.py:423
  66.1 0.0 collective-permute-done.1
  66.1 0.9 %add_multiply_fusion = f32[9,64,256]{2,1,0:T(8,128)} fusion(bf16[9,64,256]{2,1,0:T(8,128)(2,1)S(1)} %collective-permute-done.1, bf16[9,64,256]{2,1,0:T(8,128)(2,1)S(1)} %add_convert_fusion), kind=kLoop, calls=%fused_computation | loop fusion | flops 589824 | bytes 1179648 | tf_op jit(solution)/shard_map/div | solution.py:421
  (10 shorter events, 0.0 us)
Async XLA Ops:
  1.3 1.1 %copy-start.1 = (bf16[1,3,7,7,2048]{4,3,2,1,0:T(8,128)(2,1)S(1)}, bf16[1,3,7,7,2048]{4,3,2,1,0:T(8,128)(2,1)}, u32[]{:S(2)}) copy-start(bf16[1,3,7,7,2048]{4,3,2,1,0:T(8,128)(2,1)} %x_ref.3) | copy-start | bytes 1806340
  2.4 0.7 %copy-start.3 = (bf16[1,1,2048]{2,1,0:T(2,128)(2,1)S(1)}, bf16[1,1,2048]{2,1,0:T(2,128)(2,1)}, u32[]{:S(2)}) copy-start(bf16[1,1,2048]{2,1,0:T(2,128)(2,1)} %cot_ref.1) | copy-start | bytes 12292
  3.1 0.7 copy-start.4
  3.7 0.7 copy-start.6
  4.4 0.7 copy-start.8
  6.6 25.3 %all-to-all-start = ((bf16[8,3,7,8,256]{4,3,2,1,0:T(8,128)(2,1)}), bf16[8,3,7,8,256]{4,3,2,1,0:T(8,128)(2,1)S(1)}, u32[]{:S(2)}, u32[]{:S(2)}) async-start(bf16[8,3,7,8,256]{4,3,2,1,0:T(8,128)(2,1)} %get-tuple-element.9), calls=%async_computation | async-start | bytes 1376256 | tf_op jit(solution)/shard_map/all_to_all | solution.py:357
  31.8 10.2 %copy-start = (bf16[9,64,2048]{2,1,0:T(8,128)(2,1)S(1)}, bf16[9,64,2048]{2,1,0:T(8,128)(2,1)}, u32[]{:S(2)}) copy-start(bf16[9,64,2048]{2,1,0:T(8,128)(2,1)} %w_ref.3) | copy-start | bytes 7077892
  31.8 10.2 %copy-start.2 = (bf16[1,3,7,7,2048]{4,3,2,1,0:T(8,128)(2,1)S(1)}, bf16[1,3,7,7,2048]{4,3,2,1,0:T(8,128)(2,1)}, u32[]{:S(2)}) copy-start(bf16[1,3,7,7,2048]{4,3,2,1,0:T(8,128)(2,1)} %x_ref.3) | copy-start | bytes 1806340
  31.8 10.2 %copy-start.5 = (f32[1,3]{1,0:T(1,128)S(1)}, f32[1,3]{1,0:T(1,128)}, u32[]{:S(2)}) copy-start(f32[1,3]{1,0:T(1,128)} %weights_ref.5) | copy-start | bytes 40
  31.8 10.2 %copy-start.7 = (s32[1,3,1]{1,2,0:T(1,128)S(1)}, s32[1,3,1]{1,2,0:T(1,128)}, u32[]{:S(2)}) copy-start(s32[1,3,1]{1,2,0:T(1,128)} %param.10) | copy-start | bytes 40
  31.8 10.2 %copy-start.9 = (s32[1,8]{1,0:T(1,128)S(1)}, s32[1,8]{1,0:T(1,128)}, u32[]{:S(2)}) copy-start(s32[1,8]{1,0:T(1,128)} %owner_ref.5) | copy-start | bytes 100
  38.2 2.1 %collective-permute-start = (f32[9,64,256]{2,1,0:T(8,128)S(1)}, f32[9,64,256]{2,1,0:T(8,128)S(1)}, u32[]{:S(2)}, u32[]{:S(2)}) collective-permute-start(f32[9,64,256]{2,1,0:T(8,128)S(1)} %shard_map.97), channel_id=1, source_target_pairs={{0,1},{1,0},{2,3},{3,2},{4,5},{5,4},{6,7},{7,6},{8,9},{9,8},{10,11... | collective-permute-start | bytes 1769480 | tf_op jit(solution)/shard_map/ppermute | solution.py:330
  40.4 25.7 %collective-permute-start.1 = (bf16[9,64,256]{2,1,0:T(8,128)(2,1)S(1)}, bf16[9,64,256]{2,1,0:T(8,128)(2,1)S(1)}, u32[]{:S(2)}, u32[]{:S(2)}) collective-permute-start(bf16[9,64,256]{2,1,0:T(8,128)(2,1)S(1)} %add_convert_fusion), channel_id=1, source_target_pairs={{0,2},{1,3},{2,0},{3,1},{4,6},{5,7},{6,4},{7,5},{8,10},{9,11},{10,... | collective-permute-start | bytes 884744 | tf_op jit(solution)/shard_map/ppermute | solution.py:330
where the time goes:
time: 67.4 us; the launch traced here: 67 us
  Pallas kernels  21.6 us (32%)
  waiting for transfers between devices  19 us (28%)
  blocking collectives  10.3 us (15%)
  starting transfers between devices  8.91 us (13%)
  local copies, waits for them, and re-layouts  4.76 us (7%)
  between operations  1.35 us (2%)
  other arithmetic  1.01 us (1%)
    all_to_all x1, waiting for transfers between devices, shards(): got = lax.all_to_all(chunks, 'tile', 0, 0, tiled=True)  17 us
    all_to_all x1, blocking collectives, shards(): shares = lax.all_to_all(share, 'tile', 0, 0, tiled=True)  10.3 us
    pallas_call x1, Pallas kernels, shards(): pl.pallas_call(functools.partial(input_kernel, packed), grid=(blocks,), o...  8.4 us
    all_to_all x1, starting transfers between devices, shards(): got = lax.all_to_all(chunks, 'tile', 0, 0, tiled=True)  7.25 us
    pallas_call x1, Pallas kernels, shards(): pl.pallas_call(functools.partial(weight_kernel, packed), out_shape=jax.Sh...  6.39 us
    pallas_call x1, Pallas kernels, shards(): pl.pallas_call(local_kernel, grid=(blocks,), out_shape=(jax.ShapeDtypeStr...  5.3 us
    unnamed x20, local copies, waits for them, and re-layouts  3.78 us
    ppermute x2, waiting for transfers between devices, exchange_sum(): lax.ppermute(value, axis, [(i, i ^ step) for i in range(count)])  1.99 us
  transfers between devices with their start and end apart: 3, of which 2 were waited for; matrix products, arithmetic and copies ran while one was open for 1% of the time, Pallas kernels for 20%

commit v1 on v0

--- a/solution.py
+++ b/solution.py
@@ -106,11 +106,31 @@
     return jnp.where((lane >= 2 * slots) & (lane < 3 * slots), low, value)
 
 
-def pack_kernel(packed, counts_ref, weights_ref, slide_ref, owner_ref, x_ref, cot_ref, out_ref, info_ref):
+def own_row(coefs, targets):
+    slots = len(coefs)
+    lane = lax.broadcasted_iota(jnp.int32, (1, 128), 1)
+    value = jnp.zeros((1, 128), F32)
+    for slot in range(slots):
+        value = jnp.where(lane == slot, coefs[slot], value)
+        value = jnp.where(lane == slots + slot, targets[slot].astype(F32), value)
+    return value
+
+
+def own_route(own, slots, owner):
+    return [
+        jnp.where(own[:, slots + slot : slots + slot + 1] == owner, own[:, slot : slot + 1], 0.0)
+        for slot in range(slots)
+    ]
+
+
+def pack_kernel(
+    packed, counts_ref, weights_ref, slide_ref, owner_ref, x_ref, cot_ref, out_ref, info_ref, own_ref
+):
     devices, slots, side, _, lanes = out_ref.shape
     coefs, targets = own_scalars(counts_ref, weights_ref, slide_ref, owner_ref, slots)
     info = info_row(coefs, targets, info_ref.shape[1])
     info_ref[...] = info
+    own_ref[...] = own_row(coefs, targets)
     cot = cot_ref[0].astype(F32)
     for slot in range(slots):
         for high in range(side):
@@ -127,13 +147,12 @@
                 out_ref[device, slot, high] = jnp.concatenate([part, spare], axis=0).astype(BF16)
 
 
-def local_kernel(
-    counts_ref, weights_ref, slide_ref, owner_ref, x_ref, w_ref, slope_ref, share_ref, rows_ref
-):
+def local_kernel(my_ref, own_ref, x_ref, w_ref, slope_ref, *refs):
+    *share_refs, rows_ref = refs
     step = pl.program_id(0)
     side, kept, lanes = slope_ref.shape
     slots = kept // ROW
-    devices = share_ref.shape[0]
+    devices = len(share_refs) * share_refs[0].shape[0]
     pitch = rows_ref.shape[1] // (side + 2)
     width = w_ref.shape[1]
     for col in range(3):
@@ -165,17 +184,19 @@
         slope_ref[high] = slope[high * pitch : high * pitch + kept]
         total = total + active[high * pitch : (high + 1) * pitch]
     place = lax.broadcasted_iota(jnp.int32, (ROW, lanes), 0)
-    coefs, targets = own_scalars(counts_ref, weights_ref, slide_ref, owner_ref, slots)
+    own = own_ref[...]
     means = []
     for slot in range(slots):
         here = jnp.where(place < side, total[slot * ROW : (slot + 1) * ROW], 0.0)
         mean = jnp.sum(here, axis=0, keepdims=True) / (side * side)
         means.append(mean.astype(BF16).astype(F32))
-    for owner in range(devices):
+    for index in range(devices):
+        owner = index if len(share_refs) == 1 else my_ref[0] ^ index
         share = jnp.zeros((1, lanes), F32)
-        for slot in range(slots):
-            share = share + jnp.where(targets[slot] == owner, coefs[slot], 0.0) * means[slot]
-        share_ref[owner, pl.ds(step, 1), :] = share
+        for mean, weight in zip(means, own_route(own, slots, jnp.float32(owner))):
+            share = share + weight * mean
+        place_ref = share_refs[index % len(share_refs)]
+        place_ref[index // len(share_refs), pl.ds(step, 1), :] = share
 
 
 def weight_kernel(packed, my_ref, got_ref, w_ref, *refs):
@@ -249,23 +270,18 @@
 def input_kernel(
     packed,
     my_ref,
-    counts_ref,
-    weights_ref,
-    slide_ref,
-    owner_ref,
+    own_ref,
     slope_ref,
     w_ref,
     cot_ref,
     info_ref,
-    share_ref,
-    out_ref,
-    pooled_ref,
-    rows_ref,
+    *refs,
 ):
+    *share_refs, out_ref, pooled_ref, rows_ref = refs
     step = pl.program_id(0)
     side, kept, lanes = slope_ref.shape
     slots = kept // ROW
-    devices = share_ref.shape[0]
+    devices = cot_ref.shape[0]
     pitch = rows_ref.shape[1] // (side + 2)
     width = w_ref.shape[1]
     if packed:
@@ -278,17 +294,18 @@
     scaled = scaled_rows(cot, denominator)
     owners = lax.broadcasted_iota(jnp.int32, (1, 128), 1)
     mine = jnp.sum(jnp.where(owners == my_ref[0], denominator, 0.0), axis=1, keepdims=True)
-    shares = share_ref[:, pl.ds(step, 1), :]
-    pooled_ref[0] = jnp.sum(shares, axis=0) / mine
-
-    coefs, targets = own_scalars(counts_ref, weights_ref, slide_ref, owner_ref, slots)
+    shares = [jnp.sum(ref[:, pl.ds(step, 1), :], axis=0) for ref in share_refs]
+    pooled_ref[0] = sum(shares[1:], shares[0]) / mine
+
     place = lax.broadcasted_iota(jnp.int32, (ROW, lanes), 0)
+    own = own_ref[...]
     pieces = []
-    for slot in range(slots):
-        row = jnp.zeros((1, lanes), F32)
-        for owner in range(devices):
-            row = row + jnp.where(targets[slot] == owner, coefs[slot], 0.0) * scaled[owner]
-        spread = jnp.broadcast_to(row, (ROW, lanes)) / (side * side)
+    sums = [jnp.zeros((1, lanes), F32)] * slots
+    for owner in range(devices):
+        weights = own_route(own, slots, owner)
+        sums = [sums[slot] + weights[slot] * scaled[owner] for slot in range(slots)]
+    for slot in range(slots):
+        spread = jnp.broadcast_to(sums[slot], (ROW, lanes)) / (side * side)
         pieces.append(jnp.where(place < side, spread, 0.0))
     tile_grad = jnp.concatenate(pieces, axis=0)
 
@@ -325,9 +342,8 @@
     return pl.CostEstimate(flops=flops, bytes_accessed=moved, transcendentals=0)
 
 
-def exchange_sum(value, axis, step):
-    count = lax.axis_size(axis)
-    return value, lax.ppermute(value, axis, [(i, i ^ step) for i in range(count)])
+def swap(value, axis, step):
+    return lax.ppermute(value, axis, [(i, i ^ step) for i in range(lax.axis_size(axis))])
 
 
 def shards(tiles, tile_counts, tile_weights, slide_of, owner_map, cotangent, conv_weight):
@@ -344,39 +360,52 @@
     pitch = -(-kept // 16) * 16
     macs = slots * side * side * taps * width * channels
 
-    chunks, info = pl.pallas_call(
+    chunks, info, routes = pl.pallas_call(
         functools.partial(pack_kernel, packed),
         out_shape=(
             jax.ShapeDtypeStruct((devices, slots, side, ROW, lanes), BF16),
             jax.ShapeDtypeStruct((1, max(lanes, 128)), F32),
+            jax.ShapeDtypeStruct((1, 128), F32),
         ),
         in_specs=[smem_whole()] * 4 + [vmem_whole()] * 2,
-        out_specs=(vmem_whole(), vmem_whole()),
-        compiler_params=params(16),
+        out_specs=(vmem_whole(), vmem_whole(), vmem_whole()),
+        compiler_params=params(56),
     )(*scalars, tiles, cotangent)
     got = lax.all_to_all(chunks, "tile", 0, 0, tiled=True)
 
-    slope, share = pl.pallas_call(
+    halves = 2 if packed else 1
+    slope, *sent = pl.pallas_call(
         local_kernel,
         grid=(blocks,),
         out_shape=(
             jax.ShapeDtypeStruct((side, kept, channels), F32),
-            jax.ShapeDtypeStruct((devices, blocks, BLOCK), F32),
-        ),
-        in_specs=[smem_whole()] * 4
-        + [
+        )
+        + (jax.ShapeDtypeStruct((devices // halves, blocks, BLOCK), F32),) * halves,
+        in_specs=[
+            smem_whole(),
+            pl.BlockSpec((1, 128), lambda j: (0, 0)),
             pl.BlockSpec((1, slots, side, side, BLOCK), lambda j: (0, 0, 0, 0, j)),
             pl.BlockSpec((taps, width, BLOCK), lambda j: (0, 0, j)),
         ],
         out_specs=(
             pl.BlockSpec((side, kept, BLOCK), lambda j: (0, 0, j)),
-            pl.BlockSpec((devices, blocks, BLOCK), lambda j: (0, 0, 0)),
-        ),
+        )
+        + (pl.BlockSpec((devices // halves, blocks, BLOCK), lambda j: (0, 0, 0)),) * halves,
         scratch_shapes=[pltpu.VMEM((3, (side + 2) * pitch, BLOCK), BF16)],
-        compiler_params=params(24),
+        compiler_params=params(56),
         cost_estimate=cost(8 * macs, 4 * 2**20),
-    )(*scalars, tiles, conv_weight)
-    shares = lax.all_to_all(share, "tile", 0, 0, tiled=True)
+    )(mine, routes, tiles, conv_weight)
+    if packed:
+        toward = sent[0] + swap(sent[1], "tile", 1)
+    else:
+        toward = sent[0]
+
+    got, slope, _ = lax.optimization_barrier((got, slope, toward))
+    if packed:
+        shares = [toward[:1]]
+        shares += [swap(toward[i : i + 1], "tile", 2 * i) for i in range(1, devices // 2)]
+    else:
+        shares = [lax.all_to_all(toward, "tile", 0, 0, tiled=True)]
 
     own_weight = lax.dynamic_slice_in_dim(conv_weight, mine[0] * lanes, lanes, 2)
     if packed:
@@ -411,12 +440,12 @@
         cost_estimate=cost(16 * macs, 4 * 2**20),
     )(mine, got, own_weight, *extra)
 
-    own, other = exchange_sum(terms, "slide", 1)
-    total = own + other
+    terms, shares = lax.optimization_barrier((terms, shares))
+    total = terms + swap(terms, "slide", 1)
     step = 2
     while step < lax.axis_size("slide"):
-        own, other = exchange_sum(total.astype(BF16), "slide", step)
-        total = own.astype(F32) + other.astype(F32)
+        sent = total.astype(BF16)
+        total = sent.astype(F32) + swap(sent, "slide", step).astype(F32)
         step *= 2
     weight_grads = total / LOSS_SCALE
 
@@ -427,13 +456,14 @@
             jax.ShapeDtypeStruct((slots, side, side, 1, channels), F32),
             jax.ShapeDtypeStruct((1, 1, channels), F32),
         ),
-        in_specs=[smem_whole()] * 5
-        + [
+        in_specs=[
+            smem_whole(),
+            pl.BlockSpec((1, 128), lambda j: (0, 0)),
             pl.BlockSpec((side, kept, BLOCK), lambda j: (0, 0, j)),
             pl.BlockSpec((taps, width, BLOCK), lambda j: (0, 0, j)),
         ]
         + cot_specs
-        + [pl.BlockSpec((devices, blocks, BLOCK), lambda j: (0, 0, 0))],
+        + [pl.BlockSpec((part.shape[0], blocks, BLOCK), lambda j: (0, 0, 0)) for part in shares],
         out_specs=(
             pl.BlockSpec((slots, side, side, 1, BLOCK), lambda j: (0, 0, 0, 0, j)),
             pl.BlockSpec((1, 1, BLOCK), lambda j: (0, 0, j)),
@@ -441,7 +471,7 @@
         scratch_shapes=[pltpu.VMEM((3, (side + 2) * pitch, BLOCK), BF16)],
         compiler_params=params(24),
         cost_estimate=cost(8 * macs, 4 * 2**20),
-    )(mine, *scalars, slope, conv_weight, *cot_args, shares)
+    )(mine, routes, slope, conv_weight, *cot_args, *shares)
     input_grads = jnp.transpose(grads, (3, 0, 1, 2, 4))
     return (pooled, input_grads, weight_grads)
 

time: 67.4 us -> 48 us (0.71)
  waiting for transfers between devices: 19 us -> 5.24 us
  blocking collectives: 10.3 us -> 0 us
  starting transfers between devices: 8.91 us -> 15.4 us
  local copies, waits for them, and re-layouts: 4.76 us -> 0.06 us
  Pallas kernels: 21.6 us -> 23.8 us
  other arithmetic: 1.01 us -> 1.77 us
    all_to_all x1, waiting for transfers between devices: 17 us -> 0.82 us  [shards(): got = lax.all_to_all(chunks, 'tile', 0, 0, tiled=True)]
    all_to_all x1 -> x0, blocking collectives: 10.3 us -> none  [shards(): shares = lax.all_to_all(share, 'tile', 0, 0, tiled=True)]
    ppermute x2 -> x6, starting transfers between devices: 1.65 us -> 8.12 us  [swap(): lax.ppermute(value, axis, [(i, i ^ step) for i in range(lax.axis_size(axi...]
    unnamed x20 -> x6, local copies, waits for them, and re-layouts: 3.78 us -> 0.01 us
    pallas_call x1, Pallas kernels: 5.3 us -> 7.74 us  [shards(): pl.pallas_call(local_kernel, grid=(blocks,), out_shape=(jax.ShapeDtypeStr...]
    ppermute x2 -> x6, waiting for transfers between devices: 1.99 us -> 4.41 us  [swap(): lax.ppermute(value, axis, [(i, i ^ step) for i in range(lax.axis_size(axi...]
    dynamic_slice x1, local copies, waits for them, and re-layouts: 0.98 us -> 0.04 us  [shards(): lax.dynamic_slice_in_dim(conv_weight, mine[0] * lanes, lanes, 2)]
    pallas_call x1, Pallas kernels: 8.4 us -> 7.54 us  [shards(): pl.pallas_call(functools.partial(input_kernel, packed), grid=(blocks,), o...]
  transfers between devices with their start and end apart: 3 -> 7, of which waited for: 2 -> 3; matrix products, arithmetic and copies ran while one was open for 1% -> 2% of each run, Pallas kernels for 20% -> 46%
where the time goes in v1:
time: 48 us; the launch traced here: 47.5 us
  Pallas kernels  23.8 us (50%)
  starting transfers between devices  15.4 us (32%)
  waiting for transfers between devices  5.24 us (11%)
  other arithmetic  1.77 us (4%)
  between operations  1.34 us (3%)
    ppermute x6, starting transfers between devices, swap(): lax.ppermute(value, axis, [(i, i ^ step) for i in range(lax.axis_size(axi...  8.12 us
    pallas_call x1, Pallas kernels, shards(): pl.pallas_call(local_kernel, grid=(blocks,), out_shape=(jax.ShapeDtypeStr...  7.74 us
    pallas_call x1, Pallas kernels, shards(): pl.pallas_call(functools.partial(input_kernel, packed), grid=(blocks,), o...  7.54 us
    all_to_all x1, starting transfers between devices, shards(): got = lax.all_to_all(chunks, 'tile', 0, 0, tiled=True)  7.25 us
    pallas_call x1, Pallas kernels, shards(): pl.pallas_call(functools.partial(weight_kernel, packed), out_shape=jax.Sh...  6.39 us
    ppermute x6, waiting for transfers between devices, swap(): lax.ppermute(value, axis, [(i, i ^ step) for i in range(lax.axis_size(axi...  4.41 us
    pallas_call x1, Pallas kernels, shards(): pl.pallas_call(functools.partial(pack_kernel, packed), out_shape=(jax.Sha...  2.09 us
  transfers between devices with their start and end apart: 7, of which 3 were waited for; matrix products, arithmetic and copies ran while one was open for 2% of the time, Pallas kernels for 46%

profile of v1, /device:TPU:0, one launch (start us, length us, event | category | flops | bytes accessed | tf_op | source)
XLA Modules:
  0.0 47.5 jit_solution(16939650867810038515)
XLA Ops:
  1.3 2.1 %shard_map.94 = (bf16[8,3,7,8,256]{4,3,2,1,0:T(8,128)(2,1)}, f32[1,256]{1,0:T(1,128)}, f32[1,128]{1,0:T(1,128)}) custom-call(s32[1,1]{1,0:T(1,128)S(6)} %copy.10.counts_ref, f32[1,3]{1,0:T(1,128)} %weights_ref.1, s32[1,3]{1,0:T(1,128)} %bitcast.3, s32[1,8]{1,0:T(1,128)} %owner_ref.1, bf16[1,3,7,7,2048]{4,3,2,1,0:T(8,128)(2,1)} %x_ref.3, ...), custom_call_target="tpu_custom_call" | custom-call | tf_op jit(solution)/shard_map/pallas_call | solution.py:363
  3.4 7.3 %all-to-all-start = ((bf16[8,3,7,8,256]{4,3,2,1,0:T(8,128)(2,1)}), bf16[8,3,7,8,256]{4,3,2,1,0:T(8,128)(2,1)S(1)}, u32[]{:S(2)}, u32[]{:S(2)}) async-start(bf16[8,3,7,8,256]{4,3,2,1,0:T(8,128)(2,1)} %get-tuple-element.18), calls=%async_computation | async-start | bytes 1376256 | tf_op jit(solution)/shard_map/all_to_all | solution.py:374
  10.6 7.7 %shard_map.95 = (f32[7,24,2048]{2,1,0:T(8,128)}, f32[4,8,256]{2,1,0:T(8,128)}, f32[4,8,256]{2,1,0:T(8,128)}) custom-call(s32[1]{0:T(128)} %bitcast.my_ref, f32[1,128]{1,0:T(1,128)} %get-tuple-element.17.own_ref, bf16[1,3,7,7,2048]{4,3,2,1,0:T(8,128)(2,1)} %x_ref.3, bf16[9,64,2048]{2,1,0:T(8,128)(2,1)} %w_ref.3), custom_call_target="tpu_custom_call" | custom-call | flops 1387266048 | bytes 4194304 | tf_op jit(solution)/shard_map/pallas_call | solution.py:377
  18.4 2.0 %collective-permute-start = (f32[4,8,256]{2,1,0:T(8,128)}, f32[4,8,256]{2,1,0:T(8,128)S(1)}, u32[]{:S(2)}, u32[]{:S(2)}) collective-permute-start(f32[4,8,256]{2,1,0:T(8,128)} %get-tuple-element.21), channel_id=1, source_target_pairs={{0,4},{4,0},{8,12},{12,8},{16,20},{20,16},{24,28},{28,24},{1,5},{5... | collective-permute-start | bytes 98312 | tf_op jit(solution)/shard_map/ppermute | solution.py:346
  20.4 0.0 copy-done
  20.4 2.4 %collective-permute-done = f32[4,8,256]{2,1,0:T(8,128)S(1)} collective-permute-done((f32[4,8,256]{2,1,0:T(8,128)}, f32[4,8,256]{2,1,0:T(8,128)S(1)}, u32[]{:S(2)}, u32[]{:S(2)}) %collective-permute-start) | collective-permute-done | bytes 32800 | tf_op jit(solution)/shard_map/ppermute | solution.py:346
  22.8 0.8 %add.12 = f32[4,8,256]{2,1,0:T(8,128)S(1)} add(f32[4,8,256]{2,1,0:T(8,128)} %get-tuple-element.20, f32[4,8,256]{2,1,0:T(8,128)S(1)} %collective-permute-done) | non-fusion elementwise | flops 8192 | bytes 98304 | tf_op jit(solution)/shard_map/add | solution.py:399
  23.6 3.5 %collective-permute-start.3 = (f32[1,8,256]{2,1,0:T(8,128)S(1)}, f32[1,8,256]{2,1,0:T(8,128)S(1)}, u32[]{:S(2)}, u32[]{:S(2)}) collective-permute-start(f32[1,8,256]{2,1,0:T(8,128)S(1)} %get-tuple-element.31), channel_id=1, source_target_pairs={{0,24},{4,28},{8,16},{12,20},{16,8},{20,12},{24,0},{28,4},{1,25},{... | collective-permute-start | bytes 24584 | tf_op jit(solution)/shard_map/ppermute | solution.py:346
  27.1 0.3 collective-permute-start.2
  27.5 0.6 %collective-permute-start.1 = (f32[1,8,256]{2,1,0:T(8,128)S(1)}, f32[1,8,256]{2,1,0:T(8,128)S(1)}, u32[]{:S(2)}, u32[]{:S(2)}) collective-permute-start(f32[1,8,256]{2,1,0:T(8,128)S(1)} %get-tuple-element.33), channel_id=1, source_target_pairs={{0,8},{4,12},{8,0},{12,4},{16,24},{20,28},{24,16},{28,20},{1,9},{5... | collective-permute-start | bytes 24584 | tf_op jit(solution)/shard_map/ppermute | solution.py:346
  28.1 0.8 %all-to-all-done.got_ref.cot_ref.info_ref = bf16[8,3,7,8,256]{4,3,2,1,0:T(8,128)(2,1)S(1)} async-done(((bf16[8,3,7,8,256]{4,3,2,1,0:T(8,128)(2,1)}), bf16[8,3,7,8,256]{4,3,2,1,0:T(8,128)(2,1)S(1)}, u32[]{:S(2)}, u32[]{:S(2)}) %all-to-all-start) | async-done | bytes 688160 | tf_op jit(solution)/shard_map/all_to_all | solution.py:374
  28.9 6.4 %shard_map.96 = f32[9,64,256]{2,1,0:T(8,128)S(1)} custom-call(s32[1]{0:T(128)} %bitcast.my_ref, bf16[8,3,7,8,256]{4,3,2,1,0:T(8,128)(2,1)S(1)} %all-to-all-done.got_ref.cot_ref.info_ref, bf16[9,64,256]{2,1,0:T(8,128)(2,1)S(1)} %constant_dynamic-slice_fusion.w_ref), custom_call_target="tpu_custom_call" | custom-call | flops 2774532096 | bytes 4194304 | tf_op jit(solution)/shard_map/pallas_call | solution.py:430
  35.3 0.0 collective-permute-done.3.refs_3_
  35.3 0.0 collective-permute-done.2.refs_2_
  35.3 0.0 collective-permute-done.1.refs_1_
  35.3 0.1 collective-permute-start.4
  35.4 2.0 %collective-permute-done.4 = f32[9,64,256]{2,1,0:T(8,128)S(1)} collective-permute-done((f32[9,64,256]{2,1,0:T(8,128)S(1)}, f32[9,64,256]{2,1,0:T(8,128)S(1)}, u32[]{:S(2)}, u32[]{:S(2)}) %collective-permute-start.4) | collective-permute-done | bytes 589856 | tf_op jit(solution)/shard_map/ppermute | solution.py:346
  37.4 0.1 add_convert_fusion
  37.5 1.6 %collective-permute-start.5 = (bf16[9,64,256]{2,1,0:T(8,128)(2,1)S(1)}, bf16[9,64,256]{2,1,0:T(8,128)(2,1)S(1)}, u32[]{:S(2)}, u32[]{:S(2)}) collective-permute-start(bf16[9,64,256]{2,1,0:T(8,128)(2,1)S(1)} %add_convert_fusion), channel_id=1, source_target_pairs={{0,2},{1,3},{2,0},{3,1},{4,6},{5,7},{6,4},{7,5},{8,10},{9,11},{10,... | collective-permute-start | bytes 884744 | tf_op jit(solution)/shard_map/ppermute | solution.py:346
  39.1 0.0 copy-done.1
  39.1 0.0 copy-done.2
  39.1 7.5 %shard_map.97 = (f32[3,7,7,1,2048]{4,3,2,1,0:T(1,128)}, f32[1,1,2048]{2,1,0:T(1,128)}) custom-call(s32[1]{0:T(128)} %bitcast.my_ref, f32[1,128]{1,0:T(1,128)S(1)} %copy-done.2, f32[7,24,2048]{2,1,0:T(8,128)S(1)} %copy-done.1, bf16[9,64,2048]{2,1,0:T(8,128)(2,1)S(1)} %copy-done, bf16[8,3,7,8,256]{4,3,2,1,0:T(8,128)(2,1)S(1)} %all-to-all-done.got_ref.cot_ref.info_ref, ...), custom_call_target="tpu_custom_call" | custom-call | flops 1387266048 | bytes 4194304 | tf_op jit(solution)/shard_map/pallas_call | solution.py:452
  46.6 0.0 collective-permute-done.5
  46.6 0.9 %add_multiply_fusion = f32[9,64,256]{2,1,0:T(8,128)} fusion(bf16[9,64,256]{2,1,0:T(8,128)(2,1)S(1)} %collective-permute-done.5, bf16[9,64,256]{2,1,0:T(8,128)(2,1)S(1)} %add_convert_fusion), kind=kLoop, calls=%fused_computation | loop fusion | flops 589824 | bytes 1179648 | tf_op jit(solution)/shard_map/div | solution.py:450
  (5 shorter events, 0.1 us)
Async XLA Ops:
  3.4 25.5 %all-to-all-start = ((bf16[8,3,7,8,256]{4,3,2,1,0:T(8,128)(2,1)}), bf16[8,3,7,8,256]{4,3,2,1,0:T(8,128)(2,1)S(1)}, u32[]{:S(2)}, u32[]{:S(2)}) async-start(bf16[8,3,7,8,256]{4,3,2,1,0:T(8,128)(2,1)} %get-tuple-element.18), calls=%async_computation | async-start | bytes 1376256 | tf_op jit(solution)/shard_map/all_to_all | solution.py:374
  10.6 9.8 %copy-start = (bf16[9,64,2048]{2,1,0:T(8,128)(2,1)S(1)}, bf16[9,64,2048]{2,1,0:T(8,128)(2,1)}, u32[]{:S(2)}) copy-start(bf16[9,64,2048]{2,1,0:T(8,128)(2,1)} %w_ref.3) | copy-start | bytes 7077892
  18.4 4.5 %collective-permute-start = (f32[4,8,256]{2,1,0:T(8,128)}, f32[4,8,256]{2,1,0:T(8,128)S(1)}, u32[]{:S(2)}, u32[]{:S(2)}) collective-permute-start(f32[4,8,256]{2,1,0:T(8,128)} %get-tuple-element.21), channel_id=1, source_target_pairs={{0,4},{4,0},{8,12},{12,8},{16,20},{20,16},{24,28},{28,24},{1,5},{5... | collective-permute-start | bytes 98312 | tf_op jit(solution)/shard_map/ppermute | solution.py:346
  23.6 11.7 %collective-permute-start.3 = (f32[1,8,256]{2,1,0:T(8,128)S(1)}, f32[1,8,256]{2,1,0:T(8,128)S(1)}, u32[]{:S(2)}, u32[]{:S(2)}) collective-permute-start(f32[1,8,256]{2,1,0:T(8,128)S(1)} %get-tuple-element.31), channel_id=1, source_target_pairs={{0,24},{4,28},{8,16},{12,20},{16,8},{20,12},{24,0},{28,4},{1,25},{... | collective-permute-start | bytes 24584 | tf_op jit(solution)/shard_map/ppermute | solution.py:346
  27.1 8.2 %collective-permute-start.2 = (f32[1,8,256]{2,1,0:T(8,128)S(1)}, f32[1,8,256]{2,1,0:T(8,128)S(1)}, u32[]{:S(2)}, u32[]{:S(2)}) collective-permute-start(f32[1,8,256]{2,1,0:T(8,128)S(1)} %get-tuple-element.32), channel_id=1, source_target_pairs={{0,16},{4,20},{8,24},{12,28},{16,0},{20,4},{24,8},{28,12},{1,17},{... | collective-permute-start | bytes 24584 | tf_op jit(solution)/shard_map/ppermute | solution.py:346
  27.5 7.8 %collective-permute-start.1 = (f32[1,8,256]{2,1,0:T(8,128)S(1)}, f32[1,8,256]{2,1,0:T(8,128)S(1)}, u32[]{:S(2)}, u32[]{:S(2)}) collective-permute-start(f32[1,8,256]{2,1,0:T(8,128)S(1)} %get-tuple-element.33), channel_id=1, source_target_pairs={{0,8},{4,12},{8,0},{12,4},{16,24},{20,28},{24,16},{28,20},{1,9},{5... | collective-permute-start | bytes 24584 | tf_op jit(solution)/shard_map/ppermute | solution.py:346
  28.9 10.2 %copy-start.1 = (f32[7,24,2048]{2,1,0:T(8,128)S(1)}, f32[7,24,2048]{2,1,0:T(8,128)}, u32[]{:S(2)}) copy-start(f32[7,24,2048]{2,1,0:T(8,128)} %get-tuple-element.22.slope_ref) | copy-start | bytes 4128772
  28.9 10.2 %copy-start.2 = (f32[1,128]{1,0:T(1,128)S(1)}, f32[1,128]{1,0:T(1,128)}, u32[]{:S(2)}) copy-start(f32[1,128]{1,0:T(1,128)} %get-tuple-element.17.own_ref) | copy-start | bytes 1540
  35.3 2.1 %collective-permute-start.4 = (f32[9,64,256]{2,1,0:T(8,128)S(1)}, f32[9,64,256]{2,1,0:T(8,128)S(1)}, u32[]{:S(2)}, u32[]{:S(2)}) collective-permute-start(f32[9,64,256]{2,1,0:T(8,128)S(1)} %shard_map.96), channel_id=1, source_target_pairs={{0,1},{1,0},{2,3},{3,2},{4,5},{5,4},{6,7},{7,6},{8,9},{9,8},{10,11... | collective-permute-start | bytes 1769480 | tf_op jit(solution)/shard_map/ppermute | solution.py:346
  37.5 9.1 %collective-permute-start.5 = (bf16[9,64,256]{2,1,0:T(8,128)(2,1)S(1)}, bf16[9,64,256]{2,1,0:T(8,128)(2,1)S(1)}, u32[]{:S(2)}, u32[]{:S(2)}) collective-permute-start(bf16[9,64,256]{2,1,0:T(8,128)(2,1)S(1)} %add_convert_fusion), channel_id=1, source_target_pairs={{0,2},{1,3},{2,0},{3,1},{4,6},{5,7},{6,4},{7,5},{8,10},{9,11},{10,... | collective-permute-start | bytes 884744 | tf_op jit(solution)/shard_map/ppermute | solution.py:346

commit v2 on v1

--- a/solution.py
+++ b/solution.py
@@ -9,6 +9,7 @@
 
 LOSS_SCALE = 512.0
 BLOCK = 256
+STEP = 512
 ROW = 8
 F32 = jnp.float32
 BF16 = jnp.bfloat16
@@ -63,6 +64,72 @@
         term = lax.dot_general(rows, weight_of(offset), dims, preferred_element_type=F32)
         total = term if total is None else total + term
     return total
+
+
+def left_half(count):
+    return lax.broadcasted_iota(jnp.int32, (count, 128), 1) < 64
+
+
+def split(low, middle, high):
+    left = left_half(low.shape[0])
+    turned = pltpu.roll(middle, 64, 1)
+    first = (jnp.where(left, low, turned), jnp.where(left, high, 0.0))
+    second = (jnp.where(left, turned, low), jnp.where(left, 0.0, high))
+    return tuple(jnp.concatenate(parts, axis=1).astype(BF16) for parts in (first, second))
+
+
+def joined(first, second):
+    left = left_half(first.shape[0])
+    low = jnp.where(left, first[:, :128], second[:, :128])
+    middle = pltpu.roll(jnp.where(left, second[:, :128], first[:, :128]), 64, 1)
+    high = jnp.where(left, first[:, 128:], second[:, 128:])
+    return low, middle, high
+
+
+def pair_weights(w_ref, lanes, backward):
+    rows = []
+    for outer in (-1, 0, 1):
+        taps = []
+        for inner in (-1, 0, 1):
+            row, col = (-outer, -inner) if backward else (inner, outer)
+            taps.append(w_ref[3 * (row + 1) + col + 1, :, lanes].astype(F32))
+        rows.append(split(*taps))
+    empty = jnp.zeros(rows[0][0].shape, BF16)
+    first = jnp.concatenate([rows[0][0], rows[1][0], rows[2][0], empty], axis=0)
+    second = jnp.concatenate([rows[1][1], rows[0][1], empty, rows[2][1]], axis=0)
+    return first, second
+
+
+def pair_rows(rows):
+    return split(pltpu.roll(rows, 1, 0), rows, pltpu.roll(rows, rows.shape[0] - 1, 0))
+
+
+def pair_conv(first, second, weights, pitch, dims):
+    first = lax.dot_general(first, weights[0], dims, preferred_element_type=F32)
+    second = lax.dot_general(second, weights[1], dims, preferred_element_type=F32)
+    side = first.shape[0] // pitch
+    parts = []
+    for high in range(side):
+        span = slice(high * pitch, (high + 1) * pitch)
+        parts.append(joined(first[span], second[span]))
+    sums = []
+    for high in range(side):
+        total = parts[high][1]
+        if high > 0:
+            total = total + parts[high - 1][0]
+        if high + 1 < side:
+            total = total + parts[high + 1][2]
+        sums.append(total)
+    return sums
+
+
+def slope_of(pre):
+    sigma = jax.nn.sigmoid(pre)
+    return sigma, sigma * (1.0 + pre * (1.0 - sigma))
+
+
+PLAIN = (((1,), (0,)), ((), ()))
+TURNED = (((1,), (1,)), ((), ()))
 
 
 def routing_of(info, slots):
@@ -147,42 +214,37 @@
                 out_ref[device, slot, high] = jnp.concatenate([part, spare], axis=0).astype(BF16)
 
 
-def local_kernel(my_ref, own_ref, x_ref, w_ref, slope_ref, *refs):
-    *share_refs, rows_ref = refs
+def local_kernel(my_ref, own_ref, x_ref, w_ref, slope_ref, *share_refs):
     step = pl.program_id(0)
     side, kept, lanes = slope_ref.shape
     slots = kept // ROW
     devices = len(share_refs) * share_refs[0].shape[0]
-    pitch = rows_ref.shape[1] // (side + 2)
-    width = w_ref.shape[1]
-    for col in range(3):
-        rows_ref[col, pl.ds(0, pitch), :] = jnp.zeros((pitch, lanes), BF16)
-        rows_ref[col, pl.ds((side + 1) * pitch, pitch), :] = jnp.zeros((pitch, lanes), BF16)
-    for high in range(side):
-        pieces = []
-        for slot in range(slots):
-            pieces += [x_ref[0, slot, high].astype(F32), jnp.zeros((ROW - side, lanes), F32)]
-        if pitch > kept:
-            pieces.append(jnp.zeros((pitch - kept, lanes), F32))
-        for col, rows in enumerate(shifted(jnp.concatenate(pieces, axis=0))):
-            rows_ref[col, pl.ds((high + 1) * pitch, pitch), :] = rows
-    mask = diagonal_mask(lanes, width)
-    pre = conv_taps(
-        rows_ref,
-        lambda tap: block_diagonal(w_ref[tap], mask),
-        pitch,
-        side * pitch,
-        False,
-        (((1,), (0,)), ((), ())),
-    )
-    sigma = jax.nn.sigmoid(pre)
-    slope = sigma * (1.0 + pre * (1.0 - sigma))
-    active = pre * sigma
-    total = active[:pitch]
-    slope_ref[0] = slope[:kept]
-    for high in range(1, side):
-        slope_ref[high] = slope[high * pitch : high * pitch + kept]
-        total = total + active[high * pitch : (high + 1) * pitch]
+    pitch = -(-kept // 16) * 16
+    totals = []
+    for pair in range(lanes // 128):
+        span = pl.ds(pair * 128, 128)
+        firsts, seconds = [], []
+        for high in range(side):
+            pieces = []
+            for slot in range(slots):
+                pieces += [x_ref[0, slot, high, :, span].astype(F32), jnp.zeros((ROW - side, 128), F32)]
+            if pitch > kept:
+                pieces.append(jnp.zeros((pitch - kept, 128), F32))
+            first, second = pair_rows(jnp.concatenate(pieces, axis=0))
+            firsts.append(first)
+            seconds.append(second)
+        weights = pair_weights(w_ref, span, False)
+        pres = pair_conv(
+            jnp.concatenate(firsts, axis=0), jnp.concatenate(seconds, axis=0), weights, pitch, PLAIN
+        )
+        total = jnp.zeros((kept, 128), F32)
+        for high in range(side):
+            pre = pres[high][:kept]
+            sigma, slope = slope_of(pre)
+            slope_ref[high, :, span] = slope
+            total = total + pre * sigma
+        totals.append(total)
+    total = jnp.concatenate(totals, axis=1)
     place = lax.broadcasted_iota(jnp.int32, (ROW, lanes), 0)
     own = own_ref[...]
     means = []
@@ -196,7 +258,9 @@
         for mean, weight in zip(means, own_route(own, slots, jnp.float32(owner))):
             share = share + weight * mean
         place_ref = share_refs[index % len(share_refs)]
-        place_ref[index // len(share_refs), pl.ds(step, 1), :] = share
+        for part in range(lanes // BLOCK):
+            at = pl.ds(step * (lanes // BLOCK) + part, 1)
+            place_ref[index // len(share_refs), at, :] = share[:, part * BLOCK : (part + 1) * BLOCK]
 
 
 def weight_kernel(packed, my_ref, got_ref, w_ref, *refs):
@@ -226,6 +290,43 @@
         spread = jnp.broadcast_to(rows[:, None, :], (devices, ROW, lanes)) / (side * side)
         tile_grads.append(jnp.where(place < side, spread, 0.0).reshape(part, lanes))
     tile_grad = jnp.concatenate(tile_grads, axis=0)
+
+    if lanes % 128 == 0:
+        for pair in range(lanes // 128):
+            span = pl.ds(pair * 128, 128)
+            for high in range(side):
+                rows = []
+                for slot in range(slots):
+                    here = jnp.where(place[:, :, :128] < side, got_ref[:, slot, high, :, span].astype(F32), 0.0)
+                    rows.append(here.reshape(part, 128))
+                first, second = pair_rows(jnp.concatenate(rows, axis=0))
+                rows_ref[0, pl.ds(high * pitch, pitch), :] = first
+                rows_ref[1, pl.ds(high * pitch, pitch), :] = second
+            first, second = rows_ref[0, :, :], rows_ref[1, :, :]
+            pres = pair_conv(first, second, pair_weights(w_ref, span, False), pitch, PLAIN)
+            grads = [slope_of(pre)[1] * tile_grad[:, pair * 128 : (pair + 1) * 128] for pre in pres]
+            none = jnp.zeros((pitch, 128), F32)
+            for high in range(side):
+                after = grads[high + 1] if high + 1 < side else none
+                before = grads[high - 1] if high > 0 else none
+                moved = split(after, grads[high], before)
+                for index in range(2):
+                    grad_ref[index, pl.ds(high * pitch, pitch), :] = moved[index]
+            products = [
+                lax.dot_general(
+                    rows_ref[index, :, :], grad_ref[index, :, :], (((0,), (0,)), ((), ())),
+                    preferred_element_type=F32,
+                )
+                for index in range(2)
+            ]
+            for col, quarter, other in ((0, 0, 1), (1, 1, 0), (2, 2, 3)):
+                taps = joined(
+                    products[0][quarter * width : (quarter + 1) * width],
+                    products[1][other * width : (other + 1) * width],
+                )
+                for row in range(3):
+                    out_ref[3 * row + col, :, span] = taps[row].astype(BF16)
+        return
 
     zero = jnp.zeros((pitch, lanes), BF16)
     for col in range(3):
@@ -264,7 +365,7 @@
         result = product[:width]
         for index in range(1, lanes // width):
             result = jnp.where(group == index, product[index * width : (index + 1) * width], result)
-        out_ref[offset] = result
+        out_ref[offset] = result.astype(BF16)
 
 
 def input_kernel(
@@ -273,29 +374,32 @@
     own_ref,
     slope_ref,
     w_ref,
-    cot_ref,
     info_ref,
     *refs,
 ):
-    *share_refs, out_ref, pooled_ref, rows_ref = refs
+    *refs, out_ref, pooled_ref = refs
     step = pl.program_id(0)
     side, kept, lanes = slope_ref.shape
     slots = kept // ROW
-    devices = cot_ref.shape[0]
-    pitch = rows_ref.shape[1] // (side + 2)
-    width = w_ref.shape[1]
+    devices = info_ref.shape[0]
+    pitch = -(-kept // 16) * 16
+    cot_refs, share_refs = refs[: lanes // BLOCK], refs[lanes // BLOCK :]
     if packed:
-        cot = cot_ref[:, 0, 0].astype(F32)[:, ROW - 1, :]
+        cot = jnp.concatenate(
+            [ref[:, 0, 0].astype(F32)[:, ROW - 1, :] for ref in cot_refs], axis=1
+        )
         info = info_ref[:, 0, 0].astype(F32)[:, ROW - 1, :]
     else:
-        cot = cot_ref[...]
+        cot = jnp.concatenate([ref[...] for ref in cot_refs], axis=1)
         info = info_ref[...]
     _, denominator = routing_of(info, slots)
     scaled = scaled_rows(cot, denominator)
     owners = lax.broadcasted_iota(jnp.int32, (1, 128), 1)
     mine = jnp.sum(jnp.where(owners == my_ref[0], denominator, 0.0), axis=1, keepdims=True)
-    shares = [jnp.sum(ref[:, pl.ds(step, 1), :], axis=0) for ref in share_refs]
-    pooled_ref[0] = sum(shares[1:], shares[0]) / mine
+    for part in range(lanes // BLOCK):
+        at = pl.ds(step * (lanes // BLOCK) + part, 1)
+        shares = [jnp.sum(ref[:, at, :], axis=0) for ref in share_refs]
+        pooled_ref[0, :, part * BLOCK : (part + 1) * BLOCK] = sum(shares[1:], shares[0]) / mine
 
     place = lax.broadcasted_iota(jnp.int32, (ROW, lanes), 0)
     own = own_ref[...]
@@ -309,29 +413,25 @@
         pieces.append(jnp.where(place < side, spread, 0.0))
     tile_grad = jnp.concatenate(pieces, axis=0)
 
-    for col in range(3):
-        rows_ref[col, pl.ds(0, pitch), :] = jnp.zeros((pitch, lanes), BF16)
-        rows_ref[col, pl.ds((side + 1) * pitch, pitch), :] = jnp.zeros((pitch, lanes), BF16)
-    for high in range(side):
-        rows = slope_ref[high] * tile_grad
-        if pitch > kept:
-            rows = jnp.concatenate([rows, jnp.zeros((pitch - kept, lanes), F32)], axis=0)
-        for col, moved in enumerate(shifted(rows)):
-            rows_ref[col, pl.ds((high + 1) * pitch, pitch), :] = moved
-    mask = diagonal_mask(lanes, width)
-    total = conv_taps(
-        rows_ref,
-        lambda tap: block_diagonal(w_ref[tap], mask),
-        pitch,
-        side * pitch,
-        True,
-        (((1,), (1,)), ((), ())),
-    )
-    for high in range(side):
-        for slot in range(slots):
-            start = high * pitch + slot * ROW
-            for wide in range(side):
-                out_ref[slot, high, wide] = total[start + wide : start + wide + 1]
+    for pair in range(lanes // 128):
+        span = pl.ds(pair * 128, 128)
+        firsts, seconds = [], []
+        for high in range(side):
+            rows = slope_ref[high, :, span] * tile_grad[:, pair * 128 : (pair + 1) * 128]
+            if pitch > kept:
+                rows = jnp.concatenate([rows, jnp.zeros((pitch - kept, 128), F32)], axis=0)
+            first, second = pair_rows(rows)
+            firsts.append(first)
+            seconds.append(second)
+        weights = pair_weights(w_ref, span, True)
+        sums = pair_conv(
+            jnp.concatenate(firsts, axis=0), jnp.concatenate(seconds, axis=0), weights, pitch, TURNED
+        )
+        for high in range(side):
+            for slot in range(slots):
+                for wide in range(side):
+                    at = slot * ROW + wide
+                    out_ref[slot, high, wide, :, span] = sums[high][at : at + 1]
 
 
 def params(mebibytes):
@@ -344,6 +444,27 @@
 
 def swap(value, axis, step):
     return lax.ppermute(value, axis, [(i, i ^ step) for i in range(lax.axis_size(axis))])
+
+
+def sum_over_slide(terms, beside):
+    count = lax.axis_size("slide")
+    total = terms.astype(F32) + swap(terms, "slide", 1).astype(F32)
+    step = 2
+    while step < count:
+        sent = total.astype(BF16)
+        if 2 * step < count:
+            other = swap(sent, "slide", step)
+        else:
+            half = sent.shape[1] // 2
+            second = lax.axis_index("slide") % 2 == 1
+            part = swap(jnp.where(second, sent[:, half:], sent[:, :half]), "slide", step)
+            part, beside = lax.optimization_barrier((part, beside))
+            rest = swap(part, "slide", 1)
+            low = jnp.where(second, rest, part)
+            other = jnp.concatenate([low, jnp.where(second, part, rest)], axis=1)
+        total = sent.astype(F32) + other.astype(F32)
+        step *= 2
+    return total, beside
 
 
 def shards(tiles, tile_counts, tile_weights, slide_of, owner_map, cotangent, conv_weight):
@@ -357,7 +478,6 @@
     packed = lanes == BLOCK and devices + 1 <= slots * side
     scalars = (tile_counts, tile_weights, slides, owner_map)
     kept = slots * ROW
-    pitch = -(-kept // 16) * 16
     macs = slots * side * side * taps * width * channels
 
     chunks, info, routes = pl.pallas_call(
@@ -376,7 +496,7 @@
     halves = 2 if packed else 1
     slope, *sent = pl.pallas_call(
         local_kernel,
-        grid=(blocks,),
+        grid=(channels // STEP,),
         out_shape=(
             jax.ShapeDtypeStruct((side, kept, channels), F32),
         )
@@ -384,14 +504,13 @@
         in_specs=[
             smem_whole(),
             pl.BlockSpec((1, 128), lambda j: (0, 0)),
-            pl.BlockSpec((1, slots, side, side, BLOCK), lambda j: (0, 0, 0, 0, j)),
-            pl.BlockSpec((taps, width, BLOCK), lambda j: (0, 0, j)),
+            pl.BlockSpec((1, slots, side, side, STEP), lambda j: (0, 0, 0, 0, j)),
+            pl.BlockSpec((taps, width, STEP), lambda j: (0, 0, j)),
         ],
         out_specs=(
-            pl.BlockSpec((side, kept, BLOCK), lambda j: (0, 0, j)),
+            pl.BlockSpec((side, kept, STEP), lambda j: (0, 0, j)),
         )
         + (pl.BlockSpec((devices // halves, blocks, BLOCK), lambda j: (0, 0, 0)),) * halves,
-        scratch_shapes=[pltpu.VMEM((3, (side + 2) * pitch, BLOCK), BF16)],
         compiler_params=params(56),
         cost_estimate=cost(8 * macs, 4 * 2**20),
     )(mine, routes, tiles, conv_weight)
@@ -407,51 +526,70 @@
     else:
         shares = [lax.all_to_all(toward, "tile", 0, 0, tiled=True)]
 
-    own_weight = lax.dynamic_slice_in_dim(conv_weight, mine[0] * lanes, lanes, 2)
     if packed:
         extra = ()
-        cot_args = (got, got)
+        cot_args = (got,) * (1 + STEP // BLOCK)
         cot_specs = [
-            pl.BlockSpec((devices, 1, 1, ROW, lanes), lambda j: (0, j // side, j % side, 0, 0)),
             pl.BlockSpec(
                 (devices, 1, 1, ROW, lanes), lambda j: (0, devices // side, devices % side, 0, 0)
-            ),
+            )
         ]
+        for part in range(STEP // BLOCK):
+            cot_specs.append(
+                pl.BlockSpec(
+                    (devices, 1, 1, ROW, lanes),
+                    lambda j, part=part: (
+                        0,
+                        (j * (STEP // BLOCK) + part) // side,
+                        (j * (STEP // BLOCK) + part) % side,
+                        0,
+                        0,
+                    ),
+                )
+            )
     else:
         cot_all = lax.all_gather(cotangent[0], "tile", axis=0, tiled=True).astype(F32)
         info_all = lax.all_gather(info, "tile", axis=0, tiled=True)
         extra = (lax.dynamic_slice_in_dim(cot_all, mine[0] * lanes, lanes, 1), info_all)
-        cot_args = (cot_all, info_all)
-        cot_specs = [
-            pl.BlockSpec((devices, BLOCK), lambda j: (0, j)),
-            pl.BlockSpec((devices, 128), lambda j: (0, 0)),
+        cot_args = (info_all,) + (cot_all,) * (STEP // BLOCK)
+        cot_specs = [pl.BlockSpec((devices, 128), lambda j: (0, 0))]
+        for part in range(STEP // BLOCK):
+            cot_specs.append(
+                pl.BlockSpec((devices, BLOCK), lambda j, part=part: (0, j * (STEP // BLOCK) + part))
+            )
+    pitch_all = slots * devices * ROW
+    if lanes % 128 == 0:
+        scratch = [pltpu.VMEM((2, side * pitch_all, BLOCK), BF16)] * 2
+    else:
+        scratch = [
+            pltpu.VMEM((3, (side + 2) * pitch_all, lanes), BF16),
+            pltpu.VMEM(((side + 2) * pitch_all, lanes), BF16),
         ]
-    pitch_all = slots * devices * ROW
+    if packed:
+        weight_spec = pl.BlockSpec((taps, width, lanes), lambda j, my: (0, 0, my[0]))
+        weight = conv_weight
+    else:
+        weight_spec = pl.BlockSpec((taps, width, lanes), lambda j, my: (0, 0, 0))
+        weight = lax.dynamic_slice_in_dim(conv_weight, mine[0] * lanes, lanes, 2)
+    whole = lambda value: pl.BlockSpec(value.shape, lambda j, my: (0,) * value.ndim)
     terms = pl.pallas_call(
         functools.partial(weight_kernel, packed),
-        out_shape=jax.ShapeDtypeStruct((taps, width, lanes), F32),
-        in_specs=[smem_whole()] + [vmem_whole()] * (2 + len(extra)),
-        out_specs=vmem_whole(),
-        scratch_shapes=[
-            pltpu.VMEM((3, (side + 2) * pitch_all, lanes), BF16),
-            pltpu.VMEM(((side + 2) * pitch_all, lanes), BF16),
-        ],
-        compiler_params=params(32),
+        out_shape=jax.ShapeDtypeStruct((taps, width, lanes), BF16),
+        grid_spec=pltpu.PrefetchScalarGridSpec(
+            num_scalar_prefetch=1,
+            grid=(1,),
+            in_specs=[whole(got), weight_spec] + [whole(value) for value in extra],
+            out_specs=pl.BlockSpec((taps, width, lanes), lambda j, my: (0, 0, 0)),
+            scratch_shapes=scratch,
+        ),
+        compiler_params=params(48),
         cost_estimate=cost(16 * macs, 4 * 2**20),
-    )(mine, got, own_weight, *extra)
+    )(mine, got, weight, *extra)
 
     terms, shares = lax.optimization_barrier((terms, shares))
-    total = terms + swap(terms, "slide", 1)
-    step = 2
-    while step < lax.axis_size("slide"):
-        sent = total.astype(BF16)
-        total = sent.astype(F32) + swap(sent, "slide", step).astype(F32)
-        step *= 2
-    weight_grads = total / LOSS_SCALE
-
     grads, pooled = pl.pallas_call(
         functools.partial(input_kernel, packed),
-        grid=(blocks,),
+        grid=(channels // STEP,),
         out_shape=(
             jax.ShapeDtypeStruct((slots, side, side, 1, channels), F32),
             jax.ShapeDtypeStruct((1, 1, channels), F32),
@@ -459,19 +597,20 @@
         in_specs=[
             smem_whole(),
             pl.BlockSpec((1, 128), lambda j: (0, 0)),
-            pl.BlockSpec((side, kept, BLOCK), lambda j: (0, 0, j)),
-            pl.BlockSpec((taps, width, BLOCK), lambda j: (0, 0, j)),
+            pl.BlockSpec((side, kept, STEP), lambda j: (0, 0, j)),
+            pl.BlockSpec((taps, width, STEP), lambda j: (0, 0, j)),
         ]
         + cot_specs
         + [pl.BlockSpec((part.shape[0], blocks, BLOCK), lambda j: (0, 0, 0)) for part in shares],
         out_specs=(
-            pl.BlockSpec((slots, side, side, 1, BLOCK), lambda j: (0, 0, 0, 0, j)),
-            pl.BlockSpec((1, 1, BLOCK), lambda j: (0, 0, j)),
+            pl.BlockSpec((slots, side, side, 1, STEP), lambda j: (0, 0, 0, 0, j)),
+            pl.BlockSpec((1, 1, STEP), lambda j: (0, 0, j)),
         ),
-        scratch_shapes=[pltpu.VMEM((3, (side + 2) * pitch, BLOCK), BF16)],
-        compiler_params=params(24),
+        compiler_params=params(56),
         cost_estimate=cost(8 * macs, 4 * 2**20),
     )(mine, routes, slope, conv_weight, *cot_args, *shares)
+    total, (grads, pooled) = sum_over_slide(terms, (grads, pooled))
+    weight_grads = total / LOSS_SCALE
     input_grads = jnp.transpose(grads, (3, 0, 1, 2, 4))
     return (pooled, input_grads, weight_grads)
 

time: 48 us -> 45 us (0.938)
  Pallas kernels: 23.8 us -> 17 us
  waiting for transfers between devices: 5.24 us -> 7.21 us
  starting transfers between devices: 15.4 us -> 16.5 us
  local copies, waits for them, and re-layouts: 0.06 us -> 0.62 us
    pallas_call x2, Pallas kernels: 15.3 us -> 11.5 us  [the longest x1 6.21 us: shards(): pl.pallas_call(functools.partial(input_kernel, packed), grid=(channels //...]
    pallas_call x1, Pallas kernels: 6.39 us -> 3.39 us  [shards(): pl.pallas_call(functools.partial(weight_kernel, packed), out_shape=jax.Sh...]
    ppermute x6 -> x7, waiting for transfers between devices: 4.41 us -> 5.63 us  [swap(): lax.ppermute(value, axis, [(i, i ^ step) for i in range(lax.axis_size(axi...]
    ppermute x6 -> x7, starting transfers between devices: 8.12 us -> 9.27 us  [swap(): lax.ppermute(value, axis, [(i, i ^ step) for i in range(lax.axis_size(axi...]
    all_to_all x1, waiting for transfers between devices: 0.82 us -> 1.58 us  [shards(): got = lax.all_to_all(chunks, 'tile', 0, 0, tiled=True)]
    slice x1, local copies, waits for them, and re-layouts: 0.01 us -> 0.6 us  [shards(): toward[i:i + 1]]
  transfers between devices with their start and end apart: 7 -> 8, of which waited for: 3 -> 4; matrix products, arithmetic and copies ran while one was open for 2% -> 3% of each run, Pallas kernels for 46% -> 33%
where the time goes in v2:
time: 45 us; the launch traced here: 44.6 us
  Pallas kernels  17 us (38%)
  starting transfers between devices  16.5 us (37%)
  waiting for transfers between devices  7.21 us (16%)
  other arithmetic  1.78 us (4%)
  between operations  1.39 us (3%)
  local copies, waits for them, and re-layouts  0.62 us (1%)
    ppermute x7, starting transfers between devices, swap(): lax.ppermute(value, axis, [(i, i ^ step) for i in range(lax.axis_size(axi...  9.27 us
    all_to_all x1, starting transfers between devices, shards(): got = lax.all_to_all(chunks, 'tile', 0, 0, tiled=True)  7.25 us
    pallas_call x1, Pallas kernels, shards(): pl.pallas_call(functools.partial(input_kernel, packed), grid=(channels //...  6.21 us
    ppermute x7, waiting for transfers between devices, swap(): lax.ppermute(value, axis, [(i, i ^ step) for i in range(lax.axis_size(axi...  5.63 us
    pallas_call x1, Pallas kernels, shards(): pl.pallas_call(local_kernel, grid=(channels // STEP,), out_shape=(jax.Sha...  5.33 us
    pallas_call x1, Pallas kernels, shards(): pl.pallas_call(functools.partial(weight_kernel, packed), out_shape=jax.Sh...  3.39 us
    pallas_call x1, Pallas kernels, shards(): pl.pallas_call(functools.partial(pack_kernel, packed), out_shape=(jax.Sha...  2.09 us
    all_to_all x1, waiting for transfers between devices, shards(): got = lax.all_to_all(chunks, 'tile', 0, 0, tiled=True)  1.58 us
  transfers between devices with their start and end apart: 8, of which 4 were waited for; matrix products, arithmetic and copies ran while one was open for 3% of the time, Pallas kernels for 33%

profile of v2, /device:TPU:0, one launch (start us, length us, event | category | flops | bytes accessed | tf_op | source)
XLA Modules:
  0.0 44.6 jit_solution(4392627283351805312)
XLA Ops:
  1.3 2.1 %shard_map.94 = (bf16[8,3,7,8,256]{4,3,2,1,0:T(8,128)(2,1)}, f32[1,256]{1,0:T(1,128)}, f32[1,128]{1,0:T(1,128)}) custom-call(s32[1,1]{1,0:T(1,128)S(6)} %copy.10.counts_ref, f32[1,3]{1,0:T(1,128)} %weights_ref.1, s32[1,3]{1,0:T(1,128)} %bitcast.3, s32[1,8]{1,0:T(1,128)} %owner_ref.1, bf16[1,3,7,7,2048]{4,3,2,1,0:T(8,128)(2,1)} %x_ref.3, ...), custom_call_target="tpu_custom_call" | custom-call | tf_op jit(solution)/shard_map/pallas_call | solution.py:483
  3.4 7.3 %all-to-all-start = ((bf16[8,3,7,8,256]{4,3,2,1,0:T(8,128)(2,1)}), bf16[8,3,7,8,256]{4,3,2,1,0:T(8,128)(2,1)S(1)}, u32[]{:S(2)}, u32[]{:S(2)}) async-start(bf16[8,3,7,8,256]{4,3,2,1,0:T(8,128)(2,1)} %get-tuple-element.20), calls=%async_computation | async-start | bytes 1376256 | tf_op jit(solution)/shard_map/all_to_all | solution.py:494
  10.6 5.3 %shard_map.95 = (f32[7,24,2048]{2,1,0:T(8,128)}, f32[4,8,256]{2,1,0:T(8,128)}, f32[4,8,256]{2,1,0:T(8,128)}) custom-call(s32[1]{0:T(128)} %bitcast.my_ref, f32[1,128]{1,0:T(1,128)} %get-tuple-element.21.own_ref, bf16[1,3,7,7,2048]{4,3,2,1,0:T(8,128)(2,1)} %x_ref.3, bf16[9,64,2048]{2,1,0:T(8,128)(2,1)} %w_ref.5), custom_call_target="tpu_custom_call" | custom-call | flops 1387266048 | bytes 4194304 | tf_op jit(solution)/shard_map/pallas_call | solution.py:497
  16.0 2.0 %collective-permute-start = (f32[4,8,256]{2,1,0:T(8,128)}, f32[4,8,256]{2,1,0:T(8,128)S(1)}, u32[]{:S(2)}, u32[]{:S(2)}) collective-permute-start(f32[4,8,256]{2,1,0:T(8,128)} %get-tuple-element.24), channel_id=1, source_target_pairs={{0,4},{4,0},{8,12},{12,8},{16,20},{20,16},{24,28},{28,24},{1,5},{5... | collective-permute-start | bytes 98312 | tf_op jit(solution)/shard_map/ppermute | solution.py:446
  18.0 2.7 %collective-permute-done = f32[4,8,256]{2,1,0:T(8,128)S(1)} collective-permute-done((f32[4,8,256]{2,1,0:T(8,128)}, f32[4,8,256]{2,1,0:T(8,128)S(1)}, u32[]{:S(2)}, u32[]{:S(2)}) %collective-permute-start) | collective-permute-done | bytes 32800 | tf_op jit(solution)/shard_map/ppermute | solution.py:446
  20.7 0.8 %add.14 = f32[4,8,256]{2,1,0:T(8,128)S(1)} add(f32[4,8,256]{2,1,0:T(8,128)} %get-tuple-element.23, f32[4,8,256]{2,1,0:T(8,128)S(1)} %collective-permute-done) | non-fusion elementwise | flops 8192 | bytes 98304 | tf_op jit(solution)/shard_map/add | solution.py:518
  21.4 0.6 %fusion = (f32[1,8,256]{2,1,0:T(8,128)S(1)}, f32[1,8,256]{2,1,0:T(8,128)S(1)}, f32[1,8,256]{2,1,0:T(8,128)S(1)}, f32[1,8,256]{2,1,0:T(8,128)}) fusion(f32[4,8,256]{2,1,0:T(8,128)S(1)} %add.14), kind=kLoop, calls=%fused_computation.5 | loop fusion | bytes 65536 | tf_op jit(solution)/shard_map/slice | solution.py:525
  22.0 5.0 %collective-permute-start.3 = (f32[1,8,256]{2,1,0:T(8,128)S(1)}, f32[1,8,256]{2,1,0:T(8,128)S(1)}, u32[]{:S(2)}, u32[]{:S(2)}) collective-permute-start(f32[1,8,256]{2,1,0:T(8,128)S(1)} %get-tuple-element.39), channel_id=1, source_target_pairs={{0,24},{4,28},{8,16},{12,20},{16,8},{20,12},{24,0},{28,4},{1,25},{... | collective-permute-start | bytes 24584 | tf_op jit(solution)/shard_map/ppermute | solution.py:446
  27.0 0.0 collective-permute-start.2
  27.0 0.6 %collective-permute-start.1 = (f32[1,8,256]{2,1,0:T(8,128)S(1)}, f32[1,8,256]{2,1,0:T(8,128)S(1)}, u32[]{:S(2)}, u32[]{:S(2)}) collective-permute-start(f32[1,8,256]{2,1,0:T(8,128)S(1)} %get-tuple-element.41), channel_id=1, source_target_pairs={{0,8},{4,12},{8,0},{12,4},{16,24},{20,28},{24,16},{28,20},{1,9},{5... | collective-permute-start | bytes 24584 | tf_op jit(solution)/shard_map/ppermute | solution.py:446
  27.6 1.6 %all-to-all-done.got_ref.info_ref.refs_0_.refs_1_ = bf16[8,3,7,8,256]{4,3,2,1,0:T(8,128)(2,1)S(1)} async-done(((bf16[8,3,7,8,256]{4,3,2,1,0:T(8,128)(2,1)}), bf16[8,3,7,8,256]{4,3,2,1,0:T(8,128)(2,1)S(1)}, u32[]{:S(2)}, u32[]{:S(2)}) %all-to-all-start) | async-done | bytes 688160 | tf_op jit(solution)/shard_map/all_to_all | solution.py:494
  29.1 3.4 %shard_map.96 = bf16[9,64,256]{2,1,0:T(8,128)(2,1)S(1)} custom-call(s32[1]{0:T(128)} %bitcast.my_ref, bf16[8,3,7,8,256]{4,3,2,1,0:T(8,128)(2,1)S(1)} %all-to-all-done.got_ref.info_ref.refs_0_.refs_1_, bf16[9,64,2048]{2,1,0:T(8,128)(2,1)S(1)} %copy-done.1), custom_call_target="tpu_custom_call" | custom-call | flops 2774532096 | bytes 4194304 | tf_op jit(solution)/shard_map/pallas_call | solution.py:575
  32.5 0.0 collective-permute-done.3.refs_5_
  32.6 0.0 collective-permute-done.2.refs_4_
  32.6 0.0 collective-permute-done.1.refs_3_
  32.6 0.1 collective-permute-start.4
  32.7 1.6 %collective-permute-done.4 = bf16[9,64,256]{2,1,0:T(8,128)(2,1)S(1)} collective-permute-done((bf16[9,64,256]{2,1,0:T(8,128)(2,1)S(1)}, bf16[9,64,256]{2,1,0:T(8,128)(2,1)S(1)}, u32[]{:S(2)}, u32[]{:S(2)}) %collective-permute-start.4) | collective-permute-done | bytes 294944 | tf_op jit(solution)/shard_map/ppermute | solution.py:446
  34.3 0.1 add_convert_fusion
  34.4 1.6 %collective-permute-start.5 = (bf16[9,32,256]{2,1,0:T(8,128)(2,1)S(1)}, bf16[9,32,256]{2,1,0:T(8,128)(2,1)S(1)}, u32[]{:S(2)}, u32[]{:S(2)}) collective-permute-start(bf16[9,32,256]{2,1,0:T(8,128)(2,1)S(1)} %slice_select_fusion), channel_id=1, source_target_pairs={{0,2},{1,3},{2,0},{3,1},{4,6},{5,7},{6,4},{7,5},{8,10},{9,11},{10,... | collective-permute-start | bytes 442376 | tf_op jit(solution)/shard_map/ppermute | solution.py:446
  36.0 6.2 %shard_map.97 = (f32[3,7,7,1,2048]{4,3,2,1,0:T(1,128)}, f32[1,1,2048]{2,1,0:T(1,128)}) custom-call(s32[1]{0:T(128)} %bitcast.my_ref, f32[1,128]{1,0:T(1,128)} %get-tuple-element.21.own_ref, f32[7,24,2048]{2,1,0:T(8,128)} %get-tuple-element.27.slope_ref, bf16[9,64,2048]{2,1,0:T(8,128)(2,1)} %w_ref.5, bf16[8,3,7,8,256]{4,3,2,1,0:T(8,128)(2,1)} %copy-done, ...), custom_call_target="tpu_custom_call" | custom-call | flops 1387266048 | bytes 4194304 | tf_op jit(solution)/shard_map/pallas_call | solution.py:590
  42.2 0.0 collective-permute-done.5
  42.2 0.1 collective-permute-start.6
  42.3 1.4 %collective-permute-done.6 = bf16[9,32,256]{2,1,0:T(8,128)(2,1)S(1)} collective-permute-done((bf16[9,32,256]{2,1,0:T(8,128)(2,1)S(1)}, bf16[9,32,256]{2,1,0:T(8,128)(2,1)S(1)}, u32[]{:S(2)}, u32[]{:S(2)}) %collective-permute-start.6) | collective-permute-done | bytes 147488 | tf_op jit(solution)/shard_map/ppermute | solution.py:446
  43.6 0.9 %add_multiply_fusion = f32[9,64,256]{2,1,0:T(8,128)} fusion(bf16[9,64,256]{2,1,0:T(8,128)(2,1)S(1)} %add_convert_fusion, bf16[9,32,256]{2,1,0:T(8,128)(2,1)S(1)} %get-tuple-element.38, bf16[9,32,256]{2,1,0:T(8,128)(2,1)S(1)} %get-tuple-element.37), kind=kLoop, calls=%fused_computation | loop fusion | flops 1032192 | bytes 1179648 | tf_op jit(solution)/shard_map/div | solution.py:613
  (12 shorter events, 0.1 us)
Async XLA Ops:
  3.4 25.8 %all-to-all-start = ((bf16[8,3,7,8,256]{4,3,2,1,0:T(8,128)(2,1)}), bf16[8,3,7,8,256]{4,3,2,1,0:T(8,128)(2,1)S(1)}, u32[]{:S(2)}, u32[]{:S(2)}) async-start(bf16[8,3,7,8,256]{4,3,2,1,0:T(8,128)(2,1)} %get-tuple-element.20), calls=%async_computation | async-start | bytes 1376256 | tf_op jit(solution)/shard_map/all_to_all | solution.py:494
  10.6 18.5 %copy-start.1 = (bf16[9,64,2048]{2,1,0:T(8,128)(2,1)S(1)}, bf16[9,64,2048]{2,1,0:T(8,128)(2,1)}, u32[]{:S(2)}) copy-start(bf16[9,64,2048]{2,1,0:T(8,128)(2,1)} %w_ref.5) | copy-start | bytes 7077892
  16.0 4.7 %collective-permute-start = (f32[4,8,256]{2,1,0:T(8,128)}, f32[4,8,256]{2,1,0:T(8,128)S(1)}, u32[]{:S(2)}, u32[]{:S(2)}) collective-permute-start(f32[4,8,256]{2,1,0:T(8,128)} %get-tuple-element.24), channel_id=1, source_target_pairs={{0,4},{4,0},{8,12},{12,8},{16,20},{20,16},{24,28},{28,24},{1,5},{5... | collective-permute-start | bytes 98312 | tf_op jit(solution)/shard_map/ppermute | solution.py:446
  22.0 10.5 %collective-permute-start.3 = (f32[1,8,256]{2,1,0:T(8,128)S(1)}, f32[1,8,256]{2,1,0:T(8,128)S(1)}, u32[]{:S(2)}, u32[]{:S(2)}) collective-permute-start(f32[1,8,256]{2,1,0:T(8,128)S(1)} %get-tuple-element.39), channel_id=1, source_target_pairs={{0,24},{4,28},{8,16},{12,20},{16,8},{20,12},{24,0},{28,4},{1,25},{... | collective-permute-start | bytes 24584 | tf_op jit(solution)/shard_map/ppermute | solution.py:446
  27.0 5.6 %collective-permute-start.2 = (f32[1,8,256]{2,1,0:T(8,128)S(1)}, f32[1,8,256]{2,1,0:T(8,128)S(1)}, u32[]{:S(2)}, u32[]{:S(2)}) collective-permute-start(f32[1,8,256]{2,1,0:T(8,128)S(1)} %get-tuple-element.40), channel_id=1, source_target_pairs={{0,16},{4,20},{8,24},{12,28},{16,0},{20,4},{24,8},{28,12},{1,17},{... | collective-permute-start | bytes 24584 | tf_op jit(solution)/shard_map/ppermute | solution.py:446
  27.0 5.6 %collective-permute-start.1 = (f32[1,8,256]{2,1,0:T(8,128)S(1)}, f32[1,8,256]{2,1,0:T(8,128)S(1)}, u32[]{:S(2)}, u32[]{:S(2)}) collective-permute-start(f32[1,8,256]{2,1,0:T(8,128)S(1)} %get-tuple-element.41), channel_id=1, source_target_pairs={{0,8},{4,12},{8,0},{12,4},{16,24},{20,28},{24,16},{28,20},{1,9},{5... | collective-permute-start | bytes 24584 | tf_op jit(solution)/shard_map/ppermute | solution.py:446
  29.1 3.4 %copy-start = (bf16[8,3,7,8,256]{4,3,2,1,0:T(8,128)(2,1)}, bf16[8,3,7,8,256]{4,3,2,1,0:T(8,128)(2,1)S(1)}, u32[]{:S(2)}) copy-start(bf16[8,3,7,8,256]{4,3,2,1,0:T(8,128)(2,1)S(1)} %all-to-all-done.got_ref.info_ref.refs_0_.refs_1_) | copy-start | bytes 2064388
  32.6 3.4 %copy-start.2 = (f32[1,8,256]{2,1,0:T(8,128)}, f32[1,8,256]{2,1,0:T(8,128)S(1)}, u32[]{:S(2)}) copy-start(f32[1,8,256]{2,1,0:T(8,128)S(1)} %collective-permute-done.3.refs_5_) | copy-start | bytes 24580
  32.6 3.4 %copy-start.3 = (f32[1,8,256]{2,1,0:T(8,128)}, f32[1,8,256]{2,1,0:T(8,128)S(1)}, u32[]{:S(2)}) copy-start(f32[1,8,256]{2,1,0:T(8,128)S(1)} %collective-permute-done.2.refs_4_) | copy-start | bytes 24580
  32.6 3.4 %copy-start.4 = (f32[1,8,256]{2,1,0:T(8,128)}, f32[1,8,256]{2,1,0:T(8,128)S(1)}, u32[]{:S(2)}) copy-start(f32[1,8,256]{2,1,0:T(8,128)S(1)} %collective-permute-done.1.refs_3_) | copy-start | bytes 24580
  32.6 1.6 %collective-permute-start.4 = (bf16[9,64,256]{2,1,0:T(8,128)(2,1)S(1)}, bf16[9,64,256]{2,1,0:T(8,128)(2,1)S(1)}, u32[]{:S(2)}, u32[]{:S(2)}) collective-permute-start(bf16[9,64,256]{2,1,0:T(8,128)(2,1)S(1)} %shard_map.96), channel_id=1, source_target_pairs={{0,1},{1,0},{2,3},{3,2},{4,5},{5,4},{6,7},{7,6},{8,9},{9,8},{10,11... | collective-permute-start | bytes 884744 | tf_op jit(solution)/shard_map/ppermute | solution.py:446
  34.4 7.8 %collective-permute-start.5 = (bf16[9,32,256]{2,1,0:T(8,128)(2,1)S(1)}, bf16[9,32,256]{2,1,0:T(8,128)(2,1)S(1)}, u32[]{:S(2)}, u32[]{:S(2)}) collective-permute-start(bf16[9,32,256]{2,1,0:T(8,128)(2,1)S(1)} %slice_select_fusion), channel_id=1, source_target_pairs={{0,2},{1,3},{2,0},{3,1},{4,6},{5,7},{6,4},{7,5},{8,10},{9,11},{10,... | collective-permute-start | bytes 442376 | tf_op jit(solution)/shard_map/ppermute | solution.py:446
  42.2 1.4 %collective-permute-start.6 = (bf16[9,32,256]{2,1,0:T(8,128)(2,1)S(1)}, bf16[9,32,256]{2,1,0:T(8,128)(2,1)S(1)}, u32[]{:S(2)}, u32[]{:S(2)}) collective-permute-start(bf16[9,32,256]{2,1,0:T(8,128)(2,1)S(1)} %collective-permute-done.5), channel_id=1, source_target_pairs={{0,1},{1,0},{2,3},{3,2},{4,5},{5,4},{6,7},{7,6},{8,9},{9,8},{10,11... | collective-permute-start | bytes 442376 | tf_op jit(solution)/shard_map/ppermute | solution.py:446

commit v3 on v2

--- a/solution.py
+++ b/solution.py
@@ -9,7 +9,7 @@
 
 LOSS_SCALE = 512.0
 BLOCK = 256
-STEP = 512
+STEP = 1024
 ROW = 8
 F32 = jnp.float32
 BF16 = jnp.bfloat16
@@ -150,12 +150,13 @@
     return routes, jnp.maximum(total, 1.0)
 
 
-def scaled_rows(cot, denominator):
-    rows = []
-    for owner in range(cot.shape[0]):
-        value = LOSS_SCALE * cot[owner : owner + 1] / denominator[:, owner : owner + 1]
-        rows.append(value.astype(BF16).astype(F32))
-    return rows
+def scaled_rows(cot, denominator, base=0):
+    owners = cot.shape[0]
+    same = (lax.broadcasted_iota(jnp.int32, (owners, 128), 0) ^ base) == lax.broadcasted_iota(
+        jnp.int32, (owners, 128), 1
+    )
+    column = jnp.sum(jnp.where(same, denominator, 0.0), axis=1, keepdims=True)
+    return (LOSS_SCALE * cot / column).astype(BF16).astype(F32)
 
 
 def info_row(coefs, targets, lanes):
@@ -191,55 +192,51 @@
 
 
 def pack_kernel(
-    packed, counts_ref, weights_ref, slide_ref, owner_ref, x_ref, cot_ref, out_ref, info_ref, own_ref
+    counts_ref,
+    weights_ref,
+    slide_ref,
+    owner_ref,
+    x_ref,
+    cot_ref,
+    out_ref,
+    own_ref,
+    flat_ref,
 ):
-    devices, slots, side, _, lanes = out_ref.shape
+    devices, groups, _, lanes = out_ref.shape
+    _, slots, side, _, channels = x_ref.shape
+    rows = slots * side * side
+    for index in range(slots * side):
+        values = x_ref[0, index // side, index % side].astype(F32)
+        flat_ref[pl.ds(index * side, side), :] = values
+    flat_ref[pl.ds(rows, 1), :] = cot_ref[0].astype(F32)
     coefs, targets = own_scalars(counts_ref, weights_ref, slide_ref, owner_ref, slots)
-    info = info_row(coefs, targets, info_ref.shape[1])
-    info_ref[...] = info
     own_ref[...] = own_row(coefs, targets)
-    cot = cot_ref[0].astype(F32)
-    for slot in range(slots):
-        for high in range(side):
-            index = slot * side + high
-            rows = x_ref[0, slot, high].astype(F32)
-            if packed and index < devices:
-                spare = cot[:, index * lanes : (index + 1) * lanes]
-            elif packed and index == devices:
-                spare = info[:, :lanes]
-            else:
-                spare = jnp.zeros((1, lanes), F32)
-            for device in range(devices):
-                part = rows[:, device * lanes : (device + 1) * lanes]
-                out_ref[device, slot, high] = jnp.concatenate([part, spare], axis=0).astype(BF16)
-
-
-def local_kernel(my_ref, own_ref, x_ref, w_ref, slope_ref, *share_refs):
+    info = info_row(coefs, targets, lanes)
+    flat_ref[pl.ds(rows + 1, 1), :] = jnp.concatenate([info] * devices, axis=1)
+    spare = groups * ROW - rows - 2
+    flat_ref[pl.ds(rows + 2, spare), :] = jnp.zeros((spare, channels), F32)
+    for device in range(devices):
+        part = flat_ref[:, pl.ds(device * lanes, lanes)].astype(BF16)
+        out_ref[device] = part.reshape(groups, ROW, lanes)
+
+
+def local_kernel(my_ref, own_ref, cot_ref, x_ref, w_ref, slope_ref, *share_refs):
     step = pl.program_id(0)
     side, kept, lanes = slope_ref.shape
     slots = kept // ROW
-    devices = len(share_refs) * share_refs[0].shape[0]
-    pitch = -(-kept // 16) * 16
+    devices = len(share_refs) * (share_refs[0].shape[0] - 1)
     totals = []
     for pair in range(lanes // 128):
         span = pl.ds(pair * 128, 128)
-        firsts, seconds = [], []
+        pieces = []
         for high in range(side):
-            pieces = []
             for slot in range(slots):
                 pieces += [x_ref[0, slot, high, :, span].astype(F32), jnp.zeros((ROW - side, 128), F32)]
-            if pitch > kept:
-                pieces.append(jnp.zeros((pitch - kept, 128), F32))
-            first, second = pair_rows(jnp.concatenate(pieces, axis=0))
-            firsts.append(first)
-            seconds.append(second)
-        weights = pair_weights(w_ref, span, False)
-        pres = pair_conv(
-            jnp.concatenate(firsts, axis=0), jnp.concatenate(seconds, axis=0), weights, pitch, PLAIN
-        )
+        first, second = pair_rows(jnp.concatenate(pieces, axis=0))
+        pres = pair_conv(first, second, pair_weights(w_ref, span, False), kept, PLAIN)
         total = jnp.zeros((kept, 128), F32)
         for high in range(side):
-            pre = pres[high][:kept]
+            pre = pres[high]
             sigma, slope = slope_of(pre)
             slope_ref[high, :, span] = slope
             total = total + pre * sigma
@@ -261,24 +258,23 @@
         for part in range(lanes // BLOCK):
             at = pl.ds(step * (lanes // BLOCK) + part, 1)
             place_ref[index // len(share_refs), at, :] = share[:, part * BLOCK : (part + 1) * BLOCK]
-
-
-def weight_kernel(packed, my_ref, got_ref, w_ref, *refs):
-    if packed:
-        out_ref, rows_ref, grad_ref = refs
-    else:
-        cot_ref, info_ref, out_ref, rows_ref, grad_ref = refs
-    devices, slots, side, _, lanes = got_ref.shape
+    for part in range(lanes // BLOCK):
+        at = pl.ds(step * (lanes // BLOCK) + part, 1)
+        for place_ref in share_refs:
+            span = slice(part * BLOCK, (part + 1) * BLOCK)
+            place_ref[devices // len(share_refs), at, :] = cot_ref[0, :, span].astype(F32)
+
+
+def weight_kernel(packed, side, my_ref, got_ref, w_ref, out_ref, rows_ref, grad_ref, flat_ref):
+    del my_ref
+    devices, groups, _, lanes = got_ref.shape
+    slots = groups * ROW // (side * side)
     width = w_ref.shape[1]
     part = devices * ROW
     pitch = slots * part
-    if packed:
-        mine = my_ref[0]
-        cot = got_ref[:, mine // side, mine % side].astype(F32)[:, ROW - 1, :]
-        info = got_ref[:, devices // side, devices % side].astype(F32)[:, ROW - 1, :]
-    else:
-        cot = cot_ref[...]
-        info = info_ref[...]
+    flat_ref[...] = got_ref[...].astype(F32).reshape(devices, groups * ROW, lanes)
+    cot = flat_ref[:, slots * side * side, :]
+    info = flat_ref[:, slots * side * side + 1, :]
     routes, denominator = routing_of(info, slots)
     scaled = scaled_rows(cot, denominator)
     place = lax.broadcasted_iota(jnp.int32, (devices, ROW, lanes), 1)
@@ -286,18 +282,19 @@
     for slot in range(slots):
         rows = jnp.zeros((devices, lanes), F32)
         for owner in range(devices):
-            rows = rows + routes[slot][:, owner : owner + 1] * scaled[owner]
+            rows = rows + routes[slot][:, owner : owner + 1] * scaled[owner : owner + 1]
         spread = jnp.broadcast_to(rows[:, None, :], (devices, ROW, lanes)) / (side * side)
         tile_grads.append(jnp.where(place < side, spread, 0.0).reshape(part, lanes))
     tile_grad = jnp.concatenate(tile_grads, axis=0)
 
-    if lanes % 128 == 0:
+    if packed:
         for pair in range(lanes // 128):
             span = pl.ds(pair * 128, 128)
             for high in range(side):
                 rows = []
                 for slot in range(slots):
-                    here = jnp.where(place[:, :, :128] < side, got_ref[:, slot, high, :, span].astype(F32), 0.0)
+                    here = flat_ref[:, pl.ds((slot * side + high) * side, ROW), span]
+                    here = jnp.where(place[:, :, :128] < side, here, 0.0)
                     rows.append(here.reshape(part, 128))
                 first, second = pair_rows(jnp.concatenate(rows, axis=0))
                 rows_ref[0, pl.ds(high * pitch, pitch), :] = first
@@ -336,7 +333,8 @@
     grad_ref[pl.ds((side + 1) * pitch, pitch), :] = zero
     for high in range(side):
         for slot in range(slots):
-            rows = jnp.where(place < side, got_ref[:, slot, high].astype(F32), 0.0)
+            here = flat_ref[:, pl.ds((slot * side + high) * side, ROW), :]
+            rows = jnp.where(place < side, here, 0.0)
             for col, moved in enumerate(shifted(rows.reshape(part, lanes))):
                 rows_ref[col, pl.ds((high + 1) * pitch + slot * part, part), :] = moved
     mask = diagonal_mask(lanes, width) if lanes > width else None
@@ -382,51 +380,40 @@
     side, kept, lanes = slope_ref.shape
     slots = kept // ROW
     devices = info_ref.shape[0]
-    pitch = -(-kept // 16) * 16
-    cot_refs, share_refs = refs[: lanes // BLOCK], refs[lanes // BLOCK :]
-    if packed:
-        cot = jnp.concatenate(
-            [ref[:, 0, 0].astype(F32)[:, ROW - 1, :] for ref in cot_refs], axis=1
-        )
-        info = info_ref[:, 0, 0].astype(F32)[:, ROW - 1, :]
-    else:
-        cot = jnp.concatenate([ref[...] for ref in cot_refs], axis=1)
-        info = info_ref[...]
+    info = info_ref[:, 0].astype(F32)[:, (slots * side * side + 1) % ROW, :]
     _, denominator = routing_of(info, slots)
-    scaled = scaled_rows(cot, denominator)
     owners = lax.broadcasted_iota(jnp.int32, (1, 128), 1)
     mine = jnp.sum(jnp.where(owners == my_ref[0], denominator, 0.0), axis=1, keepdims=True)
+    base = my_ref[0] if packed else 0
+    cots = []
     for part in range(lanes // BLOCK):
         at = pl.ds(step * (lanes // BLOCK) + part, 1)
-        shares = [jnp.sum(ref[:, at, :], axis=0) for ref in share_refs]
+        if packed:
+            shares = [ref[0, at, :] for ref in refs]
+            rows = [ref[row, at, :] for ref in refs for row in (1, 2)]
+            cots.append(jnp.concatenate(rows, axis=0))
+        else:
+            shares = [jnp.sum(refs[0][:, at, :], axis=0)]
+            cots.append(refs[1][:, at, :].reshape(devices, BLOCK))
         pooled_ref[0, :, part * BLOCK : (part + 1) * BLOCK] = sum(shares[1:], shares[0]) / mine
+    scaled = scaled_rows(jnp.concatenate(cots, axis=1), denominator, base)
 
     place = lax.broadcasted_iota(jnp.int32, (ROW, lanes), 0)
     own = own_ref[...]
     pieces = []
-    sums = [jnp.zeros((1, lanes), F32)] * slots
-    for owner in range(devices):
-        weights = own_route(own, slots, owner)
-        sums = [sums[slot] + weights[slot] * scaled[owner] for slot in range(slots)]
-    for slot in range(slots):
-        spread = jnp.broadcast_to(sums[slot], (ROW, lanes)) / (side * side)
+    owner = (lax.broadcasted_iota(jnp.int32, (devices, 1), 0) ^ base).astype(F32)
+    for weight in own_route(own, slots, owner):
+        row = jnp.sum(weight * scaled, axis=0, keepdims=True)
+        spread = jnp.broadcast_to(row, (ROW, lanes)) / (side * side)
         pieces.append(jnp.where(place < side, spread, 0.0))
     tile_grad = jnp.concatenate(pieces, axis=0)
 
     for pair in range(lanes // 128):
         span = pl.ds(pair * 128, 128)
-        firsts, seconds = [], []
-        for high in range(side):
-            rows = slope_ref[high, :, span] * tile_grad[:, pair * 128 : (pair + 1) * 128]
-            if pitch > kept:
-                rows = jnp.concatenate([rows, jnp.zeros((pitch - kept, 128), F32)], axis=0)
-            first, second = pair_rows(rows)
-            firsts.append(first)
-            seconds.append(second)
-        weights = pair_weights(w_ref, span, True)
-        sums = pair_conv(
-            jnp.concatenate(firsts, axis=0), jnp.concatenate(seconds, axis=0), weights, pitch, TURNED
-        )
+        here = tile_grad[:, pair * 128 : (pair + 1) * 128]
+        rows = jnp.concatenate([slope_ref[high, :, span] * here for high in range(side)], axis=0)
+        first, second = pair_rows(rows)
+        sums = pair_conv(first, second, pair_weights(w_ref, span, True), kept, TURNED)
         for high in range(side):
             for slot in range(slots):
                 for wide in range(side):
@@ -448,23 +435,22 @@
 
 def sum_over_slide(terms, beside):
     count = lax.axis_size("slide")
-    total = terms.astype(F32) + swap(terms, "slide", 1).astype(F32)
+    second = lax.axis_index("slide") % 2 == 1
+    low, high = jnp.split(terms, 2, axis=1)
+    sent = swap(jnp.where(second, low, high), "slide", 1)
+    total = jnp.where(second, high, low).astype(F32) + sent.astype(F32)
     step = 2
     while step < count:
         sent = total.astype(BF16)
-        if 2 * step < count:
-            other = swap(sent, "slide", step)
-        else:
-            half = sent.shape[1] // 2
-            second = lax.axis_index("slide") % 2 == 1
-            part = swap(jnp.where(second, sent[:, half:], sent[:, :half]), "slide", step)
-            part, beside = lax.optimization_barrier((part, beside))
-            rest = swap(part, "slide", 1)
-            low = jnp.where(second, rest, part)
-            other = jnp.concatenate([low, jnp.where(second, part, rest)], axis=1)
+        other = swap(sent, "slide", step)
+        if 2 * step >= count:
+            other, beside = lax.optimization_barrier((other, beside))
         total = sent.astype(F32) + other.astype(F32)
         step *= 2
-    return total, beside
+    half = total.astype(BF16)
+    rest = swap(half, "slide", 1)
+    whole = [jnp.where(second, rest, half), jnp.where(second, half, rest)]
+    return jnp.concatenate(whole, axis=1).astype(F32), beside
 
 
 def shards(tiles, tile_counts, tile_weights, slide_of, owner_map, cotangent, conv_weight):
@@ -475,22 +461,22 @@
     blocks = channels // BLOCK
     mine = lax.axis_index("tile").astype(jnp.int32).reshape(1)
     slides = slide_of[:, :, 0]
-    packed = lanes == BLOCK and devices + 1 <= slots * side
-    scalars = (tile_counts, tile_weights, slides, owner_map)
+    packed = lanes == BLOCK
+    groups = -(-(slots * side * side + 2) // ROW)
     kept = slots * ROW
     macs = slots * side * side * taps * width * channels
 
-    chunks, info, routes = pl.pallas_call(
-        functools.partial(pack_kernel, packed),
+    chunks, routes = pl.pallas_call(
+        pack_kernel,
         out_shape=(
-            jax.ShapeDtypeStruct((devices, slots, side, ROW, lanes), BF16),
-            jax.ShapeDtypeStruct((1, max(lanes, 128)), F32),
+            jax.ShapeDtypeStruct((devices, groups, ROW, lanes), BF16),
             jax.ShapeDtypeStruct((1, 128), F32),
         ),
         in_specs=[smem_whole()] * 4 + [vmem_whole()] * 2,
-        out_specs=(vmem_whole(), vmem_whole(), vmem_whole()),
+        out_specs=(vmem_whole(), vmem_whole()),
+        scratch_shapes=[pltpu.VMEM((groups * ROW, channels), F32)],
         compiler_params=params(56),
-    )(*scalars, tiles, cotangent)
+    )(tile_counts, tile_weights, slides, owner_map, tiles, cotangent)
     got = lax.all_to_all(chunks, "tile", 0, 0, tiled=True)
 
     halves = 2 if packed else 1
@@ -500,91 +486,64 @@
         out_shape=(
             jax.ShapeDtypeStruct((side, kept, channels), F32),
         )
-        + (jax.ShapeDtypeStruct((devices // halves, blocks, BLOCK), F32),) * halves,
+        + (jax.ShapeDtypeStruct((devices // halves + 1, blocks, BLOCK), F32),) * halves,
         in_specs=[
             smem_whole(),
             pl.BlockSpec((1, 128), lambda j: (0, 0)),
+            pl.BlockSpec((1, 1, STEP), lambda j: (0, 0, j)),
             pl.BlockSpec((1, slots, side, side, STEP), lambda j: (0, 0, 0, 0, j)),
             pl.BlockSpec((taps, width, STEP), lambda j: (0, 0, j)),
         ],
         out_specs=(
             pl.BlockSpec((side, kept, STEP), lambda j: (0, 0, j)),
         )
-        + (pl.BlockSpec((devices // halves, blocks, BLOCK), lambda j: (0, 0, 0)),) * halves,
+        + (pl.BlockSpec((devices // halves + 1, blocks, BLOCK), lambda j: (0, 0, 0)),) * halves,
         compiler_params=params(56),
         cost_estimate=cost(8 * macs, 4 * 2**20),
-    )(mine, routes, tiles, conv_weight)
+    )(mine, routes, cotangent, tiles, conv_weight)
     if packed:
-        toward = sent[0] + swap(sent[1], "tile", 1)
+        half = devices // 2
+        other = swap(sent[1], "tile", 1)
+        toward = sent[0][:half] + other[:half]
+        cots = [sent[0][half:], other[half:]]
+        toward = [jnp.concatenate([toward[i : i + 1], *cots]) for i in range(half)]
     else:
         toward = sent[0]
-
     got, slope, _ = lax.optimization_barrier((got, slope, toward))
     if packed:
-        shares = [toward[:1]]
-        shares += [swap(toward[i : i + 1], "tile", 2 * i) for i in range(1, devices // 2)]
+        shares = toward[:1] + [swap(toward[i], "tile", 2 * i) for i in range(1, half)]
     else:
-        shares = [lax.all_to_all(toward, "tile", 0, 0, tiled=True)]
-
+        shares = [lax.all_to_all(toward[:devices], "tile", 0, 0, tiled=True)]
+        shares.append(lax.all_gather(toward[devices:], "tile", axis=0, tiled=True))
+    info_block = (slots * side * side + 1) // ROW
+    pitch_all = slots * devices * ROW
     if packed:
-        extra = ()
-        cot_args = (got,) * (1 + STEP // BLOCK)
-        cot_specs = [
-            pl.BlockSpec(
-                (devices, 1, 1, ROW, lanes), lambda j: (0, devices // side, devices % side, 0, 0)
-            )
-        ]
-        for part in range(STEP // BLOCK):
-            cot_specs.append(
-                pl.BlockSpec(
-                    (devices, 1, 1, ROW, lanes),
-                    lambda j, part=part: (
-                        0,
-                        (j * (STEP // BLOCK) + part) // side,
-                        (j * (STEP // BLOCK) + part) % side,
-                        0,
-                        0,
-                    ),
-                )
-            )
-    else:
-        cot_all = lax.all_gather(cotangent[0], "tile", axis=0, tiled=True).astype(F32)
-        info_all = lax.all_gather(info, "tile", axis=0, tiled=True)
-        extra = (lax.dynamic_slice_in_dim(cot_all, mine[0] * lanes, lanes, 1), info_all)
-        cot_args = (info_all,) + (cot_all,) * (STEP // BLOCK)
-        cot_specs = [pl.BlockSpec((devices, 128), lambda j: (0, 0))]
-        for part in range(STEP // BLOCK):
-            cot_specs.append(
-                pl.BlockSpec((devices, BLOCK), lambda j, part=part: (0, j * (STEP // BLOCK) + part))
-            )
-    pitch_all = slots * devices * ROW
-    if lanes % 128 == 0:
         scratch = [pltpu.VMEM((2, side * pitch_all, BLOCK), BF16)] * 2
     else:
         scratch = [
             pltpu.VMEM((3, (side + 2) * pitch_all, lanes), BF16),
             pltpu.VMEM(((side + 2) * pitch_all, lanes), BF16),
         ]
+    scratch.append(pltpu.VMEM((devices, groups * ROW, lanes), F32))
     if packed:
         weight_spec = pl.BlockSpec((taps, width, lanes), lambda j, my: (0, 0, my[0]))
         weight = conv_weight
     else:
         weight_spec = pl.BlockSpec((taps, width, lanes), lambda j, my: (0, 0, 0))
         weight = lax.dynamic_slice_in_dim(conv_weight, mine[0] * lanes, lanes, 2)
-    whole = lambda value: pl.BlockSpec(value.shape, lambda j, my: (0,) * value.ndim)
     terms = pl.pallas_call(
-        functools.partial(weight_kernel, packed),
+        functools.partial(weight_kernel, packed, side),
         out_shape=jax.ShapeDtypeStruct((taps, width, lanes), BF16),
         grid_spec=pltpu.PrefetchScalarGridSpec(
             num_scalar_prefetch=1,
             grid=(1,),
-            in_specs=[whole(got), weight_spec] + [whole(value) for value in extra],
+            in_specs=[pl.BlockSpec(got.shape, lambda j, my: (0, 0, 0, 0)), weight_spec],
             out_specs=pl.BlockSpec((taps, width, lanes), lambda j, my: (0, 0, 0)),
             scratch_shapes=scratch,
         ),
-        compiler_params=params(48),
+        compiler_params=params(20),
         cost_estimate=cost(16 * macs, 4 * 2**20),
-    )(mine, got, weight, *extra)
+    )(mine, got, weight)
 
     terms, shares = lax.optimization_barrier((terms, shares))
     grads, pooled = pl.pallas_call(
@@ -599,16 +558,23 @@
             pl.BlockSpec((1, 128), lambda j: (0, 0)),
             pl.BlockSpec((side, kept, STEP), lambda j: (0, 0, j)),
             pl.BlockSpec((taps, width, STEP), lambda j: (0, 0, j)),
+            pl.BlockSpec((devices, 1, ROW, lanes), lambda j: (0, info_block, 0, 0)),
         ]
-        + cot_specs
         + [pl.BlockSpec((part.shape[0], blocks, BLOCK), lambda j: (0, 0, 0)) for part in shares],
         out_specs=(
             pl.BlockSpec((slots, side, side, 1, STEP), lambda j: (0, 0, 0, 0, j)),
             pl.BlockSpec((1, 1, STEP), lambda j: (0, 0, j)),
         ),
-        compiler_params=params(56),
+        compiler_params=params(16),
         cost_estimate=cost(8 * macs, 4 * 2**20),
-    )(mine, routes, slope, conv_weight, *cot_args, *shares)
+    )(
+        mine,
+        routes,
+        pltpu.with_memory_space_constraint(slope, pltpu.HBM),
+        conv_weight,
+        got,
+        *shares,
+    )
     total, (grads, pooled) = sum_over_slide(terms, (grads, pooled))
     weight_grads = total / LOSS_SCALE
     input_grads = jnp.transpose(grads, (3, 0, 1, 2, 4))

time: 45 us -> 42.8 us (0.951)
  Pallas kernels: 17 us -> 15.2 us
    pallas_call x1, Pallas kernels: 6.21 us -> 4.72 us  [shards(): pl.pallas_call(functools.partial(input_kernel, packed), grid=(channels //...]
    pallas_call x1, Pallas kernels: 5.33 us -> 4.49 us  [shards(): pl.pallas_call(local_kernel, grid=(channels // STEP,), out_shape=(jax.Sha...]
    ppermute x7, waiting for transfers between devices: 5.63 us -> 4.87 us  [swap(): lax.ppermute(value, axis, [(i, i ^ step) for i in range(lax.axis_size(axi...]
    pallas_call x2, Pallas kernels: 5.48 us -> 5.96 us  [the longest x1 3.81 us: shards(): pl.pallas_call(functools.partial(weight_kernel, packed, side), out_shape=...]
  transfers between devices with their start and end apart: 8 -> 8, of which waited for: 4 -> 4; matrix products, arithmetic and copies ran while one was open for 3% -> 3% of each run, Pallas kernels for 33% -> 31%
where the time goes in v3:
time: 42.8 us; the launch traced here: 42.5 us
  starting transfers between devices  16.6 us (39%)
  Pallas kernels  15.2 us (36%)
  waiting for transfers between devices  6.81 us (16%)
  other arithmetic  1.79 us (4%)
  between operations  1.36 us (3%)
  local copies, waits for them, and re-layouts  0.71 us (2%)
    ppermute x7, starting transfers between devices, swap(): lax.ppermute(value, axis, [(i, i ^ step) for i in range(lax.axis_size(axi...  9.4 us
    all_to_all x1, starting transfers between devices, shards(): got = lax.all_to_all(chunks, 'tile', 0, 0, tiled=True)  7.25 us
    ppermute x7, waiting for transfers between devices, swap(): lax.ppermute(value, axis, [(i, i ^ step) for i in range(lax.axis_size(axi...  4.87 us
    pallas_call x1, Pallas kernels, shards(): pl.pallas_call(functools.partial(input_kernel, packed), grid=(channels //...  4.72 us
    pallas_call x1, Pallas kernels, shards(): pl.pallas_call(local_kernel, grid=(channels // STEP,), out_shape=(jax.Sha...  4.49 us
    pallas_call x1, Pallas kernels, shards(): pl.pallas_call(functools.partial(weight_kernel, packed, side), out_shape=...  3.81 us
    pallas_call x1, Pallas kernels, shards(): pl.pallas_call(pack_kernel, out_shape=(jax.ShapeDtypeStruct((devices, gro...  2.15 us
    all_to_all x1, waiting for transfers between devices, shards(): got = lax.all_to_all(chunks, 'tile', 0, 0, tiled=True)  1.94 us
  transfers between devices with their start and end apart: 8, of which 4 were waited for; matrix products, arithmetic and copies ran while one was open for 3% of the time, Pallas kernels for 31%

profile of v3, /device:TPU:0, one launch (start us, length us, event | category | flops | bytes accessed | tf_op | source)
XLA Modules:
  0.0 42.5 jit_solution(1443005232416141250)
XLA Ops:
  1.3 2.1 %shard_map.94 = (bf16[8,19,8,256]{3,2,1,0:T(8,128)(2,1)}, f32[1,128]{1,0:T(1,128)}) custom-call(s32[1,1]{1,0:T(1,128)S(6)} %copy.10.counts_ref, f32[1,3]{1,0:T(1,128)} %weights_ref.1, s32[1,3]{1,0:T(1,128)} %bitcast.3, s32[1,8]{1,0:T(1,128)} %owner_ref.1, bf16[1,3,7,7,2048]{4,3,2,1,0:T(8,128)(2,1)} %x_ref.3, bf16[1,1,2048]{2,1,0:T(2,128)(2,1)} %cot_ref.3), custom_call_target="tpu_custom_call" | custom-call | tf_op jit(solution)/shard_map/pallas_call | solution.py:469
  3.4 7.3 %all-to-all-start = ((bf16[8,19,8,256]{3,2,1,0:T(8,128)(2,1)}), bf16[8,19,8,256]{3,2,1,0:T(8,128)(2,1)S(1)}, u32[]{:S(2)}, u32[]{:S(2)}) async-start(bf16[8,19,8,256]{3,2,1,0:T(8,128)(2,1)} %get-tuple-element.20), calls=%async_computation | async-start | bytes 1245184 | tf_op jit(solution)/shard_map/all_to_all | solution.py:480
  10.7 4.5 %shard_map.95 = (f32[7,24,2048]{2,1,0:T(8,128)}, f32[5,8,256]{2,1,0:T(8,128)}, f32[5,8,256]{2,1,0:T(8,128)}) custom-call(s32[1]{0:T(128)} %bitcast.my_ref, f32[1,128]{1,0:T(1,128)} %get-tuple-element.21.own_ref, bf16[1,1,2048]{2,1,0:T(2,128)(2,1)} %cot_ref.3, bf16[1,3,7,7,2048]{4,3,2,1,0:T(8,128)(2,1)} %x_ref.3, bf16[9,64,2048]{2,1,0:T(8,128)(2,1)} %w_ref.5), custom_call_target="tpu_custom_call" | custom-call | flops 1387266048 | bytes 4194304 | tf_op jit(solution)/shard_map/pallas_call | solution.py:483
  15.2 2.0 %collective-permute-start = (f32[5,8,256]{2,1,0:T(8,128)}, f32[5,8,256]{2,1,0:T(8,128)S(1)}, u32[]{:S(2)}, u32[]{:S(2)}) collective-permute-start(f32[5,8,256]{2,1,0:T(8,128)} %get-tuple-element.24), channel_id=1, source_target_pairs={{0,4},{4,0},{8,12},{12,8},{16,20},{20,16},{24,28},{28,24},{1,5},{5... | collective-permute-start | bytes 122888 | tf_op jit(solution)/shard_map/ppermute | solution.py:433
  17.2 0.7 %slice.27 = f32[1,8,256]{2,1,0:T(8,128)S(1)} slice(f32[5,8,256]{2,1,0:T(8,128)} %get-tuple-element.23), slice={[4:5], [0:8], [0:256]} | slice | bytes 16384 | tf_op jit(solution)/shard_map/slice | solution.py:508
  17.9 2.1 %collective-permute-done = f32[5,8,256]{2,1,0:T(8,128)S(1)} collective-permute-done((f32[5,8,256]{2,1,0:T(8,128)}, f32[5,8,256]{2,1,0:T(8,128)S(1)}, u32[]{:S(2)}, u32[]{:S(2)}) %collective-permute-start) | collective-permute-done | bytes 40992 | tf_op jit(solution)/shard_map/ppermute | solution.py:433
  20.0 0.8 %slice_add_fusion = f32[4,8,256]{2,1,0:T(8,128)S(1)} fusion(f32[5,8,256]{2,1,0:T(8,128)S(1)} %collective-permute-done, f32[5,8,256]{2,1,0:T(8,128)} %get-tuple-element.23), kind=kLoop, calls=%fused_computation.14 | loop fusion | flops 8192 | bytes 98304 | tf_op jit(solution)/shard_map/add | solution.py:507
  20.8 5.0 %collective-permute-start.3 = (f32[3,8,256]{2,1,0:T(8,128)S(1)}, f32[3,8,256]{2,1,0:T(8,128)S(1)}, u32[]{:S(2)}, u32[]{:S(2)}) collective-permute-start(f32[3,8,256]{2,1,0:T(8,128)S(1)} %get-tuple-element.43), channel_id=1, source_target_pairs={{0,24},{4,28},{8,16},{12,20},{16,8},{20,12},{24,0},{28,4},{1,25},{... | collective-permute-start | bytes 73736 | tf_op jit(solution)/shard_map/ppermute | solution.py:433
  25.8 0.0 collective-permute-start.1
  25.8 0.6 %collective-permute-start.2 = (f32[3,8,256]{2,1,0:T(8,128)S(1)}, f32[3,8,256]{2,1,0:T(8,128)S(1)}, u32[]{:S(2)}, u32[]{:S(2)}) collective-permute-start(f32[3,8,256]{2,1,0:T(8,128)S(1)} %get-tuple-element.45), channel_id=1, source_target_pairs={{0,16},{4,20},{8,24},{12,28},{16,0},{20,4},{24,8},{28,12},{1,17},{... | collective-permute-start | bytes 73736 | tf_op jit(solution)/shard_map/ppermute | solution.py:433
  26.5 1.9 %all-to-all-done.got_ref.info_ref = bf16[8,19,8,256]{3,2,1,0:T(8,128)(2,1)S(1)} async-done(((bf16[8,19,8,256]{3,2,1,0:T(8,128)(2,1)}), bf16[8,19,8,256]{3,2,1,0:T(8,128)(2,1)S(1)}, u32[]{:S(2)}, u32[]{:S(2)}) %all-to-all-start) | async-done | bytes 622624 | tf_op jit(solution)/shard_map/all_to_all | solution.py:480
  28.4 3.8 %shard_map.96 = bf16[9,64,256]{2,1,0:T(8,128)(2,1)S(1)} custom-call(s32[1]{0:T(128)} %bitcast.my_ref, bf16[8,19,8,256]{3,2,1,0:T(8,128)(2,1)S(1)} %all-to-all-done.got_ref.info_ref, bf16[9,64,2048]{2,1,0:T(8,128)(2,1)S(1)} %copy-done), custom_call_target="tpu_custom_call" | custom-call | flops 2774532096 | bytes 4194304 | tf_op jit(solution)/shard_map/pallas_call | solution.py:534
  32.2 0.0 collective-permute-done.3.refs_3_
  32.2 0.0 collective-permute-done.1.refs_1_
  32.2 0.0 collective-permute-done.2.refs_2_
  32.3 0.1 collective-permute-start.4
  32.4 1.4 %collective-permute-done.4 = bf16[9,32,256]{2,1,0:T(8,128)(2,1)S(1)} collective-permute-done((bf16[9,32,256]{2,1,0:T(8,128)(2,1)S(1)}, bf16[9,32,256]{2,1,0:T(8,128)(2,1)S(1)}, u32[]{:S(2)}, u32[]{:S(2)}) %collective-permute-start.4) | collective-permute-done | bytes 147488 | tf_op jit(solution)/shard_map/ppermute | solution.py:433
  33.7 0.1 add_convert_fusion.1
  33.8 1.6 %collective-permute-start.5 = (bf16[9,32,256]{2,1,0:T(8,128)(2,1)S(1)}, bf16[9,32,256]{2,1,0:T(8,128)(2,1)S(1)}, u32[]{:S(2)}, u32[]{:S(2)}) collective-permute-start(bf16[9,32,256]{2,1,0:T(8,128)(2,1)S(1)} %add_convert_fusion.1), channel_id=1, source_target_pairs={{0,2},{1,3},{2,0},{3,1},{4,6},{5,7},{6,4},{7,5},{8,10},{9,11},{10,... | collective-permute-start | bytes 442376 | tf_op jit(solution)/shard_map/ppermute | solution.py:433
  35.4 4.7 %shard_map.97 = (f32[3,7,7,1,2048]{4,3,2,1,0:T(1,128)}, f32[1,1,2048]{2,1,0:T(1,128)}) custom-call(s32[1]{0:T(128)} %bitcast.my_ref, f32[1,128]{1,0:T(1,128)S(1)} %copy-done.1, f32[7,24,2048]{2,1,0:T(8,128)} %get-tuple-element.27.slope_ref, bf16[9,64,2048]{2,1,0:T(8,128)(2,1)S(1)} %copy-done, bf16[8,19,8,256]{3,2,1,0:T(8,128)(2,1)S(1)} %all-to-all-done.got_ref.info_ref, ...), custom_call_target="tpu_custom_call" | custom-call | flops 1387266048 | bytes 4194304 | tf_op jit(solution)/shard_map/pallas_call | solution.py:549
  40.1 0.0 collective-permute-done.5
  40.2 0.1 collective-permute-start.6
  40.2 1.4 %collective-permute-done.6 = bf16[9,32,256]{2,1,0:T(8,128)(2,1)S(1)} collective-permute-done((bf16[9,32,256]{2,1,0:T(8,128)(2,1)S(1)}, bf16[9,32,256]{2,1,0:T(8,128)(2,1)S(1)}, u32[]{:S(2)}, u32[]{:S(2)}) %collective-permute-start.6) | collective-permute-done | bytes 147488 | tf_op jit(solution)/shard_map/ppermute | solution.py:433
  41.6 0.9 %convert_multiply_fusion = f32[9,64,256]{2,1,0:T(8,128)} fusion(bf16[9,32,256]{2,1,0:T(8,128)(2,1)S(1)} %get-tuple-element.38, bf16[9,32,256]{2,1,0:T(8,128)(2,1)S(1)} %get-tuple-element.37), kind=kLoop, calls=%fused_computation | loop fusion | flops 737280 | bytes 884736 | tf_op jit(solution)/shard_map/div | solution.py:579
  (10 shorter events, 0.1 us)
Async XLA Ops:
  3.4 25.0 %all-to-all-start = ((bf16[8,19,8,256]{3,2,1,0:T(8,128)(2,1)}), bf16[8,19,8,256]{3,2,1,0:T(8,128)(2,1)S(1)}, u32[]{:S(2)}, u32[]{:S(2)}) async-start(bf16[8,19,8,256]{3,2,1,0:T(8,128)(2,1)} %get-tuple-element.20), calls=%async_computation | async-start | bytes 1245184 | tf_op jit(solution)/shard_map/all_to_all | solution.py:480
  10.7 17.7 %copy-start = (bf16[9,64,2048]{2,1,0:T(8,128)(2,1)S(1)}, bf16[9,64,2048]{2,1,0:T(8,128)(2,1)}, u32[]{:S(2)}) copy-start(bf16[9,64,2048]{2,1,0:T(8,128)(2,1)} %w_ref.5) | copy-start | bytes 7077892
  15.2 4.8 %collective-permute-start = (f32[5,8,256]{2,1,0:T(8,128)}, f32[5,8,256]{2,1,0:T(8,128)S(1)}, u32[]{:S(2)}, u32[]{:S(2)}) collective-permute-start(f32[5,8,256]{2,1,0:T(8,128)} %get-tuple-element.24), channel_id=1, source_target_pairs={{0,4},{4,0},{8,12},{12,8},{16,20},{20,16},{24,28},{28,24},{1,5},{5... | collective-permute-start | bytes 122888 | tf_op jit(solution)/shard_map/ppermute | solution.py:433
  20.8 11.4 %collective-permute-start.3 = (f32[3,8,256]{2,1,0:T(8,128)S(1)}, f32[3,8,256]{2,1,0:T(8,128)S(1)}, u32[]{:S(2)}, u32[]{:S(2)}) collective-permute-start(f32[3,8,256]{2,1,0:T(8,128)S(1)} %get-tuple-element.43), channel_id=1, source_target_pairs={{0,24},{4,28},{8,16},{12,20},{16,8},{20,12},{24,0},{28,4},{1,25},{... | collective-permute-start | bytes 73736 | tf_op jit(solution)/shard_map/ppermute | solution.py:433
  25.8 6.4 %collective-permute-start.1 = (f32[3,8,256]{2,1,0:T(8,128)S(1)}, f32[3,8,256]{2,1,0:T(8,128)S(1)}, u32[]{:S(2)}, u32[]{:S(2)}) collective-permute-start(f32[3,8,256]{2,1,0:T(8,128)S(1)} %get-tuple-element.44), channel_id=1, source_target_pairs={{0,8},{4,12},{8,0},{12,4},{16,24},{20,28},{24,16},{28,20},{1,9},{5... | collective-permute-start | bytes 73736 | tf_op jit(solution)/shard_map/ppermute | solution.py:433
  25.8 6.4 %collective-permute-start.2 = (f32[3,8,256]{2,1,0:T(8,128)S(1)}, f32[3,8,256]{2,1,0:T(8,128)S(1)}, u32[]{:S(2)}, u32[]{:S(2)}) collective-permute-start(f32[3,8,256]{2,1,0:T(8,128)S(1)} %get-tuple-element.45), channel_id=1, source_target_pairs={{0,16},{4,20},{8,24},{12,28},{16,0},{20,4},{24,8},{28,12},{1,17},{... | collective-permute-start | bytes 73736 | tf_op jit(solution)/shard_map/ppermute | solution.py:433
  28.4 7.0 %copy-start.1 = (f32[1,128]{1,0:T(1,128)S(1)}, f32[1,128]{1,0:T(1,128)}, u32[]{:S(2)}) copy-start(f32[1,128]{1,0:T(1,128)} %get-tuple-element.21.own_ref) | copy-start | bytes 1540
  32.3 1.4 %collective-permute-start.4 = (bf16[9,32,256]{2,1,0:T(8,128)(2,1)S(1)}, bf16[9,32,256]{2,1,0:T(8,128)(2,1)S(1)}, u32[]{:S(2)}, u32[]{:S(2)}) collective-permute-start(bf16[9,32,256]{2,1,0:T(8,128)(2,1)S(1)} %broadcast_select_fusion.2), channel_id=1, source_target_pairs={{0,1},{1,0},{2,3},{3,2},{4,5},{5,4},{6,7},{7,6},{8,9},{9,8},{10,11... | collective-permute-start | bytes 442376 | tf_op jit(solution)/shard_map/ppermute | solution.py:433
  33.8 6.3 %collective-permute-start.5 = (bf16[9,32,256]{2,1,0:T(8,128)(2,1)S(1)}, bf16[9,32,256]{2,1,0:T(8,128)(2,1)S(1)}, u32[]{:S(2)}, u32[]{:S(2)}) collective-permute-start(bf16[9,32,256]{2,1,0:T(8,128)(2,1)S(1)} %add_convert_fusion.1), channel_id=1, source_target_pairs={{0,2},{1,3},{2,0},{3,1},{4,6},{5,7},{6,4},{7,5},{8,10},{9,11},{10,... | collective-permute-start | bytes 442376 | tf_op jit(solution)/shard_map/ppermute | solution.py:433
  40.2 1.4 %collective-permute-start.6 = (bf16[9,32,256]{2,1,0:T(8,128)(2,1)S(1)}, bf16[9,32,256]{2,1,0:T(8,128)(2,1)S(1)}, u32[]{:S(2)}, u32[]{:S(2)}) collective-permute-start(bf16[9,32,256]{2,1,0:T(8,128)(2,1)S(1)} %add_convert_fusion), channel_id=1, source_target_pairs={{0,1},{1,0},{2,3},{3,2},{4,5},{5,4},{6,7},{7,6},{8,9},{9,8},{10,11... | collective-permute-start | bytes 442376 | tf_op jit(solution)/shard_map/ppermute | solution.py:433

commit v4 on v3

--- a/solution.py
+++ b/solution.py
@@ -273,8 +273,9 @@
     part = devices * ROW
     pitch = slots * part
     flat_ref[...] = got_ref[...].astype(F32).reshape(devices, groups * ROW, lanes)
-    cot = flat_ref[:, slots * side * side, :]
-    info = flat_ref[:, slots * side * side + 1, :]
+    tail = got_ref[:, groups - 1].astype(F32)
+    cot = tail[:, slots * side * side % ROW, :]
+    info = tail[:, slots * side * side % ROW + 1, :]
     routes, denominator = routing_of(info, slots)
     scaled = scaled_rows(cot, denominator)
     place = lax.broadcasted_iota(jnp.int32, (devices, ROW, lanes), 1)
@@ -303,19 +304,20 @@
             pres = pair_conv(first, second, pair_weights(w_ref, span, False), pitch, PLAIN)
             grads = [slope_of(pre)[1] * tile_grad[:, pair * 128 : (pair + 1) * 128] for pre in pres]
             none = jnp.zeros((pitch, 128), F32)
-            for high in range(side):
-                after = grads[high + 1] if high + 1 < side else none
-                before = grads[high - 1] if high > 0 else none
-                moved = split(after, grads[high], before)
-                for index in range(2):
-                    grad_ref[index, pl.ds(high * pitch, pitch), :] = moved[index]
-            products = [
-                lax.dot_general(
-                    rows_ref[index, :, :], grad_ref[index, :, :], (((0,), (0,)), ((), ())),
-                    preferred_element_type=F32,
+            turned = jnp.concatenate([none, *grads, none], axis=0).astype(BF16).T
+            count = side * pitch
+            products = []
+            for index in range(2):
+                low, middle, high = (
+                    turned[index * width : (index + 1) * width, at * pitch : at * pitch + count]
+                    for at in (2, 1, 0)
                 )
-                for index in range(2)
-            ]
+                empty = jnp.zeros(low.shape, BF16)
+                order = [middle, low, empty, high] if index else [low, middle, high, empty]
+                product = jnp.dot(
+                    jnp.concatenate(order, axis=0), rows_ref[index, :, :], preferred_element_type=F32
+                )
+                products.append(product.T)
             for col, quarter, other in ((0, 0, 1), (1, 1, 0), (2, 2, 3)):
                 taps = joined(
                     products[0][quarter * width : (quarter + 1) * width],

time: 42.8 us -> 42.3 us (0.988)
  Pallas kernels: 15.2 us -> 14.7 us
    pallas_call x1, Pallas kernels: 3.81 us -> 3.31 us  [shards(): pl.pallas_call(functools.partial(weight_kernel, packed, side), out_shape=...]
  transfers between devices with their start and end apart: 8 -> 8, of which waited for: 4 -> 4; matrix products, arithmetic and copies ran while one was open for 3% -> 4% of each run, Pallas kernels for 31% -> 30%
where the time goes in v4:
time: 42.3 us; the launch traced here: 42 us
  starting transfers between devices  16.6 us (39%)
  Pallas kernels  14.7 us (35%)
  waiting for transfers between devices  6.81 us (16%)
  other arithmetic  1.79 us (4%)
  between operations  1.36 us (3%)
  local copies, waits for them, and re-layouts  0.71 us (2%)
    ppermute x7, starting transfers between devices, swap(): lax.ppermute(value, axis, [(i, i ^ step) for i in range(lax.axis_size(axi...  9.39 us
    all_to_all x1, starting transfers between devices, shards(): got = lax.all_to_all(chunks, 'tile', 0, 0, tiled=True)  7.25 us
    ppermute x7, waiting for transfers between devices, swap(): lax.ppermute(value, axis, [(i, i ^ step) for i in range(lax.axis_size(axi...  4.87 us
    pallas_call x1, Pallas kernels, shards(): pl.pallas_call(functools.partial(input_kernel, packed), grid=(channels //...  4.72 us
    pallas_call x1, Pallas kernels, shards(): pl.pallas_call(local_kernel, grid=(channels // STEP,), out_shape=(jax.Sha...  4.49 us
    pallas_call x1, Pallas kernels, shards(): pl.pallas_call(functools.partial(weight_kernel, packed, side), out_shape=...  3.31 us
    pallas_call x1, Pallas kernels, shards(): pl.pallas_call(pack_kernel, out_shape=(jax.ShapeDtypeStruct((devices, gro...  2.15 us
    all_to_all x1, waiting for transfers between devices, shards(): got = lax.all_to_all(chunks, 'tile', 0, 0, tiled=True)  1.94 us
  transfers between devices with their start and end apart: 8, of which 4 were waited for; matrix products, arithmetic and copies ran while one was open for 4% of the time, Pallas kernels for 30%

profile of v4, /device:TPU:0, one launch (start us, length us, event | category | flops | bytes accessed | tf_op | source)
XLA Modules:
  0.0 42.0 jit_solution(12096646348928771250)
XLA Ops:
  1.3 2.1 %shard_map.94 = (bf16[8,19,8,256]{3,2,1,0:T(8,128)(2,1)}, f32[1,128]{1,0:T(1,128)}) custom-call(s32[1,1]{1,0:T(1,128)S(6)} %copy.10.counts_ref, f32[1,3]{1,0:T(1,128)} %weights_ref.1, s32[1,3]{1,0:T(1,128)} %bitcast.3, s32[1,8]{1,0:T(1,128)} %owner_ref.1, bf16[1,3,7,7,2048]{4,3,2,1,0:T(8,128)(2,1)} %x_ref.3, bf16[1,1,2048]{2,1,0:T(2,128)(2,1)} %cot_ref.3), custom_call_target="tpu_custom_call" | custom-call | tf_op jit(solution)/shard_map/pallas_call | solution.py:471
  3.4 7.3 %all-to-all-start = ((bf16[8,19,8,256]{3,2,1,0:T(8,128)(2,1)}), bf16[8,19,8,256]{3,2,1,0:T(8,128)(2,1)S(1)}, u32[]{:S(2)}, u32[]{:S(2)}) async-start(bf16[8,19,8,256]{3,2,1,0:T(8,128)(2,1)} %get-tuple-element.20), calls=%async_computation | async-start | bytes 1245184 | tf_op jit(solution)/shard_map/all_to_all | solution.py:482
  10.7 4.5 %shard_map.95 = (f32[7,24,2048]{2,1,0:T(8,128)}, f32[5,8,256]{2,1,0:T(8,128)}, f32[5,8,256]{2,1,0:T(8,128)}) custom-call(s32[1]{0:T(128)} %bitcast.my_ref, f32[1,128]{1,0:T(1,128)} %get-tuple-element.21.own_ref, bf16[1,1,2048]{2,1,0:T(2,128)(2,1)} %cot_ref.3, bf16[1,3,7,7,2048]{4,3,2,1,0:T(8,128)(2,1)} %x_ref.3, bf16[9,64,2048]{2,1,0:T(8,128)(2,1)} %w_ref.5), custom_call_target="tpu_custom_call" | custom-call | flops 1387266048 | bytes 4194304 | tf_op jit(solution)/shard_map/pallas_call | solution.py:485
  15.2 2.0 %collective-permute-start = (f32[5,8,256]{2,1,0:T(8,128)}, f32[5,8,256]{2,1,0:T(8,128)S(1)}, u32[]{:S(2)}, u32[]{:S(2)}) collective-permute-start(f32[5,8,256]{2,1,0:T(8,128)} %get-tuple-element.24), channel_id=1, source_target_pairs={{0,4},{4,0},{8,12},{12,8},{16,20},{20,16},{24,28},{28,24},{1,5},{5... | collective-permute-start | bytes 122888 | tf_op jit(solution)/shard_map/ppermute | solution.py:435
  17.2 0.7 %slice.27 = f32[1,8,256]{2,1,0:T(8,128)S(1)} slice(f32[5,8,256]{2,1,0:T(8,128)} %get-tuple-element.23), slice={[4:5], [0:8], [0:256]} | slice | bytes 16384 | tf_op jit(solution)/shard_map/slice | solution.py:510
  17.9 2.1 %collective-permute-done = f32[5,8,256]{2,1,0:T(8,128)S(1)} collective-permute-done((f32[5,8,256]{2,1,0:T(8,128)}, f32[5,8,256]{2,1,0:T(8,128)S(1)}, u32[]{:S(2)}, u32[]{:S(2)}) %collective-permute-start) | collective-permute-done | bytes 40992 | tf_op jit(solution)/shard_map/ppermute | solution.py:435
  20.0 0.8 %slice_add_fusion = f32[4,8,256]{2,1,0:T(8,128)S(1)} fusion(f32[5,8,256]{2,1,0:T(8,128)S(1)} %collective-permute-done, f32[5,8,256]{2,1,0:T(8,128)} %get-tuple-element.23), kind=kLoop, calls=%fused_computation.14 | loop fusion | flops 8192 | bytes 98304 | tf_op jit(solution)/shard_map/add | solution.py:509
  20.8 5.0 %collective-permute-start.3 = (f32[3,8,256]{2,1,0:T(8,128)S(1)}, f32[3,8,256]{2,1,0:T(8,128)S(1)}, u32[]{:S(2)}, u32[]{:S(2)}) collective-permute-start(f32[3,8,256]{2,1,0:T(8,128)S(1)} %get-tuple-element.43), channel_id=1, source_target_pairs={{0,24},{4,28},{8,16},{12,20},{16,8},{20,12},{24,0},{28,4},{1,25},{... | collective-permute-start | bytes 73736 | tf_op jit(solution)/shard_map/ppermute | solution.py:435
  25.8 0.0 collective-permute-start.1
  25.8 0.6 %collective-permute-start.2 = (f32[3,8,256]{2,1,0:T(8,128)S(1)}, f32[3,8,256]{2,1,0:T(8,128)S(1)}, u32[]{:S(2)}, u32[]{:S(2)}) collective-permute-start(f32[3,8,256]{2,1,0:T(8,128)S(1)} %get-tuple-element.45), channel_id=1, source_target_pairs={{0,16},{4,20},{8,24},{12,28},{16,0},{20,4},{24,8},{28,12},{1,17},{... | collective-permute-start | bytes 73736 | tf_op jit(solution)/shard_map/ppermute | solution.py:435
  26.5 1.9 %all-to-all-done.got_ref.info_ref = bf16[8,19,8,256]{3,2,1,0:T(8,128)(2,1)S(1)} async-done(((bf16[8,19,8,256]{3,2,1,0:T(8,128)(2,1)}), bf16[8,19,8,256]{3,2,1,0:T(8,128)(2,1)S(1)}, u32[]{:S(2)}, u32[]{:S(2)}) %all-to-all-start) | async-done | bytes 622624 | tf_op jit(solution)/shard_map/all_to_all | solution.py:482
  28.4 3.3 %shard_map.96 = bf16[9,64,256]{2,1,0:T(8,128)(2,1)S(1)} custom-call(s32[1]{0:T(128)} %bitcast.my_ref, bf16[8,19,8,256]{3,2,1,0:T(8,128)(2,1)S(1)} %all-to-all-done.got_ref.info_ref, bf16[9,64,2048]{2,1,0:T(8,128)(2,1)S(1)} %copy-done), custom_call_target="tpu_custom_call" | custom-call | flops 2774532096 | bytes 4194304 | tf_op jit(solution)/shard_map/pallas_call | solution.py:536
  31.7 0.0 collective-permute-done.3.refs_3_
  31.7 0.0 collective-permute-done.1.refs_1_
  31.8 0.0 collective-permute-done.2.refs_2_
  31.8 0.1 collective-permute-start.4
  31.9 1.4 %collective-permute-done.4 = bf16[9,32,256]{2,1,0:T(8,128)(2,1)S(1)} collective-permute-done((bf16[9,32,256]{2,1,0:T(8,128)(2,1)S(1)}, bf16[9,32,256]{2,1,0:T(8,128)(2,1)S(1)}, u32[]{:S(2)}, u32[]{:S(2)}) %collective-permute-start.4) | collective-permute-done | bytes 147488 | tf_op jit(solution)/shard_map/ppermute | solution.py:435
  33.2 0.1 add_convert_fusion.1
  33.3 1.6 %collective-permute-start.5 = (bf16[9,32,256]{2,1,0:T(8,128)(2,1)S(1)}, bf16[9,32,256]{2,1,0:T(8,128)(2,1)S(1)}, u32[]{:S(2)}, u32[]{:S(2)}) collective-permute-start(bf16[9,32,256]{2,1,0:T(8,128)(2,1)S(1)} %add_convert_fusion.1), channel_id=1, source_target_pairs={{0,2},{1,3},{2,0},{3,1},{4,6},{5,7},{6,4},{7,5},{8,10},{9,11},{10,... | collective-permute-start | bytes 442376 | tf_op jit(solution)/shard_map/ppermute | solution.py:435
  34.9 4.7 %shard_map.97 = (f32[3,7,7,1,2048]{4,3,2,1,0:T(1,128)}, f32[1,1,2048]{2,1,0:T(1,128)}) custom-call(s32[1]{0:T(128)} %bitcast.my_ref, f32[1,128]{1,0:T(1,128)S(1)} %copy-done.1, f32[7,24,2048]{2,1,0:T(8,128)} %get-tuple-element.27.slope_ref, bf16[9,64,2048]{2,1,0:T(8,128)(2,1)S(1)} %copy-done, bf16[8,19,8,256]{3,2,1,0:T(8,128)(2,1)S(1)} %all-to-all-done.got_ref.info_ref, ...), custom_call_target="tpu_custom_call" | custom-call | flops 1387266048 | bytes 4194304 | tf_op jit(solution)/shard_map/pallas_call | solution.py:551
  39.6 0.0 collective-permute-done.5
  39.6 0.1 collective-permute-start.6
  39.7 1.4 %collective-permute-done.6 = bf16[9,32,256]{2,1,0:T(8,128)(2,1)S(1)} collective-permute-done((bf16[9,32,256]{2,1,0:T(8,128)(2,1)S(1)}, bf16[9,32,256]{2,1,0:T(8,128)(2,1)S(1)}, u32[]{:S(2)}, u32[]{:S(2)}) %collective-permute-start.6) | collective-permute-done | bytes 147488 | tf_op jit(solution)/shard_map/ppermute | solution.py:435
  41.1 0.9 %convert_multiply_fusion = f32[9,64,256]{2,1,0:T(8,128)} fusion(bf16[9,32,256]{2,1,0:T(8,128)(2,1)S(1)} %get-tuple-element.38, bf16[9,32,256]{2,1,0:T(8,128)(2,1)S(1)} %get-tuple-element.37), kind=kLoop, calls=%fused_computation | loop fusion | flops 737280 | bytes 884736 | tf_op jit(solution)/shard_map/div | solution.py:581
  (10 shorter events, 0.1 us)
Async XLA Ops:
  3.4 25.0 %all-to-all-start = ((bf16[8,19,8,256]{3,2,1,0:T(8,128)(2,1)}), bf16[8,19,8,256]{3,2,1,0:T(8,128)(2,1)S(1)}, u32[]{:S(2)}, u32[]{:S(2)}) async-start(bf16[8,19,8,256]{3,2,1,0:T(8,128)(2,1)} %get-tuple-element.20), calls=%async_computation | async-start | bytes 1245184 | tf_op jit(solution)/shard_map/all_to_all | solution.py:482
  10.7 17.7 %copy-start = (bf16[9,64,2048]{2,1,0:T(8,128)(2,1)S(1)}, bf16[9,64,2048]{2,1,0:T(8,128)(2,1)}, u32[]{:S(2)}) copy-start(bf16[9,64,2048]{2,1,0:T(8,128)(2,1)} %w_ref.5) | copy-start | bytes 7077892
  15.2 4.8 %collective-permute-start = (f32[5,8,256]{2,1,0:T(8,128)}, f32[5,8,256]{2,1,0:T(8,128)S(1)}, u32[]{:S(2)}, u32[]{:S(2)}) collective-permute-start(f32[5,8,256]{2,1,0:T(8,128)} %get-tuple-element.24), channel_id=1, source_target_pairs={{0,4},{4,0},{8,12},{12,8},{16,20},{20,16},{24,28},{28,24},{1,5},{5... | collective-permute-start | bytes 122888 | tf_op jit(solution)/shard_map/ppermute | solution.py:435
  20.8 10.9 %collective-permute-start.3 = (f32[3,8,256]{2,1,0:T(8,128)S(1)}, f32[3,8,256]{2,1,0:T(8,128)S(1)}, u32[]{:S(2)}, u32[]{:S(2)}) collective-permute-start(f32[3,8,256]{2,1,0:T(8,128)S(1)} %get-tuple-element.43), channel_id=1, source_target_pairs={{0,24},{4,28},{8,16},{12,20},{16,8},{20,12},{24,0},{28,4},{1,25},{... | collective-permute-start | bytes 73736 | tf_op jit(solution)/shard_map/ppermute | solution.py:435
  25.8 5.9 %collective-permute-start.1 = (f32[3,8,256]{2,1,0:T(8,128)S(1)}, f32[3,8,256]{2,1,0:T(8,128)S(1)}, u32[]{:S(2)}, u32[]{:S(2)}) collective-permute-start(f32[3,8,256]{2,1,0:T(8,128)S(1)} %get-tuple-element.44), channel_id=1, source_target_pairs={{0,8},{4,12},{8,0},{12,4},{16,24},{20,28},{24,16},{28,20},{1,9},{5... | collective-permute-start | bytes 73736 | tf_op jit(solution)/shard_map/ppermute | solution.py:435
  25.8 5.9 %collective-permute-start.2 = (f32[3,8,256]{2,1,0:T(8,128)S(1)}, f32[3,8,256]{2,1,0:T(8,128)S(1)}, u32[]{:S(2)}, u32[]{:S(2)}) collective-permute-start(f32[3,8,256]{2,1,0:T(8,128)S(1)} %get-tuple-element.45), channel_id=1, source_target_pairs={{0,16},{4,20},{8,24},{12,28},{16,0},{20,4},{24,8},{28,12},{1,17},{... | collective-permute-start | bytes 73736 | tf_op jit(solution)/shard_map/ppermute | solution.py:435
  28.4 6.5 %copy-start.1 = (f32[1,128]{1,0:T(1,128)S(1)}, f32[1,128]{1,0:T(1,128)}, u32[]{:S(2)}) copy-start(f32[1,128]{1,0:T(1,128)} %get-tuple-element.21.own_ref) | copy-start | bytes 1540
  31.8 1.4 %collective-permute-start.4 = (bf16[9,32,256]{2,1,0:T(8,128)(2,1)S(1)}, bf16[9,32,256]{2,1,0:T(8,128)(2,1)S(1)}, u32[]{:S(2)}, u32[]{:S(2)}) collective-permute-start(bf16[9,32,256]{2,1,0:T(8,128)(2,1)S(1)} %broadcast_select_fusion.2), channel_id=1, source_target_pairs={{0,1},{1,0},{2,3},{3,2},{4,5},{5,4},{6,7},{7,6},{8,9},{9,8},{10,11... | collective-permute-start | bytes 442376 | tf_op jit(solution)/shard_map/ppermute | solution.py:435
  33.3 6.3 %collective-permute-start.5 = (bf16[9,32,256]{2,1,0:T(8,128)(2,1)S(1)}, bf16[9,32,256]{2,1,0:T(8,128)(2,1)S(1)}, u32[]{:S(2)}, u32[]{:S(2)}) collective-permute-start(bf16[9,32,256]{2,1,0:T(8,128)(2,1)S(1)} %add_convert_fusion.1), channel_id=1, source_target_pairs={{0,2},{1,3},{2,0},{3,1},{4,6},{5,7},{6,4},{7,5},{8,10},{9,11},{10,... | collective-permute-start | bytes 442376 | tf_op jit(solution)/shard_map/ppermute | solution.py:435
  39.6 1.4 %collective-permute-start.6 = (bf16[9,32,256]{2,1,0:T(8,128)(2,1)S(1)}, bf16[9,32,256]{2,1,0:T(8,128)(2,1)S(1)}, u32[]{:S(2)}, u32[]{:S(2)}) collective-permute-start(bf16[9,32,256]{2,1,0:T(8,128)(2,1)S(1)} %add_convert_fusion), channel_id=1, source_target_pairs={{0,1},{1,0},{2,3},{3,2},{4,5},{5,4},{6,7},{7,6},{8,9},{9,8},{10,11... | collective-permute-start | bytes 442376 | tf_op jit(solution)/shard_map/ppermute | solution.py:435

commit v5 on v4

--- a/solution.py
+++ b/solution.py
@@ -132,8 +132,9 @@
 TURNED = (((1,), (1,)), ((), ()))
 
 
-def routing_of(info, slots):
+def routing_of(info, slots, cores):
     devices = info.shape[0]
+    core = (lax.broadcasted_iota(jnp.int32, (devices, 1), 0) % cores).astype(F32)
     owners = lax.broadcasted_iota(jnp.int32, (devices, 128), 1).astype(F32)
     routes = []
     total = jnp.zeros((1, 128), F32)
@@ -143,18 +144,15 @@
             + info[:, slots + slot : slots + slot + 1]
             + info[:, 2 * slots + slot : 2 * slots + slot + 1]
         )
-        target = info[:, 3 * slots + slot : 3 * slots + slot + 1]
+        target = info[:, 3 * slots + slot : 3 * slots + slot + 1] * cores + core
         route = jnp.where(target == owners, coef, 0.0)
         routes.append(route)
         total = total + jnp.sum(route, axis=0, keepdims=True)
     return routes, jnp.maximum(total, 1.0)
 
 
-def scaled_rows(cot, denominator, base=0):
-    owners = cot.shape[0]
-    same = (lax.broadcasted_iota(jnp.int32, (owners, 128), 0) ^ base) == lax.broadcasted_iota(
-        jnp.int32, (owners, 128), 1
-    )
+def scaled_rows(cot, denominator, ids):
+    same = ids == lax.broadcasted_iota(jnp.int32, (cot.shape[0], 128), 1)
     column = jnp.sum(jnp.where(same, denominator, 0.0), axis=1, keepdims=True)
     return (LOSS_SCALE * cot / column).astype(BF16).astype(F32)
 
@@ -220,7 +218,7 @@
         out_ref[device] = part.reshape(groups, ROW, lanes)
 
 
-def local_kernel(my_ref, own_ref, cot_ref, x_ref, w_ref, slope_ref, *share_refs):
+def local_kernel(cores, my_ref, own_ref, cot_ref, x_ref, w_ref, slope_ref, *share_refs):
     step = pl.program_id(0)
     side, kept, lanes = slope_ref.shape
     slots = kept // ROW
@@ -250,7 +248,7 @@
         mean = jnp.sum(here, axis=0, keepdims=True) / (side * side)
         means.append(mean.astype(BF16).astype(F32))
     for index in range(devices):
-        owner = index if len(share_refs) == 1 else my_ref[0] ^ index
+        owner = index if len(share_refs) == 1 else (my_ref[0] // cores) ^ index
         share = jnp.zeros((1, lanes), F32)
         for mean, weight in zip(means, own_route(own, slots, jnp.float32(owner))):
             share = share + weight * mean
@@ -265,7 +263,7 @@
             place_ref[devices // len(share_refs), at, :] = cot_ref[0, :, span].astype(F32)
 
 
-def weight_kernel(packed, side, my_ref, got_ref, w_ref, out_ref, rows_ref, grad_ref, flat_ref):
+def weight_kernel(packed, cores, side, my_ref, got_ref, w_ref, out_ref, rows_ref, grad_ref, flat_ref):
     del my_ref
     devices, groups, _, lanes = got_ref.shape
     slots = groups * ROW // (side * side)
@@ -276,8 +274,8 @@
     tail = got_ref[:, groups - 1].astype(F32)
     cot = tail[:, slots * side * side % ROW, :]
     info = tail[:, slots * side * side % ROW + 1, :]
-    routes, denominator = routing_of(info, slots)
-    scaled = scaled_rows(cot, denominator)
+    routes, denominator = routing_of(info, slots, cores)
+    scaled = scaled_rows(cot, denominator, lax.broadcasted_iota(jnp.int32, (devices, 128), 0))
     place = lax.broadcasted_iota(jnp.int32, (devices, ROW, lanes), 1)
     tile_grads = []
     for slot in range(slots):
@@ -370,6 +368,7 @@
 
 def input_kernel(
     packed,
+    cores,
     my_ref,
     own_ref,
     slope_ref,
@@ -381,12 +380,12 @@
     step = pl.program_id(0)
     side, kept, lanes = slope_ref.shape
     slots = kept // ROW
-    devices = info_ref.shape[0]
+    devices = info_ref.shape[0] // cores
     info = info_ref[:, 0].astype(F32)[:, (slots * side * side + 1) % ROW, :]
-    _, denominator = routing_of(info, slots)
+    _, denominator = routing_of(info, slots, cores)
     owners = lax.broadcasted_iota(jnp.int32, (1, 128), 1)
     mine = jnp.sum(jnp.where(owners == my_ref[0], denominator, 0.0), axis=1, keepdims=True)
-    base = my_ref[0] if packed else 0
+    base = my_ref[0] // cores if packed else 0
     cots = []
     for part in range(lanes // BLOCK):
         at = pl.ds(step * (lanes // BLOCK) + part, 1)
@@ -398,7 +397,8 @@
             shares = [jnp.sum(refs[0][:, at, :], axis=0)]
             cots.append(refs[1][:, at, :].reshape(devices, BLOCK))
         pooled_ref[0, :, part * BLOCK : (part + 1) * BLOCK] = sum(shares[1:], shares[0]) / mine
-    scaled = scaled_rows(jnp.concatenate(cots, axis=1), denominator, base)
+    ids = (lax.broadcasted_iota(jnp.int32, (devices, 128), 0) ^ base) * cores + my_ref[0] % cores
+    scaled = scaled_rows(jnp.concatenate(cots, axis=1), denominator, ids)
 
     place = lax.broadcasted_iota(jnp.int32, (ROW, lanes), 0)
     own = own_ref[...]
@@ -435,13 +435,9 @@
     return lax.ppermute(value, axis, [(i, i ^ step) for i in range(lax.axis_size(axis))])
 
 
-def sum_over_slide(terms, beside):
+def sum_over_slide(terms, cores, beside):
     count = lax.axis_size("slide")
-    second = lax.axis_index("slide") % 2 == 1
-    low, high = jnp.split(terms, 2, axis=1)
-    sent = swap(jnp.where(second, low, high), "slide", 1)
-    total = jnp.where(second, high, low).astype(F32) + sent.astype(F32)
-    step = 2
+    total, step = terms, cores
     while step < count:
         sent = total.astype(BF16)
         other = swap(sent, "slide", step)
@@ -449,21 +445,28 @@
             other, beside = lax.optimization_barrier((other, beside))
         total = sent.astype(F32) + other.astype(F32)
         step *= 2
-    half = total.astype(BF16)
-    rest = swap(half, "slide", 1)
-    whole = [jnp.where(second, rest, half), jnp.where(second, half, rest)]
-    return jnp.concatenate(whole, axis=1).astype(F32), beside
+    if cores == 2:
+        second = lax.axis_index("slide") % 2 == 1
+        half = total.astype(BF16)
+        rest = swap(half, "slide", 1)
+        whole = [jnp.where(second, rest, half), jnp.where(second, half, rest)]
+        total = jnp.concatenate(whole, axis=2)
+    return total.astype(F32), beside
 
 
 def shards(tiles, tile_counts, tile_weights, slide_of, owner_map, cotangent, conv_weight):
     _, slots, side, _, channels = tiles.shape
     taps, width, _ = conv_weight.shape
     devices = lax.axis_size("tile")
-    lanes = channels // devices
+    count = lax.axis_size("slide")
+    packed = channels // devices == BLOCK and count % 2 == 0
+    cores = 2 if packed else 1
+    exchange = devices * cores
+    lanes = channels // exchange
     blocks = channels // BLOCK
-    mine = lax.axis_index("tile").astype(jnp.int32).reshape(1)
+    mine = lax.axis_index("tile") * cores + lax.axis_index("slide") % cores
+    mine = mine.astype(jnp.int32).reshape(1)
     slides = slide_of[:, :, 0]
-    packed = lanes == BLOCK
     groups = -(-(slots * side * side + 2) // ROW)
     kept = slots * ROW
     macs = slots * side * side * taps * width * channels
@@ -471,7 +474,7 @@
     chunks, routes = pl.pallas_call(
         pack_kernel,
         out_shape=(
-            jax.ShapeDtypeStruct((devices, groups, ROW, lanes), BF16),
+            jax.ShapeDtypeStruct((exchange, groups, ROW, lanes), BF16),
             jax.ShapeDtypeStruct((1, 128), F32),
         ),
         in_specs=[smem_whole()] * 4 + [vmem_whole()] * 2,
@@ -479,11 +482,20 @@
         scratch_shapes=[pltpu.VMEM((groups * ROW, channels), F32)],
         compiler_params=params(56),
     )(tile_counts, tile_weights, slides, owner_map, tiles, cotangent)
-    got = lax.all_to_all(chunks, "tile", 0, 0, tiled=True)
+    if packed:
+        chips = [
+            [tile * count + chip * cores + core for tile in range(devices) for core in range(cores)]
+            for chip in range(count // cores)
+        ]
+        got = lax.all_to_all(
+            chunks, ("tile", "slide"), 0, 0, tiled=True, axis_index_groups=chips
+        )
+    else:
+        got = lax.all_to_all(chunks, "tile", 0, 0, tiled=True)
 
     halves = 2 if packed else 1
     slope, *sent = pl.pallas_call(
-        local_kernel,
+        functools.partial(local_kernel, cores),
         grid=(channels // STEP,),
         out_shape=(
             jax.ShapeDtypeStruct((side, kept, channels), F32),
@@ -518,7 +530,7 @@
         shares = [lax.all_to_all(toward[:devices], "tile", 0, 0, tiled=True)]
         shares.append(lax.all_gather(toward[devices:], "tile", axis=0, tiled=True))
     info_block = (slots * side * side + 1) // ROW
-    pitch_all = slots * devices * ROW
+    pitch_all = slots * exchange * ROW
     if packed:
         scratch = [pltpu.VMEM((2, side * pitch_all, BLOCK), BF16)] * 2
     else:
@@ -526,7 +538,7 @@
             pltpu.VMEM((3, (side + 2) * pitch_all, lanes), BF16),
             pltpu.VMEM(((side + 2) * pitch_all, lanes), BF16),
         ]
-    scratch.append(pltpu.VMEM((devices, groups * ROW, lanes), F32))
+    scratch.append(pltpu.VMEM((exchange, groups * ROW, lanes), F32))
     if packed:
         weight_spec = pl.BlockSpec((taps, width, lanes), lambda j, my: (0, 0, my[0]))
         weight = conv_weight
@@ -534,7 +546,7 @@
         weight_spec = pl.BlockSpec((taps, width, lanes), lambda j, my: (0, 0, 0))
         weight = lax.dynamic_slice_in_dim(conv_weight, mine[0] * lanes, lanes, 2)
     terms = pl.pallas_call(
-        functools.partial(weight_kernel, packed, side),
+        functools.partial(weight_kernel, packed, cores, side),
         out_shape=jax.ShapeDtypeStruct((taps, width, lanes), BF16),
         grid_spec=pltpu.PrefetchScalarGridSpec(
             num_scalar_prefetch=1,
@@ -549,7 +561,7 @@
 
     terms, shares = lax.optimization_barrier((terms, shares))
     grads, pooled = pl.pallas_call(
-        functools.partial(input_kernel, packed),
+        functools.partial(input_kernel, packed, cores),
         grid=(channels // STEP,),
         out_shape=(
             jax.ShapeDtypeStruct((slots, side, side, 1, channels), F32),
@@ -560,7 +572,7 @@
             pl.BlockSpec((1, 128), lambda j: (0, 0)),
             pl.BlockSpec((side, kept, STEP), lambda j: (0, 0, j)),
             pl.BlockSpec((taps, width, STEP), lambda j: (0, 0, j)),
-            pl.BlockSpec((devices, 1, ROW, lanes), lambda j: (0, info_block, 0, 0)),
+            pl.BlockSpec((exchange, 1, ROW, lanes), lambda j: (0, info_block, 0, 0)),
         ]
         + [pl.BlockSpec((part.shape[0], blocks, BLOCK), lambda j: (0, 0, 0)) for part in shares],
         out_specs=(
@@ -577,7 +589,7 @@
         got,
         *shares,
     )
-    total, (grads, pooled) = sum_over_slide(terms, (grads, pooled))
+    total, (grads, pooled) = sum_over_slide(terms, cores, (grads, pooled))
     weight_grads = total / LOSS_SCALE
     input_grads = jnp.transpose(grads, (3, 0, 1, 2, 4))
     return (pooled, input_grads, weight_grads)

time: 42.3 us -> 39.6 us (0.936)
  waiting for transfers between devices: 6.81 us -> 5.36 us
  starting transfers between devices: 16.6 us -> 15.4 us
    ppermute x7 -> x6, waiting for transfers between devices: 4.87 us -> 3.47 us  [swap(): lax.ppermute(value, axis, [(i, i ^ step) for i in range(lax.axis_size(axi...]
    ppermute x7 -> x6, starting transfers between devices: 9.39 us -> 8.06 us  [swap(): lax.ppermute(value, axis, [(i, i ^ step) for i in range(lax.axis_size(axi...]
  transfers between devices with their start and end apart: 8 -> 7, of which waited for: 4 -> 3; matrix products, arithmetic and copies ran while one was open for 4% -> 4% of each run, Pallas kernels for 30% -> 32%
where the time goes in v5:
time: 39.6 us; the launch traced here: 39.2 us
  starting transfers between devices  15.4 us (39%)
  Pallas kernels  14.6 us (37%)
  waiting for transfers between devices  5.36 us (14%)
  other arithmetic  1.71 us (4%)
  between operations  1.37 us (3%)
  local copies, waits for them, and re-layouts  0.72 us (2%)
    ppermute x6, starting transfers between devices, swap(): lax.ppermute(value, axis, [(i, i ^ step) for i in range(lax.axis_size(axi...  8.06 us
    all_to_all x1, starting transfers between devices, shards(): lax.all_to_all(chunks, ('tile', 'slide'), 0, 0, tiled=True, axis_index_gr...  7.36 us
    pallas_call x1, Pallas kernels, shards(): pl.pallas_call(functools.partial(input_kernel, packed, cores), grid=(chan...  4.86 us
    pallas_call x1, Pallas kernels, shards(): pl.pallas_call(functools.partial(local_kernel, cores), grid=(channels //...  4.45 us
    ppermute x6, waiting for transfers between devices, swap(): lax.ppermute(value, axis, [(i, i ^ step) for i in range(lax.axis_size(axi...  3.47 us
    pallas_call x1, Pallas kernels, shards(): pl.pallas_call(functools.partial(weight_kernel, packed, cores, side), out...  3.14 us
    pallas_call x1, Pallas kernels, shards(): pl.pallas_call(pack_kernel, out_shape=(jax.ShapeDtypeStruct((exchange, gr...  2.15 us
    all_to_all x1, waiting for transfers between devices, shards(): lax.all_to_all(chunks, ('tile', 'slide'), 0, 0, tiled=True, axis_index_gr...  1.9 us
  transfers between devices with their start and end apart: 7, of which 3 were waited for; matrix products, arithmetic and copies ran while one was open for 4% of the time, Pallas kernels for 32%

profile of v5, /device:TPU:0, one launch (start us, length us, event | category | flops | bytes accessed | tf_op | source)
XLA Modules:
  0.0 39.2 jit_solution(6346406518722396599)
XLA Ops:
  1.3 2.1 %shard_map.94 = (bf16[16,19,8,128]{3,2,1,0:T(8,128)(2,1)}, f32[1,128]{1,0:T(1,128)}) custom-call(s32[1,1]{1,0:T(1,128)S(6)} %copy.10.counts_ref, f32[1,3]{1,0:T(1,128)} %weights_ref.1, s32[1,3]{1,0:T(1,128)} %bitcast.3, s32[1,8]{1,0:T(1,128)} %owner_ref.1, bf16[1,3,7,7,2048]{4,3,2,1,0:T(8,128)(2,1)} %x_ref.3, bf16[1,1,2048]{2,1,0:T(2,128)(2,1)} %cot_ref.3), custom_call_target="tpu_custom_call" | custom-call | tf_op jit(solution)/shard_map/pallas_call | solution.py:474
  3.4 7.4 %all-to-all-start = ((bf16[16,19,8,128]{3,2,1,0:T(8,128)(2,1)}), bf16[16,19,8,128]{3,2,1,0:T(8,128)(2,1)S(1)}, u32[]{:S(2)}, u32[]{:S(2)}) async-start(bf16[16,19,8,128]{3,2,1,0:T(8,128)(2,1)} %get-tuple-element.20), calls=%async_computation | async-start | bytes 1245184 | tf_op jit(solution)/shard_map/all_to_all | solution.py:490
  10.8 0.0 copy-start
  10.8 4.4 %shard_map.95 = (f32[7,24,2048]{2,1,0:T(8,128)}, f32[5,8,256]{2,1,0:T(8,128)}, f32[5,8,256]{2,1,0:T(8,128)}) custom-call(s32[1]{0:T(128)} %bitcast.my_ref, f32[1,128]{1,0:T(1,128)} %get-tuple-element.21.own_ref, bf16[1,1,2048]{2,1,0:T(2,128)(2,1)} %cot_ref.3, bf16[1,3,7,7,2048]{4,3,2,1,0:T(8,128)(2,1)} %x_ref.3, bf16[9,64,2048]{2,1,0:T(8,128)(2,1)} %w_ref.5), custom_call_target="tpu_custom_call" | custom-call | flops 1387266048 | bytes 4194304 | tf_op jit(solution)/shard_map/pallas_call | solution.py:497
  15.3 1.9 %collective-permute-start = (f32[5,8,256]{2,1,0:T(8,128)}, f32[5,8,256]{2,1,0:T(8,128)S(1)}, u32[]{:S(2)}, u32[]{:S(2)}) collective-permute-start(f32[5,8,256]{2,1,0:T(8,128)} %get-tuple-element.24), channel_id=1, source_target_pairs={{0,4},{4,0},{8,12},{12,8},{16,20},{20,16},{24,28},{28,24},{1,5},{5... | collective-permute-start | bytes 122888 | tf_op jit(solution)/shard_map/ppermute | solution.py:435
  17.2 0.7 %slice.27 = f32[1,8,256]{2,1,0:T(8,128)S(1)} slice(f32[5,8,256]{2,1,0:T(8,128)} %get-tuple-element.23), slice={[4:5], [0:8], [0:256]} | slice | bytes 16384 | tf_op jit(solution)/shard_map/slice | solution.py:522
  17.9 2.1 %collective-permute-done = f32[5,8,256]{2,1,0:T(8,128)S(1)} collective-permute-done((f32[5,8,256]{2,1,0:T(8,128)}, f32[5,8,256]{2,1,0:T(8,128)S(1)}, u32[]{:S(2)}, u32[]{:S(2)}) %collective-permute-start) | collective-permute-done | bytes 40992 | tf_op jit(solution)/shard_map/ppermute | solution.py:435
  20.0 0.8 %slice_add_fusion = f32[4,8,256]{2,1,0:T(8,128)S(1)} fusion(f32[5,8,256]{2,1,0:T(8,128)S(1)} %collective-permute-done, f32[5,8,256]{2,1,0:T(8,128)} %get-tuple-element.23), kind=kLoop, calls=%fused_computation.12 | loop fusion | flops 8192 | bytes 98304 | tf_op jit(solution)/shard_map/add | solution.py:521
  20.8 3.9 %collective-permute-start.3 = (f32[3,8,256]{2,1,0:T(8,128)S(1)}, f32[3,8,256]{2,1,0:T(8,128)S(1)}, u32[]{:S(2)}, u32[]{:S(2)}) collective-permute-start(f32[3,8,256]{2,1,0:T(8,128)S(1)} %get-tuple-element.43), channel_id=1, source_target_pairs={{0,24},{4,28},{8,16},{12,20},{16,8},{20,12},{24,0},{28,4},{1,25},{... | collective-permute-start | bytes 73736 | tf_op jit(solution)/shard_map/ppermute | solution.py:435
  24.6 0.0 collective-permute-start.1
  24.6 0.6 %collective-permute-start.2 = (f32[3,8,256]{2,1,0:T(8,128)S(1)}, f32[3,8,256]{2,1,0:T(8,128)S(1)}, u32[]{:S(2)}, u32[]{:S(2)}) collective-permute-start(f32[3,8,256]{2,1,0:T(8,128)S(1)} %get-tuple-element.45), channel_id=1, source_target_pairs={{0,16},{4,20},{8,24},{12,28},{16,0},{20,4},{24,8},{28,12},{1,17},{... | collective-permute-start | bytes 73736 | tf_op jit(solution)/shard_map/ppermute | solution.py:435
  25.3 1.9 %all-to-all-done.got_ref.info_ref = bf16[16,19,8,128]{3,2,1,0:T(8,128)(2,1)S(1)} async-done(((bf16[16,19,8,128]{3,2,1,0:T(8,128)(2,1)}), bf16[16,19,8,128]{3,2,1,0:T(8,128)(2,1)S(1)}, u32[]{:S(2)}, u32[]{:S(2)}) %all-to-all-start) | async-done | bytes 622624 | tf_op jit(solution)/shard_map/all_to_all | solution.py:490
  27.2 0.0 copy-done
  27.2 3.1 %shard_map.96 = bf16[9,64,128]{2,1,0:T(8,128)(2,1)S(1)} custom-call(s32[1]{0:T(128)} %bitcast.my_ref, bf16[16,19,8,128]{3,2,1,0:T(8,128)(2,1)S(1)} %all-to-all-done.got_ref.info_ref, bf16[9,64,2048]{2,1,0:T(8,128)(2,1)S(1)} %copy-done), custom_call_target="tpu_custom_call" | custom-call | flops 2774532096 | bytes 4194304 | tf_op jit(solution)/shard_map/pallas_call | solution.py:548
  30.3 0.0 collective-permute-done.3.refs_3_
  30.3 0.0 collective-permute-done.1.refs_1_
  30.3 0.0 collective-permute-done.2.refs_2_
  30.3 1.6 %collective-permute-start.4 = (bf16[9,64,128]{2,1,0:T(8,128)(2,1)S(1)}, bf16[9,64,128]{2,1,0:T(8,128)(2,1)S(1)}, u32[]{:S(2)}, u32[]{:S(2)}) collective-permute-start(bf16[9,64,128]{2,1,0:T(8,128)(2,1)S(1)} %shard_map.96), channel_id=1, source_target_pairs={{0,2},{1,3},{2,0},{3,1},{4,6},{5,7},{6,4},{7,5},{8,10},{9,11},{10,... | collective-permute-start | bytes 442376 | tf_op jit(solution)/shard_map/ppermute | solution.py:435
  31.9 0.0 copy-done.1
  31.9 4.9 %shard_map.97 = (f32[3,7,7,1,2048]{4,3,2,1,0:T(1,128)}, f32[1,1,2048]{2,1,0:T(1,128)}) custom-call(s32[1]{0:T(128)} %bitcast.my_ref, f32[1,128]{1,0:T(1,128)S(1)} %copy-done.1, f32[7,24,2048]{2,1,0:T(8,128)} %get-tuple-element.27.slope_ref, bf16[9,64,2048]{2,1,0:T(8,128)(2,1)S(1)} %copy-done, bf16[16,19,8,128]{3,2,1,0:T(8,128)(2,1)S(1)} %all-to-all-done.got_ref.info_ref, ...), custom_call_target="tpu_custom_call" | custom-call | flops 1387266048 | bytes 4194304 | tf_op jit(solution)/shard_map/pallas_call | solution.py:563
  36.8 0.0 collective-permute-done.4
  36.8 0.1 collective-permute-start.5
  36.9 1.4 %collective-permute-done.5 = bf16[9,64,128]{2,1,0:T(8,128)(2,1)S(1)} collective-permute-done((bf16[9,64,128]{2,1,0:T(8,128)(2,1)S(1)}, bf16[9,64,128]{2,1,0:T(8,128)(2,1)S(1)}, u32[]{:S(2)}, u32[]{:S(2)}) %collective-permute-start.5) | collective-permute-done | bytes 147488 | tf_op jit(solution)/shard_map/ppermute | solution.py:435
  38.3 0.9 %convert_multiply_fusion = f32[9,64,256]{2,1,0:T(8,128)} fusion(bf16[9,64,128]{2,1,0:T(8,128)(2,1)S(1)} %get-tuple-element.38, bf16[9,64,128]{2,1,0:T(8,128)(2,1)S(1)} %get-tuple-element.37), kind=kLoop, calls=%fused_computation | loop fusion | flops 737280 | bytes 884736 | tf_op jit(solution)/shard_map/div | solution.py:593
  (6 shorter events, 0.1 us)
Async XLA Ops:
  3.4 23.7 %all-to-all-start = ((bf16[16,19,8,128]{3,2,1,0:T(8,128)(2,1)}), bf16[16,19,8,128]{3,2,1,0:T(8,128)(2,1)S(1)}, u32[]{:S(2)}, u32[]{:S(2)}) async-start(bf16[16,19,8,128]{3,2,1,0:T(8,128)(2,1)} %get-tuple-element.20), calls=%async_computation | async-start | bytes 1245184 | tf_op jit(solution)/shard_map/all_to_all | solution.py:490
  10.8 16.4 %copy-start = (bf16[9,64,2048]{2,1,0:T(8,128)(2,1)S(1)}, bf16[9,64,2048]{2,1,0:T(8,128)(2,1)}, u32[]{:S(2)}) copy-start(bf16[9,64,2048]{2,1,0:T(8,128)(2,1)} %w_ref.5) | copy-start | bytes 7077892
  15.3 4.7 %collective-permute-start = (f32[5,8,256]{2,1,0:T(8,128)}, f32[5,8,256]{2,1,0:T(8,128)S(1)}, u32[]{:S(2)}, u32[]{:S(2)}) collective-permute-start(f32[5,8,256]{2,1,0:T(8,128)} %get-tuple-element.24), channel_id=1, source_target_pairs={{0,4},{4,0},{8,12},{12,8},{16,20},{20,16},{24,28},{28,24},{1,5},{5... | collective-permute-start | bytes 122888 | tf_op jit(solution)/shard_map/ppermute | solution.py:435
  20.8 9.6 %collective-permute-start.3 = (f32[3,8,256]{2,1,0:T(8,128)S(1)}, f32[3,8,256]{2,1,0:T(8,128)S(1)}, u32[]{:S(2)}, u32[]{:S(2)}) collective-permute-start(f32[3,8,256]{2,1,0:T(8,128)S(1)} %get-tuple-element.43), channel_id=1, source_target_pairs={{0,24},{4,28},{8,16},{12,20},{16,8},{20,12},{24,0},{28,4},{1,25},{... | collective-permute-start | bytes 73736 | tf_op jit(solution)/shard_map/ppermute | solution.py:435
  24.6 5.7 %collective-permute-start.1 = (f32[3,8,256]{2,1,0:T(8,128)S(1)}, f32[3,8,256]{2,1,0:T(8,128)S(1)}, u32[]{:S(2)}, u32[]{:S(2)}) collective-permute-start(f32[3,8,256]{2,1,0:T(8,128)S(1)} %get-tuple-element.44), channel_id=1, source_target_pairs={{0,8},{4,12},{8,0},{12,4},{16,24},{20,28},{24,16},{28,20},{1,9},{5... | collective-permute-start | bytes 73736 | tf_op jit(solution)/shard_map/ppermute | solution.py:435
  24.6 5.7 %collective-permute-start.2 = (f32[3,8,256]{2,1,0:T(8,128)S(1)}, f32[3,8,256]{2,1,0:T(8,128)S(1)}, u32[]{:S(2)}, u32[]{:S(2)}) collective-permute-start(f32[3,8,256]{2,1,0:T(8,128)S(1)} %get-tuple-element.45), channel_id=1, source_target_pairs={{0,16},{4,20},{8,24},{12,28},{16,0},{20,4},{24,8},{28,12},{1,17},{... | collective-permute-start | bytes 73736 | tf_op jit(solution)/shard_map/ppermute | solution.py:435
  27.2 4.8 %copy-start.1 = (f32[1,128]{1,0:T(1,128)S(1)}, f32[1,128]{1,0:T(1,128)}, u32[]{:S(2)}) copy-start(f32[1,128]{1,0:T(1,128)} %get-tuple-element.21.own_ref) | copy-start | bytes 1540
  30.3 6.5 %collective-permute-start.4 = (bf16[9,64,128]{2,1,0:T(8,128)(2,1)S(1)}, bf16[9,64,128]{2,1,0:T(8,128)(2,1)S(1)}, u32[]{:S(2)}, u32[]{:S(2)}) collective-permute-start(bf16[9,64,128]{2,1,0:T(8,128)(2,1)S(1)} %shard_map.96), channel_id=1, source_target_pairs={{0,2},{1,3},{2,0},{3,1},{4,6},{5,7},{6,4},{7,5},{8,10},{9,11},{10,... | collective-permute-start | bytes 442376 | tf_op jit(solution)/shard_map/ppermute | solution.py:435
  36.8 1.4 %collective-permute-start.5 = (bf16[9,64,128]{2,1,0:T(8,128)(2,1)S(1)}, bf16[9,64,128]{2,1,0:T(8,128)(2,1)S(1)}, u32[]{:S(2)}, u32[]{:S(2)}) collective-permute-start(bf16[9,64,128]{2,1,0:T(8,128)(2,1)S(1)} %add_convert_fusion), channel_id=1, source_target_pairs={{0,1},{1,0},{2,3},{3,2},{4,5},{5,4},{6,7},{7,6},{8,9},{9,8},{10,11... | collective-permute-start | bytes 442376 | tf_op jit(solution)/shard_map/ppermute | solution.py:435

commit v6 on v5

--- a/solution.py
+++ b/solution.py
@@ -263,7 +263,9 @@
             place_ref[devices // len(share_refs), at, :] = cot_ref[0, :, span].astype(F32)
 
 
-def weight_kernel(packed, cores, side, my_ref, got_ref, w_ref, out_ref, rows_ref, grad_ref, flat_ref):
+def weight_kernel(
+    packed, cores, side, my_ref, got_ref, w_ref, out_ref, below_ref, rows_ref, grad_ref, flat_ref
+):
     del my_ref
     devices, groups, _, lanes = got_ref.shape
     slots = groups * ROW // (side * side)
@@ -275,6 +277,7 @@
     cot = tail[:, slots * side * side % ROW, :]
     info = tail[:, slots * side * side % ROW + 1, :]
     routes, denominator = routing_of(info, slots, cores)
+    below_ref[...] = denominator
     scaled = scaled_rows(cot, denominator, lax.broadcasted_iota(jnp.int32, (devices, 128), 0))
     place = lax.broadcasted_iota(jnp.int32, (devices, ROW, lanes), 1)
     tile_grads = []
@@ -373,16 +376,15 @@
     own_ref,
     slope_ref,
     w_ref,
-    info_ref,
+    below_ref,
     *refs,
 ):
     *refs, out_ref, pooled_ref = refs
     step = pl.program_id(0)
     side, kept, lanes = slope_ref.shape
     slots = kept // ROW
-    devices = info_ref.shape[0] // cores
-    info = info_ref[:, 0].astype(F32)[:, (slots * side * side + 1) % ROW, :]
-    _, denominator = routing_of(info, slots, cores)
+    devices = 2 * len(refs) if packed else refs[1].shape[0]
+    denominator = below_ref[...]
     owners = lax.broadcasted_iota(jnp.int32, (1, 128), 1)
     mine = jnp.sum(jnp.where(owners == my_ref[0], denominator, 0.0), axis=1, keepdims=True)
     base = my_ref[0] // cores if packed else 0
@@ -398,7 +400,8 @@
             cots.append(refs[1][:, at, :].reshape(devices, BLOCK))
         pooled_ref[0, :, part * BLOCK : (part + 1) * BLOCK] = sum(shares[1:], shares[0]) / mine
     ids = (lax.broadcasted_iota(jnp.int32, (devices, 128), 0) ^ base) * cores + my_ref[0] % cores
-    scaled = scaled_rows(jnp.concatenate(cots, axis=1), denominator, ids)
+    cot = jnp.concatenate(cots, axis=1)
+    scaled = scaled_rows(cot, denominator, ids)
 
     place = lax.broadcasted_iota(jnp.int32, (ROW, lanes), 0)
     own = own_ref[...]
@@ -529,7 +532,6 @@
     else:
         shares = [lax.all_to_all(toward[:devices], "tile", 0, 0, tiled=True)]
         shares.append(lax.all_gather(toward[devices:], "tile", axis=0, tiled=True))
-    info_block = (slots * side * side + 1) // ROW
     pitch_all = slots * exchange * ROW
     if packed:
         scratch = [pltpu.VMEM((2, side * pitch_all, BLOCK), BF16)] * 2
@@ -545,14 +547,20 @@
     else:
         weight_spec = pl.BlockSpec((taps, width, lanes), lambda j, my: (0, 0, 0))
         weight = lax.dynamic_slice_in_dim(conv_weight, mine[0] * lanes, lanes, 2)
-    terms = pl.pallas_call(
+    terms, below = pl.pallas_call(
         functools.partial(weight_kernel, packed, cores, side),
-        out_shape=jax.ShapeDtypeStruct((taps, width, lanes), BF16),
+        out_shape=(
+            jax.ShapeDtypeStruct((taps, width, lanes), BF16),
+            jax.ShapeDtypeStruct((1, 128), F32),
+        ),
         grid_spec=pltpu.PrefetchScalarGridSpec(
             num_scalar_prefetch=1,
             grid=(1,),
             in_specs=[pl.BlockSpec(got.shape, lambda j, my: (0, 0, 0, 0)), weight_spec],
-            out_specs=pl.BlockSpec((taps, width, lanes), lambda j, my: (0, 0, 0)),
+            out_specs=(
+                pl.BlockSpec((taps, width, lanes), lambda j, my: (0, 0, 0)),
+                pl.BlockSpec((1, 128), lambda j, my: (0, 0)),
+            ),
             scratch_shapes=scratch,
         ),
         compiler_params=params(20),
@@ -572,7 +580,7 @@
             pl.BlockSpec((1, 128), lambda j: (0, 0)),
             pl.BlockSpec((side, kept, STEP), lambda j: (0, 0, j)),
             pl.BlockSpec((taps, width, STEP), lambda j: (0, 0, j)),
-            pl.BlockSpec((exchange, 1, ROW, lanes), lambda j: (0, info_block, 0, 0)),
+            pl.BlockSpec((1, 128), lambda j: (0, 0)),
         ]
         + [pl.BlockSpec((part.shape[0], blocks, BLOCK), lambda j: (0, 0, 0)) for part in shares],
         out_specs=(
@@ -586,7 +594,7 @@
         routes,
         pltpu.with_memory_space_constraint(slope, pltpu.HBM),
         conv_weight,
-        got,
+        below,
         *shares,
     )
     total, (grads, pooled) = sum_over_slide(terms, cores, (grads, pooled))

time: 39.6 us -> 39.2 us (0.990)
  transfers between devices with their start and end apart: 7 -> 7, of which waited for: 3 -> 3; matrix products, arithmetic and copies ran while one was open for 4% -> 4% of each run, Pallas kernels for 32% -> 31%
where the time goes in v6:
time: 39.2 us; the launch traced here: 38.8 us
  starting transfers between devices  15.4 us (39%)
  Pallas kernels  14.3 us (36%)
  waiting for transfers between devices  5.34 us (14%)
  other arithmetic  1.71 us (4%)
  between operations  1.37 us (3%)
  local copies, waits for them, and re-layouts  0.72 us (2%)
    ppermute x6, starting transfers between devices, swap(): lax.ppermute(value, axis, [(i, i ^ step) for i in range(lax.axis_size(axi...  8.04 us
    all_to_all x1, starting transfers between devices, shards(): lax.all_to_all(chunks, ('tile', 'slide'), 0, 0, tiled=True, axis_index_gr...  7.36 us
    pallas_call x1, Pallas kernels, shards(): pl.pallas_call(functools.partial(input_kernel, packed, cores), grid=(chan...  4.5 us
    pallas_call x1, Pallas kernels, shards(): pl.pallas_call(functools.partial(local_kernel, cores), grid=(channels //...  4.48 us
    ppermute x6, waiting for transfers between devices, swap(): lax.ppermute(value, axis, [(i, i ^ step) for i in range(lax.axis_size(axi...  3.46 us
    pallas_call x1, Pallas kernels, shards(): pl.pallas_call(functools.partial(weight_kernel, packed, cores, side), out...  3.15 us
    pallas_call x1, Pallas kernels, shards(): pl.pallas_call(pack_kernel, out_shape=(jax.ShapeDtypeStruct((exchange, gr...  2.15 us
    all_to_all x1, waiting for transfers between devices, shards(): lax.all_to_all(chunks, ('tile', 'slide'), 0, 0, tiled=True, axis_index_gr...  1.88 us
  transfers between devices with their start and end apart: 7, of which 3 were waited for; matrix products, arithmetic and copies ran while one was open for 4% of the time, Pallas kernels for 31%

profile of v6, /device:TPU:0, one launch (start us, length us, event | category | flops | bytes accessed | tf_op | source)
XLA Modules:
  0.0 38.8 jit_solution(2873943560061086990)
XLA Ops:
  1.3 2.1 %shard_map.94 = (bf16[16,19,8,128]{3,2,1,0:T(8,128)(2,1)}, f32[1,128]{1,0:T(1,128)}) custom-call(s32[1,1]{1,0:T(1,128)S(6)} %copy.10.counts_ref, f32[1,3]{1,0:T(1,128)} %weights_ref.1, s32[1,3]{1,0:T(1,128)} %bitcast.3, s32[1,8]{1,0:T(1,128)} %owner_ref.1, bf16[1,3,7,7,2048]{4,3,2,1,0:T(8,128)(2,1)} %x_ref.3, bf16[1,1,2048]{2,1,0:T(2,128)(2,1)} %cot_ref.3), custom_call_target="tpu_custom_call" | custom-call | tf_op jit(solution)/shard_map/pallas_call | solution.py:477
  3.4 7.4 %all-to-all-start = ((bf16[16,19,8,128]{3,2,1,0:T(8,128)(2,1)}), bf16[16,19,8,128]{3,2,1,0:T(8,128)(2,1)S(1)}, u32[]{:S(2)}, u32[]{:S(2)}) async-start(bf16[16,19,8,128]{3,2,1,0:T(8,128)(2,1)} %get-tuple-element.22), calls=%async_computation | async-start | bytes 1245184 | tf_op jit(solution)/shard_map/all_to_all | solution.py:493
  10.8 0.0 copy-start
  10.8 4.5 %shard_map.95 = (f32[7,24,2048]{2,1,0:T(8,128)}, f32[5,8,256]{2,1,0:T(8,128)}, f32[5,8,256]{2,1,0:T(8,128)}) custom-call(s32[1]{0:T(128)} %bitcast.my_ref, f32[1,128]{1,0:T(1,128)} %get-tuple-element.23.own_ref, bf16[1,1,2048]{2,1,0:T(2,128)(2,1)} %cot_ref.3, bf16[1,3,7,7,2048]{4,3,2,1,0:T(8,128)(2,1)} %x_ref.3, bf16[9,64,2048]{2,1,0:T(8,128)(2,1)} %w_ref.5), custom_call_target="tpu_custom_call" | custom-call | flops 1387266048 | bytes 4194304 | tf_op jit(solution)/shard_map/pallas_call | solution.py:500
  15.3 1.9 %collective-permute-start = (f32[5,8,256]{2,1,0:T(8,128)}, f32[5,8,256]{2,1,0:T(8,128)S(1)}, u32[]{:S(2)}, u32[]{:S(2)}) collective-permute-start(f32[5,8,256]{2,1,0:T(8,128)} %get-tuple-element.26), channel_id=1, source_target_pairs={{0,4},{4,0},{8,12},{12,8},{16,20},{20,16},{24,28},{28,24},{1,5},{5... | collective-permute-start | bytes 122888 | tf_op jit(solution)/shard_map/ppermute | solution.py:438
  17.2 0.7 %slice.27 = f32[1,8,256]{2,1,0:T(8,128)S(1)} slice(f32[5,8,256]{2,1,0:T(8,128)} %get-tuple-element.25), slice={[4:5], [0:8], [0:256]} | slice | bytes 16384 | tf_op jit(solution)/shard_map/slice | solution.py:525
  17.9 2.1 %collective-permute-done = f32[5,8,256]{2,1,0:T(8,128)S(1)} collective-permute-done((f32[5,8,256]{2,1,0:T(8,128)}, f32[5,8,256]{2,1,0:T(8,128)S(1)}, u32[]{:S(2)}, u32[]{:S(2)}) %collective-permute-start) | collective-permute-done | bytes 40992 | tf_op jit(solution)/shard_map/ppermute | solution.py:438
  20.0 0.8 %slice_add_fusion = f32[4,8,256]{2,1,0:T(8,128)S(1)} fusion(f32[5,8,256]{2,1,0:T(8,128)S(1)} %collective-permute-done, f32[5,8,256]{2,1,0:T(8,128)} %get-tuple-element.25), kind=kLoop, calls=%fused_computation.12 | loop fusion | flops 8192 | bytes 98304 | tf_op jit(solution)/shard_map/add | solution.py:524
  20.8 3.8 %collective-permute-start.3 = (f32[3,8,256]{2,1,0:T(8,128)S(1)}, f32[3,8,256]{2,1,0:T(8,128)S(1)}, u32[]{:S(2)}, u32[]{:S(2)}) collective-permute-start(f32[3,8,256]{2,1,0:T(8,128)S(1)} %get-tuple-element.47), channel_id=1, source_target_pairs={{0,24},{4,28},{8,16},{12,20},{16,8},{20,12},{24,0},{28,4},{1,25},{... | collective-permute-start | bytes 73736 | tf_op jit(solution)/shard_map/ppermute | solution.py:438
  24.6 0.0 collective-permute-start.1
  24.6 0.6 %collective-permute-start.2 = (f32[3,8,256]{2,1,0:T(8,128)S(1)}, f32[3,8,256]{2,1,0:T(8,128)S(1)}, u32[]{:S(2)}, u32[]{:S(2)}) collective-permute-start(f32[3,8,256]{2,1,0:T(8,128)S(1)} %get-tuple-element.49), channel_id=1, source_target_pairs={{0,16},{4,20},{8,24},{12,28},{16,0},{20,4},{24,8},{28,12},{1,17},{... | collective-permute-start | bytes 73736 | tf_op jit(solution)/shard_map/ppermute | solution.py:438
  25.3 1.9 %all-to-all-done.got_ref = bf16[16,19,8,128]{3,2,1,0:T(8,128)(2,1)S(1)} async-done(((bf16[16,19,8,128]{3,2,1,0:T(8,128)(2,1)}), bf16[16,19,8,128]{3,2,1,0:T(8,128)(2,1)S(1)}, u32[]{:S(2)}, u32[]{:S(2)}) %all-to-all-start) | async-done | bytes 622624 | tf_op jit(solution)/shard_map/all_to_all | solution.py:493
  27.2 0.0 copy-done
  27.2 3.2 %shard_map.96 = (bf16[9,64,128]{2,1,0:T(8,128)(2,1)S(1)}, f32[1,128]{1,0:T(1,128)S(1)}) custom-call(s32[1]{0:T(128)} %bitcast.my_ref, bf16[16,19,8,128]{3,2,1,0:T(8,128)(2,1)S(1)} %all-to-all-done.got_ref, bf16[9,64,2048]{2,1,0:T(8,128)(2,1)S(1)} %copy-done), custom_call_target="tpu_custom_call" | custom-call | flops 2774532096 | bytes 4194304 | tf_op jit(solution)/shard_map/pallas_call | solution.py:550
  30.3 0.0 collective-permute-done.3.refs_3_
  30.3 0.0 collective-permute-done.1.refs_1_
  30.3 0.0 collective-permute-done.2.refs_2_
  30.3 1.6 %collective-permute-start.4 = (bf16[9,64,128]{2,1,0:T(8,128)(2,1)S(1)}, bf16[9,64,128]{2,1,0:T(8,128)(2,1)S(1)}, u32[]{:S(2)}, u32[]{:S(2)}) collective-permute-start(bf16[9,64,128]{2,1,0:T(8,128)(2,1)S(1)} %get-tuple-element.29), channel_id=1, source_target_pairs={{0,2},{1,3},{2,0},{3,1},{4,6},{5,7},{6,4},{7,5},{8,10},{9,11},{10,... | collective-permute-start | bytes 442376 | tf_op jit(solution)/shard_map/ppermute | solution.py:438
  31.9 0.0 copy-done.1
  31.9 4.5 %shard_map.97 = (f32[3,7,7,1,2048]{4,3,2,1,0:T(1,128)}, f32[1,1,2048]{2,1,0:T(1,128)}) custom-call(s32[1]{0:T(128)} %bitcast.my_ref, f32[1,128]{1,0:T(1,128)S(1)} %copy-done.1, f32[7,24,2048]{2,1,0:T(8,128)} %get-tuple-element.30.slope_ref, bf16[9,64,2048]{2,1,0:T(8,128)(2,1)S(1)} %copy-done, f32[1,128]{1,0:T(1,128)S(1)} %get-tuple-element.31.below_ref, ...), custom_call_target="tpu_custom_call" | custom-call | flops 1387266048 | bytes 4194304 | tf_op jit(solution)/shard_map/pallas_call | solution.py:571
  36.4 0.0 collective-permute-done.4
  36.5 0.1 collective-permute-start.5
  36.6 1.4 %collective-permute-done.5 = bf16[9,64,128]{2,1,0:T(8,128)(2,1)S(1)} collective-permute-done((bf16[9,64,128]{2,1,0:T(8,128)(2,1)S(1)}, bf16[9,64,128]{2,1,0:T(8,128)(2,1)S(1)}, u32[]{:S(2)}, u32[]{:S(2)}) %collective-permute-start.5) | collective-permute-done | bytes 147488 | tf_op jit(solution)/shard_map/ppermute | solution.py:438
  38.0 0.9 %convert_multiply_fusion = f32[9,64,256]{2,1,0:T(8,128)} fusion(bf16[9,64,128]{2,1,0:T(8,128)(2,1)S(1)} %get-tuple-element.42, bf16[9,64,128]{2,1,0:T(8,128)(2,1)S(1)} %get-tuple-element.41), kind=kLoop, calls=%fused_computation | loop fusion | flops 737280 | bytes 884736 | tf_op jit(solution)/shard_map/div | solution.py:601
  (6 shorter events, 0.1 us)
Async XLA Ops:
  3.4 23.7 %all-to-all-start = ((bf16[16,19,8,128]{3,2,1,0:T(8,128)(2,1)}), bf16[16,19,8,128]{3,2,1,0:T(8,128)(2,1)S(1)}, u32[]{:S(2)}, u32[]{:S(2)}) async-start(bf16[16,19,8,128]{3,2,1,0:T(8,128)(2,1)} %get-tuple-element.22), calls=%async_computation | async-start | bytes 1245184 | tf_op jit(solution)/shard_map/all_to_all | solution.py:493
  10.8 16.4 %copy-start = (bf16[9,64,2048]{2,1,0:T(8,128)(2,1)S(1)}, bf16[9,64,2048]{2,1,0:T(8,128)(2,1)}, u32[]{:S(2)}) copy-start(bf16[9,64,2048]{2,1,0:T(8,128)(2,1)} %w_ref.5) | copy-start | bytes 7077892
  15.3 4.7 %collective-permute-start = (f32[5,8,256]{2,1,0:T(8,128)}, f32[5,8,256]{2,1,0:T(8,128)S(1)}, u32[]{:S(2)}, u32[]{:S(2)}) collective-permute-start(f32[5,8,256]{2,1,0:T(8,128)} %get-tuple-element.26), channel_id=1, source_target_pairs={{0,4},{4,0},{8,12},{12,8},{16,20},{20,16},{24,28},{28,24},{1,5},{5... | collective-permute-start | bytes 122888 | tf_op jit(solution)/shard_map/ppermute | solution.py:438
  20.8 9.5 %collective-permute-start.3 = (f32[3,8,256]{2,1,0:T(8,128)S(1)}, f32[3,8,256]{2,1,0:T(8,128)S(1)}, u32[]{:S(2)}, u32[]{:S(2)}) collective-permute-start(f32[3,8,256]{2,1,0:T(8,128)S(1)} %get-tuple-element.47), channel_id=1, source_target_pairs={{0,24},{4,28},{8,16},{12,20},{16,8},{20,12},{24,0},{28,4},{1,25},{... | collective-permute-start | bytes 73736 | tf_op jit(solution)/shard_map/ppermute | solution.py:438
  24.6 5.7 %collective-permute-start.1 = (f32[3,8,256]{2,1,0:T(8,128)S(1)}, f32[3,8,256]{2,1,0:T(8,128)S(1)}, u32[]{:S(2)}, u32[]{:S(2)}) collective-permute-start(f32[3,8,256]{2,1,0:T(8,128)S(1)} %get-tuple-element.48), channel_id=1, source_target_pairs={{0,8},{4,12},{8,0},{12,4},{16,24},{20,28},{24,16},{28,20},{1,9},{5... | collective-permute-start | bytes 73736 | tf_op jit(solution)/shard_map/ppermute | solution.py:438
  24.6 5.7 %collective-permute-start.2 = (f32[3,8,256]{2,1,0:T(8,128)S(1)}, f32[3,8,256]{2,1,0:T(8,128)S(1)}, u32[]{:S(2)}, u32[]{:S(2)}) collective-permute-start(f32[3,8,256]{2,1,0:T(8,128)S(1)} %get-tuple-element.49), channel_id=1, source_target_pairs={{0,16},{4,20},{8,24},{12,28},{16,0},{20,4},{24,8},{28,12},{1,17},{... | collective-permute-start | bytes 73736 | tf_op jit(solution)/shard_map/ppermute | solution.py:438
  27.2 4.8 %copy-start.1 = (f32[1,128]{1,0:T(1,128)S(1)}, f32[1,128]{1,0:T(1,128)}, u32[]{:S(2)}) copy-start(f32[1,128]{1,0:T(1,128)} %get-tuple-element.23.own_ref) | copy-start | bytes 1540
  30.3 6.1 %collective-permute-start.4 = (bf16[9,64,128]{2,1,0:T(8,128)(2,1)S(1)}, bf16[9,64,128]{2,1,0:T(8,128)(2,1)S(1)}, u32[]{:S(2)}, u32[]{:S(2)}) collective-permute-start(bf16[9,64,128]{2,1,0:T(8,128)(2,1)S(1)} %get-tuple-element.29), channel_id=1, source_target_pairs={{0,2},{1,3},{2,0},{3,1},{4,6},{5,7},{6,4},{7,5},{8,10},{9,11},{10,... | collective-permute-start | bytes 442376 | tf_op jit(solution)/shard_map/ppermute | solution.py:438
  36.5 1.4 %collective-permute-start.5 = (bf16[9,64,128]{2,1,0:T(8,128)(2,1)S(1)}, bf16[9,64,128]{2,1,0:T(8,128)(2,1)S(1)}, u32[]{:S(2)}, u32[]{:S(2)}) collective-permute-start(bf16[9,64,128]{2,1,0:T(8,128)(2,1)S(1)} %add_convert_fusion), channel_id=1, source_target_pairs={{0,1},{1,0},{2,3},{3,2},{4,5},{5,4},{6,7},{7,6},{8,9},{9,8},{10,11... | collective-permute-start | bytes 442376 | tf_op jit(solution)/shard_map/ppermute | solution.py:438

commit v7 on v6

--- a/solution.py
+++ b/solution.py
@@ -236,7 +236,7 @@
         for high in range(side):
             pre = pres[high]
             sigma, slope = slope_of(pre)
-            slope_ref[high, :, span] = slope
+            slope_ref[high, :, span] = slope.astype(BF16)
             total = total + pre * sigma
         totals.append(total)
     total = jnp.concatenate(totals, axis=1)
@@ -416,7 +416,7 @@
     for pair in range(lanes // 128):
         span = pl.ds(pair * 128, 128)
         here = tile_grad[:, pair * 128 : (pair + 1) * 128]
-        rows = jnp.concatenate([slope_ref[high, :, span] * here for high in range(side)], axis=0)
+        rows = jnp.concatenate([slope_ref[high, :, span].astype(F32) * here for high in range(side)], axis=0)
         first, second = pair_rows(rows)
         sums = pair_conv(first, second, pair_weights(w_ref, span, True), kept, TURNED)
         for high in range(side):
@@ -501,7 +501,7 @@
         functools.partial(local_kernel, cores),
         grid=(channels // STEP,),
         out_shape=(
-            jax.ShapeDtypeStruct((side, kept, channels), F32),
+            jax.ShapeDtypeStruct((side, kept, channels), BF16),
         )
         + (jax.ShapeDtypeStruct((devices // halves + 1, blocks, BLOCK), F32),) * halves,
         in_specs=[

time: 39.2 us -> 39.4 us (level)
  waiting for transfers between devices: 5.34 us -> 5.83 us
    ppermute x6, waiting for transfers between devices: 3.46 us -> 3.87 us  [swap(): lax.ppermute(value, axis, [(i, i ^ step) for i in range(lax.axis_size(axi...]
  transfers between devices with their start and end apart: 7 -> 7, of which waited for: 3 -> 4; matrix products, arithmetic and copies ran while one was open for 4% -> 4% of each run, Pallas kernels for 31% -> 30%
where the time goes in v7:
time: 39.4 us; the launch traced here: 39.1 us
  starting transfers between devices  15.4 us (39%)
  Pallas kernels  14 us (36%)
  waiting for transfers between devices  5.83 us (15%)
  other arithmetic  1.71 us (4%)
  between operations  1.36 us (3%)
  local copies, waits for them, and re-layouts  0.72 us (2%)
    ppermute x6, starting transfers between devices, swap(): lax.ppermute(value, axis, [(i, i ^ step) for i in range(lax.axis_size(axi...  8.06 us
    all_to_all x1, starting transfers between devices, shards(): lax.all_to_all(chunks, ('tile', 'slide'), 0, 0, tiled=True, axis_index_gr...  7.36 us
    pallas_call x1, Pallas kernels, shards(): pl.pallas_call(functools.partial(input_kernel, packed, cores), grid=(chan...  4.41 us
    pallas_call x1, Pallas kernels, shards(): pl.pallas_call(functools.partial(local_kernel, cores), grid=(channels //...  4.34 us
    ppermute x6, waiting for transfers between devices, swap(): lax.ppermute(value, axis, [(i, i ^ step) for i in range(lax.axis_size(axi...  3.87 us
    pallas_call x1, Pallas kernels, shards(): pl.pallas_call(functools.partial(weight_kernel, packed, cores, side), out...  3.14 us
    pallas_call x1, Pallas kernels, shards(): pl.pallas_call(pack_kernel, out_shape=(jax.ShapeDtypeStruct((exchange, gr...  2.15 us
    all_to_all x1, waiting for transfers between devices, shards(): lax.all_to_all(chunks, ('tile', 'slide'), 0, 0, tiled=True, axis_index_gr...  1.95 us
  transfers between devices with their start and end apart: 7, of which 4 were waited for; matrix products, arithmetic and copies ran while one was open for 4% of the time, Pallas kernels for 30%

profile of v7, /device:TPU:0, one launch (start us, length us, event | category | flops | bytes accessed | tf_op | source)
XLA Modules:
  0.0 39.1 jit_solution(15926464152289396268)
XLA Ops:
  1.3 2.1 %shard_map.94 = (bf16[16,19,8,128]{3,2,1,0:T(8,128)(2,1)}, f32[1,128]{1,0:T(1,128)}) custom-call(s32[1,1]{1,0:T(1,128)S(6)} %copy.10.counts_ref, f32[1,3]{1,0:T(1,128)} %weights_ref.1, s32[1,3]{1,0:T(1,128)} %bitcast.3, s32[1,8]{1,0:T(1,128)} %owner_ref.1, bf16[1,3,7,7,2048]{4,3,2,1,0:T(8,128)(2,1)} %x_ref.3, bf16[1,1,2048]{2,1,0:T(2,128)(2,1)} %cot_ref.3), custom_call_target="tpu_custom_call" | custom-call | tf_op jit(solution)/shard_map/pallas_call | solution.py:477
  3.4 7.4 %all-to-all-start = ((bf16[16,19,8,128]{3,2,1,0:T(8,128)(2,1)}), bf16[16,19,8,128]{3,2,1,0:T(8,128)(2,1)S(1)}, u32[]{:S(2)}, u32[]{:S(2)}) async-start(bf16[16,19,8,128]{3,2,1,0:T(8,128)(2,1)} %get-tuple-element.22), calls=%async_computation | async-start | bytes 1245184 | tf_op jit(solution)/shard_map/all_to_all | solution.py:493
  10.8 0.0 copy-start
  10.8 4.3 %shard_map.95 = (bf16[7,24,2048]{2,1,0:T(8,128)(2,1)}, f32[5,8,256]{2,1,0:T(8,128)}, f32[5,8,256]{2,1,0:T(8,128)}) custom-call(s32[1]{0:T(128)} %bitcast.my_ref, f32[1,128]{1,0:T(1,128)} %get-tuple-element.23.own_ref, bf16[1,1,2048]{2,1,0:T(2,128)(2,1)} %cot_ref.3, bf16[1,3,7,7,2048]{4,3,2,1,0:T(8,128)(2,1)} %x_ref.3, bf16[9,64,2048]{2,1,0:T(8,128)(2,1)} %w_ref.5), custom_call_target="tpu_custom_call" | custom-call | flops 1387266048 | bytes 4194304 | tf_op jit(solution)/shard_map/pallas_call | solution.py:500
  15.2 1.9 %collective-permute-start = (f32[5,8,256]{2,1,0:T(8,128)}, f32[5,8,256]{2,1,0:T(8,128)S(1)}, u32[]{:S(2)}, u32[]{:S(2)}) collective-permute-start(f32[5,8,256]{2,1,0:T(8,128)} %get-tuple-element.26), channel_id=1, source_target_pairs={{0,4},{4,0},{8,12},{12,8},{16,20},{20,16},{24,28},{28,24},{1,5},{5... | collective-permute-start | bytes 122888 | tf_op jit(solution)/shard_map/ppermute | solution.py:438
  17.1 0.7 %slice.27 = f32[1,8,256]{2,1,0:T(8,128)S(1)} slice(f32[5,8,256]{2,1,0:T(8,128)} %get-tuple-element.25), slice={[4:5], [0:8], [0:256]} | slice | bytes 16384 | tf_op jit(solution)/shard_map/slice | solution.py:525
  17.8 2.1 %collective-permute-done = f32[5,8,256]{2,1,0:T(8,128)S(1)} collective-permute-done((f32[5,8,256]{2,1,0:T(8,128)}, f32[5,8,256]{2,1,0:T(8,128)S(1)}, u32[]{:S(2)}, u32[]{:S(2)}) %collective-permute-start) | collective-permute-done | bytes 40992 | tf_op jit(solution)/shard_map/ppermute | solution.py:438
  19.9 0.8 %slice_add_fusion = f32[4,8,256]{2,1,0:T(8,128)S(1)} fusion(f32[5,8,256]{2,1,0:T(8,128)S(1)} %collective-permute-done, f32[5,8,256]{2,1,0:T(8,128)} %get-tuple-element.25), kind=kLoop, calls=%fused_computation.12 | loop fusion | flops 8192 | bytes 98304 | tf_op jit(solution)/shard_map/add | solution.py:524
  20.7 2.1 %collective-permute-start.1 = (f32[3,8,256]{2,1,0:T(8,128)S(1)}, f32[3,8,256]{2,1,0:T(8,128)S(1)}, u32[]{:S(2)}, u32[]{:S(2)}) collective-permute-start(f32[3,8,256]{2,1,0:T(8,128)S(1)} %get-tuple-element.48), channel_id=1, source_target_pairs={{0,8},{4,12},{8,0},{12,4},{16,24},{20,28},{24,16},{28,20},{1,9},{5... | collective-permute-start | bytes 73736 | tf_op jit(solution)/shard_map/ppermute | solution.py:438
  22.8 2.4 %collective-permute-start.2 = (f32[3,8,256]{2,1,0:T(8,128)S(1)}, f32[3,8,256]{2,1,0:T(8,128)S(1)}, u32[]{:S(2)}, u32[]{:S(2)}) collective-permute-start(f32[3,8,256]{2,1,0:T(8,128)S(1)} %get-tuple-element.49), channel_id=1, source_target_pairs={{0,16},{4,20},{8,24},{12,28},{16,0},{20,4},{24,8},{28,12},{1,17},{... | collective-permute-start | bytes 73736 | tf_op jit(solution)/shard_map/ppermute | solution.py:438
  25.1 0.1 collective-permute-start.3
  25.2 2.0 %all-to-all-done.got_ref = bf16[16,19,8,128]{3,2,1,0:T(8,128)(2,1)S(1)} async-done(((bf16[16,19,8,128]{3,2,1,0:T(8,128)(2,1)}), bf16[16,19,8,128]{3,2,1,0:T(8,128)(2,1)S(1)}, u32[]{:S(2)}, u32[]{:S(2)}) %all-to-all-start) | async-done | bytes 622624 | tf_op jit(solution)/shard_map/all_to_all | solution.py:493
  27.2 0.0 copy-done
  27.2 3.1 %shard_map.96 = (bf16[9,64,128]{2,1,0:T(8,128)(2,1)S(1)}, f32[1,128]{1,0:T(1,128)S(1)}) custom-call(s32[1]{0:T(128)} %bitcast.my_ref, bf16[16,19,8,128]{3,2,1,0:T(8,128)(2,1)S(1)} %all-to-all-done.got_ref, bf16[9,64,2048]{2,1,0:T(8,128)(2,1)S(1)} %copy-done), custom_call_target="tpu_custom_call" | custom-call | flops 2774532096 | bytes 4194304 | tf_op jit(solution)/shard_map/pallas_call | solution.py:550
  30.4 0.0 collective-permute-done.1.refs_1_
  30.4 0.0 collective-permute-done.2.refs_2_
  30.4 0.4 collective-permute-done.3.refs_3_
  30.8 1.5 %collective-permute-start.4 = (bf16[9,64,128]{2,1,0:T(8,128)(2,1)S(1)}, bf16[9,64,128]{2,1,0:T(8,128)(2,1)S(1)}, u32[]{:S(2)}, u32[]{:S(2)}) collective-permute-start(bf16[9,64,128]{2,1,0:T(8,128)(2,1)S(1)} %get-tuple-element.29), channel_id=1, source_target_pairs={{0,2},{1,3},{2,0},{3,1},{4,6},{5,7},{6,4},{7,5},{8,10},{9,11},{10,... | collective-permute-start | bytes 442376 | tf_op jit(solution)/shard_map/ppermute | solution.py:438
  32.3 0.0 copy-done.1
  32.3 4.4 %shard_map.97 = (f32[3,7,7,1,2048]{4,3,2,1,0:T(1,128)}, f32[1,1,2048]{2,1,0:T(1,128)}) custom-call(s32[1]{0:T(128)} %bitcast.my_ref, f32[1,128]{1,0:T(1,128)S(1)} %copy-done.1, bf16[7,24,2048]{2,1,0:T(8,128)(2,1)} %get-tuple-element.30.slope_ref, bf16[9,64,2048]{2,1,0:T(8,128)(2,1)S(1)} %copy-done, f32[1,128]{1,0:T(1,128)S(1)} %get-tuple-element.31.below_ref, ...), custom_call_target="tpu_custom_call" | custom-call | flops 1387266048 | bytes 4194304 | tf_op jit(solution)/shard_map/pallas_call | solution.py:571
  36.7 0.0 collective-permute-done.4
  36.7 0.1 collective-permute-start.5
  36.8 1.4 %collective-permute-done.5 = bf16[9,64,128]{2,1,0:T(8,128)(2,1)S(1)} collective-permute-done((bf16[9,64,128]{2,1,0:T(8,128)(2,1)S(1)}, bf16[9,64,128]{2,1,0:T(8,128)(2,1)S(1)}, u32[]{:S(2)}, u32[]{:S(2)}) %collective-permute-start.5) | collective-permute-done | bytes 147488 | tf_op jit(solution)/shard_map/ppermute | solution.py:438
  38.2 0.9 %convert_multiply_fusion = f32[9,64,256]{2,1,0:T(8,128)} fusion(bf16[9,64,128]{2,1,0:T(8,128)(2,1)S(1)} %get-tuple-element.42, bf16[9,64,128]{2,1,0:T(8,128)(2,1)S(1)} %get-tuple-element.41), kind=kLoop, calls=%fused_computation | loop fusion | flops 737280 | bytes 884736 | tf_op jit(solution)/shard_map/div | solution.py:601
  (6 shorter events, 0.1 us)
Async XLA Ops:
  3.4 23.8 %all-to-all-start = ((bf16[16,19,8,128]{3,2,1,0:T(8,128)(2,1)}), bf16[16,19,8,128]{3,2,1,0:T(8,128)(2,1)S(1)}, u32[]{:S(2)}, u32[]{:S(2)}) async-start(bf16[16,19,8,128]{3,2,1,0:T(8,128)(2,1)} %get-tuple-element.22), calls=%async_computation | async-start | bytes 1245184 | tf_op jit(solution)/shard_map/all_to_all | solution.py:493
  10.8 16.4 %copy-start = (bf16[9,64,2048]{2,1,0:T(8,128)(2,1)S(1)}, bf16[9,64,2048]{2,1,0:T(8,128)(2,1)}, u32[]{:S(2)}) copy-start(bf16[9,64,2048]{2,1,0:T(8,128)(2,1)} %w_ref.5) | copy-start | bytes 7077892
  15.2 4.7 %collective-permute-start = (f32[5,8,256]{2,1,0:T(8,128)}, f32[5,8,256]{2,1,0:T(8,128)S(1)}, u32[]{:S(2)}, u32[]{:S(2)}) collective-permute-start(f32[5,8,256]{2,1,0:T(8,128)} %get-tuple-element.26), channel_id=1, source_target_pairs={{0,4},{4,0},{8,12},{12,8},{16,20},{20,16},{24,28},{28,24},{1,5},{5... | collective-permute-start | bytes 122888 | tf_op jit(solution)/shard_map/ppermute | solution.py:438
  20.7 9.7 %collective-permute-start.1 = (f32[3,8,256]{2,1,0:T(8,128)S(1)}, f32[3,8,256]{2,1,0:T(8,128)S(1)}, u32[]{:S(2)}, u32[]{:S(2)}) collective-permute-start(f32[3,8,256]{2,1,0:T(8,128)S(1)} %get-tuple-element.48), channel_id=1, source_target_pairs={{0,8},{4,12},{8,0},{12,4},{16,24},{20,28},{24,16},{28,20},{1,9},{5... | collective-permute-start | bytes 73736 | tf_op jit(solution)/shard_map/ppermute | solution.py:438
  22.8 7.6 %collective-permute-start.2 = (f32[3,8,256]{2,1,0:T(8,128)S(1)}, f32[3,8,256]{2,1,0:T(8,128)S(1)}, u32[]{:S(2)}, u32[]{:S(2)}) collective-permute-start(f32[3,8,256]{2,1,0:T(8,128)S(1)} %get-tuple-element.49), channel_id=1, source_target_pairs={{0,16},{4,20},{8,24},{12,28},{16,0},{20,4},{24,8},{28,12},{1,17},{... | collective-permute-start | bytes 73736 | tf_op jit(solution)/shard_map/ppermute | solution.py:438
  25.1 5.6 %collective-permute-start.3 = (f32[3,8,256]{2,1,0:T(8,128)S(1)}, f32[3,8,256]{2,1,0:T(8,128)S(1)}, u32[]{:S(2)}, u32[]{:S(2)}) collective-permute-start(f32[3,8,256]{2,1,0:T(8,128)S(1)} %get-tuple-element.47), channel_id=1, source_target_pairs={{0,24},{4,28},{8,16},{12,20},{16,8},{20,12},{24,0},{28,4},{1,25},{... | collective-permute-start | bytes 73736 | tf_op jit(solution)/shard_map/ppermute | solution.py:438
  27.2 5.1 %copy-start.1 = (f32[1,128]{1,0:T(1,128)S(1)}, f32[1,128]{1,0:T(1,128)}, u32[]{:S(2)}) copy-start(f32[1,128]{1,0:T(1,128)} %get-tuple-element.23.own_ref) | copy-start | bytes 1540
  30.8 5.9 %collective-permute-start.4 = (bf16[9,64,128]{2,1,0:T(8,128)(2,1)S(1)}, bf16[9,64,128]{2,1,0:T(8,128)(2,1)S(1)}, u32[]{:S(2)}, u32[]{:S(2)}) collective-permute-start(bf16[9,64,128]{2,1,0:T(8,128)(2,1)S(1)} %get-tuple-element.29), channel_id=1, source_target_pairs={{0,2},{1,3},{2,0},{3,1},{4,6},{5,7},{6,4},{7,5},{8,10},{9,11},{10,... | collective-permute-start | bytes 442376 | tf_op jit(solution)/shard_map/ppermute | solution.py:438
  36.7 1.4 %collective-permute-start.5 = (bf16[9,64,128]{2,1,0:T(8,128)(2,1)S(1)}, bf16[9,64,128]{2,1,0:T(8,128)(2,1)S(1)}, u32[]{:S(2)}, u32[]{:S(2)}) collective-permute-start(bf16[9,64,128]{2,1,0:T(8,128)(2,1)S(1)} %add_convert_fusion), channel_id=1, source_target_pairs={{0,1},{1,0},{2,3},{3,2},{4,5},{5,4},{6,7},{7,6},{8,9},{9,8},{10,11... | collective-permute-start | bytes 442376 | tf_op jit(solution)/shard_map/ppermute | solution.py:438
